TPU v7x, 512 devices: a whole 4x8x8 slice. The times are simulated.
512 devices in a mesh: seq: 64 (over y_hi, z, core), chan: 8 (over y_lo, x).
Axes of the slice: x: 4, y: 8 (y_hi: 4, y_lo: 2; y = y_hi * 2 + y_lo), z: 8, core: 2. Of those that a mesh axis runs over, the one named last changes fastest.
Arguments:
- queries: float32 [128, 524288], P(None, ('seq', 'chan')), may hold values from -6 to 6
- keys: float32 [128, 524288], P(None, ('seq', 'chan')), may hold values from -6 to 6
- values: float32 [128, 524288], P(None, ('seq', 'chan')), may hold values from -6 to 6
- short_taps: float32 [3, 3, 128], replicated, may hold values from -3 to 3
- long_filter: float32 [128, 524288], P('chan', 'seq'), may hold values from -2 to 2
- skip_gain: float32 [128], replicated, may hold values from 0.5 to 1.5
Outputs:
- gated_output: float32 [128, 524288], P(None, ('seq', 'chan'))
All inputs are finite; a program needn't handle non-finite values.
Results may differ from a plain program's by a relative error of at most 0.00016.
Values sent between devices are 32-bit elements; how exact they have to be, the bound alone decides.
No kernel may reach another device: no remote copies, remote signals or barrier semaphores. Data moves between devices by JAX's collectives and lax.ppermute only.
A program may use at most 64 MiB of HBM per device.

v0:
```python
import math

import jax
import jax.numpy as jnp
from jax import lax
from jax.sharding import PartitionSpec as P


def from_behind(block, axis, distance):
    devices = range(lax.axis_size(axis))
    route = [(i - distance, i) for i in devices if i - distance in devices]
    return lax.ppermute(block, axis, route)


def featurize(signals, before, tap_weights):
    tap_count = tap_weights.shape[1]
    length_now = signals.shape[2]
    extended = jnp.concatenate((before, signals), axis=2)
    result = tap_weights[:, 0, :, None] * signals
    for lag_step in range(1, tap_count):
        begin_at = tap_count - 1 - lag_step
        result = (
            result
            + tap_weights[:, lag_step, :, None] * extended[:, :, begin_at : begin_at + length_now]
        )
    return result


def angles(first_ids, second_ids, period):
    return (first_ids * second_ids % period).astype(jnp.float32) * (2.0 * math.pi / period)


def phase_table(row_count, col_count, period):
    rows_ids = jnp.arange(row_count, dtype=jnp.int32)[:, None]
    cols_ids = jnp.arange(col_count, dtype=jnp.int32)[None, :]
    angle_grid = angles(rows_ids, cols_ids, period)
    return (jnp.cos(angle_grid), jnp.sin(angle_grid))


def complex_contract(pattern, left_real, left_imag, table_real, table_imag):

    def contract(left_op, right_op):
        return jnp.einsum(pattern, left_op, right_op, precision=lax.Precision.HIGHEST)

    return (
        contract(left_real, table_real) - contract(left_imag, table_imag),
        contract(left_real, table_imag) + contract(left_imag, table_real),
    )


def long_convolution(drive_signal, long_filter):
    seq_count = lax.axis_size("seq")
    seq_index = lax.axis_index("seq")
    chan_width, block_len = drive_signal.shape
    group_len = block_len // seq_count
    total_len = 2 * block_len * seq_count
    inverse_scale = 1.0 / total_len
    stacked = jnp.stack((drive_signal, long_filter)).reshape(2, chan_width, seq_count, group_len)
    pieces = lax.all_to_all(stacked, "seq", split_axis=2, concat_axis=2, tiled=True)
    local_cols = seq_index * group_len + jnp.arange(group_len, dtype=jnp.int32)
    full_cols = (
        jnp.arange(seq_count, dtype=jnp.int32)[:, None] * group_len
        + jnp.arange(group_len, dtype=jnp.int32)[None, :]
    )
    freq_count = 2 * seq_count
    cos_table, sin_table = phase_table(seq_count, freq_count, freq_count)
    head_real = jnp.einsum("swpj,pc->swcj", pieces, cos_table, precision=lax.Precision.HIGHEST)
    head_imag = -jnp.einsum("swpj,pc->swcj", pieces, sin_table, precision=lax.Precision.HIGHEST)
    turn_angle = angles(
        jnp.arange(freq_count, dtype=jnp.int32)[:, None], local_cols[None, :], total_len
    )
    turn_cos = jnp.cos(turn_angle)
    turn_sin = jnp.sin(turn_angle)
    sent_real = head_real * turn_cos + head_imag * turn_sin
    sent_imag = head_imag * turn_cos - head_real * turn_sin
    outgoing = jnp.stack((sent_real, sent_imag)).reshape(2, 2, chan_width, seq_count, 2, group_len)
    incoming = lax.all_to_all(outgoing, "seq", split_axis=3, concat_axis=3, tiled=True)
    col_real = incoming[0]
    col_imag = incoming[1]
    cos_outer, sin_outer = phase_table(seq_count, seq_count, seq_count)
    section_real, section_imag = complex_contract(
        "swacb,ae->swecb", col_real, col_imag, cos_outer, -sin_outer
    )
    mid_angle = angles(
        jnp.arange(seq_count, dtype=jnp.int32)[:, None],
        jnp.arange(group_len, dtype=jnp.int32)[None, :],
        block_len,
    )
    mid_cos = jnp.cos(mid_angle)[:, None, :]
    mid_sin = jnp.sin(mid_angle)[:, None, :]
    twisted_real = section_real * mid_cos + section_imag * mid_sin
    twisted_imag = section_imag * mid_cos - section_real * mid_sin
    cos_inner, sin_inner = phase_table(group_len, group_len, group_len)
    spec_real, spec_imag = complex_contract(
        "swecb,bf->swecf", twisted_real, twisted_imag, cos_inner, -sin_inner
    )
    prod_real = spec_real[0] * spec_real[1] - spec_imag[0] * spec_imag[1]
    prod_imag = spec_real[0] * spec_imag[1] + spec_imag[0] * spec_real[1]
    reverted_real, reverted_imag = complex_contract(
        "wecf,fb->wecb", prod_real, prod_imag, cos_inner, sin_inner
    )
    untwist_real = reverted_real * mid_cos - reverted_imag * mid_sin
    untwist_imag = reverted_imag * mid_cos + reverted_real * mid_sin
    time_real, time_imag = complex_contract(
        "wecb,ea->wacb", untwist_real, untwist_imag, cos_outer, sin_outer
    )
    col_freq = 2 * seq_index + jnp.arange(2, dtype=jnp.int32)
    undo_angle = angles(full_cols[:, None, :], col_freq[None, :, None], total_len)
    undo_cos = jnp.cos(undo_angle)
    undo_sin = jnp.sin(undo_angle)
    grid_real = time_real * undo_cos - time_imag * undo_sin
    grid_imag = time_imag * undo_cos + time_real * undo_sin
    outgoing = jnp.stack((grid_real, grid_imag))
    incoming = lax.all_to_all(outgoing, "seq", split_axis=2, concat_axis=2, tiled=True)
    recv_real = incoming[0].reshape(chan_width, 2 * seq_count, group_len)
    recv_imag = incoming[1].reshape(chan_width, 2 * seq_count, group_len)
    cos_final, sin_final = phase_table(seq_count, 2 * seq_count, 2 * seq_count)
    result = (
        jnp.einsum("wcj,pc->wpj", recv_real, cos_final, precision=lax.Precision.HIGHEST)
        - jnp.einsum("wcj,pc->wpj", recv_imag, sin_final, precision=lax.Precision.HIGHEST)
    ) * inverse_scale
    settled = lax.all_to_all(result, "seq", split_axis=1, concat_axis=1, tiled=True)
    return settled.reshape(chan_width, block_len)


def local(queries, keys, values, short_taps, long_filter, skip_gain):
    chan_count = lax.axis_size("chan")
    chan_index = lax.axis_index("chan")
    channels_all = queries.shape[0]
    chan_width = channels_all // chan_count
    tap_count = short_taps.shape[1]
    stacked = jnp.stack((queries, keys, values))
    relaid = lax.all_to_all(stacked, "chan", split_axis=1, concat_axis=2, tiled=True)
    block_len = relaid.shape[2]
    rim_cols = relaid[:, :, block_len - (tap_count - 1) :]
    before = from_behind(rim_cols, "seq", 1)
    local_taps = lax.dynamic_slice_in_dim(short_taps, chan_index * chan_width, chan_width, 2)
    filtered = featurize(relaid, before, local_taps)
    drive_signal = filtered[1] * filtered[2]
    local_gain = lax.dynamic_slice_in_dim(skip_gain, chan_index * chan_width, chan_width, 0)
    convolved = long_convolution(drive_signal, long_filter)
    leaving = filtered[0] * (convolved + local_gain[:, None] * drive_signal)
    returned = lax.all_to_all(leaving, "chan", split_axis=1, concat_axis=0, tiled=True)
    return returned


def solution(mesh):
    in_specs = (
        P(None, ("seq", "chan")),
        P(None, ("seq", "chan")),
        P(None, ("seq", "chan")),
        P(),
        P("chan", "seq"),
        P(),
    )
    out_specs = P(None, ("seq", "chan"))
    return jax.shard_map(local, mesh=mesh, in_specs=in_specs, out_specs=out_specs, check_vma=False)
```

profile of v0, /device:TPU:1, one launch (start us, length us, event | category | flops | bytes accessed | tf_op | source)
XLA Modules:
  0.0 420.9 jit_solution(6338618583385626361)
XLA Ops:
  0.0 1.5 stack.39
  3.3 2.7 pad_maximum_fusion.1
  5.9 6.0 %all-to-all-start = ((f32[3,128,1024]{2,0,1:T(4,128)}), f32[3,128,1024]{2,0,1:T(4,128)S(1)}, u32[]{:S(2)}, u32[]{:S(2)}) async-start(f32[3,128,1024]{2,0,1:T(4,128)} %pad_maximum_fusion.1), calls=%async_computation | async-start | bytes 4194304 | tf_op jit(solution)/shard_map/all_to_all | solution.py:133
  12.2 24.9 %all-to-all-done = f32[3,128,1024]{2,0,1:T(4,128)S(1)} async-done(((f32[3,128,1024]{2,0,1:T(4,128)}), f32[3,128,1024]{2,0,1:T(4,128)S(1)}, u32[]{:S(2)}, u32[]{:S(2)}) %all-to-all-start) | async-done | bytes 1572896 | tf_op jit(solution)/shard_map/all_to_all | solution.py:133
  37.1 2.1 copy.94
  39.1 1.6 all_to_all.40
  40.8 5.7 %collective-permute-start = (f32[3,16,2]{2,1,0:T(8,128)S(1)}, f32[3,16,2]{2,1,0:T(8,128)S(1)}, u32[]{:S(2)}, u32[]{:S(2)}) collective-permute-start(f32[3,16,2]{2,1,0:T(8,128)S(1)} %slice.72), channel_id=1, source_target_pairs={{0,8},{8,16},{16,24},{24,32},{32,40},{40,48},{48,56},{56,64},{64,7... | collective-permute-start | bytes 1160 | tf_op jit(solution)/shard_map/ppermute | solution.py:12
  48.6 1.6 copy.33
  50.2 17.1 %all-to-all-start.1 = ((f32[2,16,64,128]{3,1,0,2:T(8,128)}), f32[2,16,64,128]{3,1,0,2:T(8,128)S(1)}, u32[]{:S(2)}, u32[]{:S(2)}) async-start(f32[2,16,64,128]{3,1,0,2:T(8,128)} %copy.33), calls=%async_computation.1 | async-start | bytes 2097152 | tf_op jit(solution)/shard_map/all_to_all | solution.py:59
  67.6 29.9 %all-to-all-done.1 = f32[2,16,64,128]{3,1,0,2:T(8,128)S(1)} async-done(((f32[2,16,64,128]{3,1,0,2:T(8,128)}), f32[2,16,64,128]{3,1,0,2:T(8,128)S(1)}, u32[]{:S(2)}, u32[]{:S(2)}) %all-to-all-start.1) | async-done | bytes 1048608 | tf_op jit(solution)/shard_map/all_to_all | solution.py:59
  97.5 2.4 fusion.36
  100.0 2.9 multiply_add_fusion.1
  102.9 4.0 pad_maximum_fusion
  106.9 4.4 %copy.58 = f32[2,2,16,64,2,128]{5,4,2,1,0,3:T(2,128)} copy(f32[2,2,16,64,2,128]{5,4,3,2,1,0:T(2,128)S(1)} %pad_maximum_fusion) | data formatting | bytes 8388608 | tf_op jit(solution)/shard_map/stack | solution.py:76
  111.3 12.4 %all-to-all-start.2 = ((f32[2,2,16,64,2,128]{5,4,2,1,0,3:T(2,128)}), f32[2,2,16,64,2,128]{5,4,2,1,0,3:T(2,128)}, u32[]{:S(2)}, u32[]{:S(2)}) async-start(f32[2,2,16,64,2,128]{5,4,2,1,0,3:T(2,128)} %copy.58), calls=%async_computation.2 | async-start | bytes 8388608 | tf_op jit(solution)/shard_map/all_to_all | solution.py:77
  124.3 117.8 %all-to-all-done.2 = f32[2,2,16,64,2,128]{5,4,2,1,0,3:T(2,128)} async-done(((f32[2,2,16,64,2,128]{5,4,2,1,0,3:T(2,128)}), f32[2,2,16,64,2,128]{5,4,2,1,0,3:T(2,128)}, u32[]{:S(2)}, u32[]{:S(2)}) %all-to-all-start.2) | async-done | bytes 4194336 | tf_op jit(solution)/shard_map/all_to_all | solution.py:77
  242.1 4.1 fusion.212
  246.2 3.1 fusion.8
  249.3 3.1 fusion.9
  252.4 3.1 fusion.13
  255.6 3.3 fusion.12
  258.8 2.2 fusion.2
  261.0 2.2 fusion
  263.2 2.2 fusion.14
  265.4 2.2 fusion.17
  268.0 1.5 fusion.31
  276.8 1.5 subtract_bitcast_fusion
  278.5 1.6 copy.40
  280.1 83.6 %all_to_all.54 = f32[2,16,64,2,128]{4,3,1,0,2:T(2,128)S(1)} all-to-all(f32[2,16,64,2,128]{4,3,1,0,2:T(2,128)S(1)} %copy.40), channel_id=1, replica_groups=mesh['seq'=64,'chan'=8] {'seq'}, dimensions={2} | all-to-all | bytes 4194304 | tf_op jit(solution)/shard_map/all_to_all | solution.py:114
  367.3 17.4 %all-to-all-start.4 = ((f32[16,64,128]{2,0,1:T(8,128)}), f32[16,64,128]{2,0,1:T(8,128)S(1)}, u32[]{:S(2)}, u32[]{:S(2)}) async-start(f32[16,64,128]{2,0,1:T(8,128)} %copy.45), calls=%async_computation.4 | async-start | bytes 1048576 | tf_op jit(solution)/shard_map/all_to_all | solution.py:122
  385.4 16.3 %all-to-all-done.4 = f32[16,64,128]{2,0,1:T(8,128)S(1)} async-done(((f32[16,64,128]{2,0,1:T(8,128)}), f32[16,64,128]{2,0,1:T(8,128)S(1)}, u32[]{:S(2)}, u32[]{:S(2)}) %all-to-all-start.4) | async-done | bytes 524320 | tf_op jit(solution)/shard_map/all_to_all | solution.py:122
  402.4 17.2 %all_to_all.55 = f32[16,8,1024]{2,0,1:T(8,128)S(1)} all-to-all(f32[16,8,1024]{2,0,1:T(8,128)S(1)} %copy.47), channel_id=1, replica_groups=mesh['seq'=64,'chan'=8] {'chan'}, dimensions={1} | all-to-all | bytes 1048576 | tf_op jit(solution)/shard_map/all_to_all | solution.py:143
  (50 shorter events, 18.6 us)
Async XLA Ops:
  0.0 2.9 copy-start
  5.9 6.0 %copy-start.1 = (f32[16,8192]{1,0:T(8,128)S(1)}, f32[16,8192]{1,0:T(8,128)}, u32[]{:S(2)}) copy-start(f32[16,8192]{1,0:T(8,128)} %param.10) | copy-start | bytes 1572868
  5.9 6.1 %copy-start.2 = (f32[3,3,128]{2,1,0:T(4,128)S(1)}, f32[3,3,128]{2,1,0:T(4,128)}, u32[]{:S(2)}) copy-start(f32[3,3,128]{2,1,0:T(4,128)} %param.9) | copy-start | bytes 13828
  5.9 31.1 %all-to-all-start = ((f32[3,128,1024]{2,0,1:T(4,128)}), f32[3,128,1024]{2,0,1:T(4,128)S(1)}, u32[]{:S(2)}, u32[]{:S(2)}) async-start(f32[3,128,1024]{2,0,1:T(4,128)} %pad_maximum_fusion.1), calls=%async_computation | async-start | bytes 4194304 | tf_op jit(solution)/shard_map/all_to_all | solution.py:133
  40.8 6.7 %collective-permute-start = (f32[3,16,2]{2,1,0:T(8,128)S(1)}, f32[3,16,2]{2,1,0:T(8,128)S(1)}, u32[]{:S(2)}, u32[]{:S(2)}) collective-permute-start(f32[3,16,2]{2,1,0:T(8,128)S(1)} %slice.72), channel_id=1, source_target_pairs={{0,8},{8,16},{16,24},{24,32},{32,40},{40,48},{48,56},{56,64},{64,7... | collective-permute-start | bytes 1160 | tf_op jit(solution)/shard_map/ppermute | solution.py:12
  50.2 47.3 %all-to-all-start.1 = ((f32[2,16,64,128]{3,1,0,2:T(8,128)}), f32[2,16,64,128]{3,1,0,2:T(8,128)S(1)}, u32[]{:S(2)}, u32[]{:S(2)}) async-start(f32[2,16,64,128]{3,1,0,2:T(8,128)} %copy.33), calls=%async_computation.1 | async-start | bytes 2097152 | tf_op jit(solution)/shard_map/all_to_all | solution.py:59
  111.3 130.8 %all-to-all-start.2 = ((f32[2,2,16,64,2,128]{5,4,2,1,0,3:T(2,128)}), f32[2,2,16,64,2,128]{5,4,2,1,0,3:T(2,128)}, u32[]{:S(2)}, u32[]{:S(2)}) async-start(f32[2,2,16,64,2,128]{5,4,2,1,0,3:T(2,128)} %copy.58), calls=%async_computation.2 | async-start | bytes 8388608 | tf_op jit(solution)/shard_map/all_to_all | solution.py:77
  365.1 19.6 %copy-start.3 = (f32[128]{0:T(128)S(1)}, f32[128]{0:T(128)}, u32[]{:S(2)}) copy-start(f32[128]{0:T(128)} %param.11) | copy-start | bytes 1540
  367.3 34.4 %all-to-all-start.4 = ((f32[16,64,128]{2,0,1:T(8,128)}), f32[16,64,128]{2,0,1:T(8,128)S(1)}, u32[]{:S(2)}, u32[]{:S(2)}) async-start(f32[16,64,128]{2,0,1:T(8,128)} %copy.45), calls=%async_computation.4 | async-start | bytes 1048576 | tf_op jit(solution)/shard_map/all_to_all | solution.py:122
where the time goes:
time: 428 us; the launch traced here: 421 us
  waiting for transfers between devices  190 us (44%)
  blocking collectives  101 us (24%)
  starting transfers between devices  58.6 us (14%)
  matrix products  39 us (9%)
  local copies, waits for them, and re-layouts  22.6 us (5%)
  other arithmetic  9.29 us (2%)
    all_to_all x1, waiting for transfers between devices, long_convolution(): lax.all_to_all(outgoing, 'seq', split_axis=3, concat_axis=3, tiled=True)  118 us
    all_to_all x1, blocking collectives, long_convolution(): lax.all_to_all(outgoing, 'seq', split_axis=2, concat_axis=2, tiled=True)  83.6 us
    dot_general x16, matrix products, contract(): jnp.einsum(pattern, left_op, right_op, precision=lax.Precision.HIGHEST)  31.6 us
    all_to_all x1, waiting for transfers between devices, long_convolution(): lax.all_to_all(stacked, 'seq', split_axis=2, concat_axis=2, tiled=True)  29.9 us
    all_to_all x1, waiting for transfers between devices, local(): lax.all_to_all(stacked, 'chan', split_axis=1, concat_axis=2, tiled=True)  24.9 us
    all_to_all x1, starting transfers between devices, long_convolution(): lax.all_to_all(result, 'seq', split_axis=1, concat_axis=1, tiled=True)  17.4 us
    all_to_all x1, blocking collectives, local(): lax.all_to_all(leaving, 'chan', split_axis=1, concat_axis=0, tiled=True)  17.2 us
    all_to_all x1, starting transfers between devices, long_convolution(): lax.all_to_all(stacked, 'seq', split_axis=2, concat_axis=2, tiled=True)  17.1 us
  transfers between devices with their start and end apart: 5, of which 5 were waited for; matrix products, arithmetic and copies ran while one was open for 0% of the time, Pallas kernels for 0%

commit v1 on v0

v1 whole, which is shorter than its diff:
```python
import functools

import jax
import jax.numpy as jnp
import numpy as np
from jax import lax
from jax.experimental import pallas as pl
from jax.experimental.pallas import tpu as pltpu
from jax.sharding import PartitionSpec as P


BF = jnp.bfloat16
F32 = jnp.float32
GROUP = 4
ROWS = 512
COLS = 1024
QUARTER = COLS // GROUP
MINE = ROWS // GROUP
LANES = 128
TOTAL = ROWS * COLS


def halves(values):
    high = np.asarray(values, np.float32).astype(jnp.bfloat16)
    low = (np.asarray(values, np.float64) - high.astype(np.float64)).astype(np.float32).astype(jnp.bfloat16)
    return high, low


@functools.lru_cache(maxsize=None)
def tables():
    k1 = np.arange(ROWS, dtype=np.float64)[:, None] + 0.25
    p = np.arange(ROWS, dtype=np.float64)[None, :]
    angle = 2.0 * np.pi * k1 * p / ROWS
    cos, sin = np.cos(angle), np.sin(angle)
    outer = np.stack((cos.reshape(GROUP, MINE, ROWS), -sin.reshape(GROUP, MINE, ROWS)), 1).reshape(2 * ROWS, ROWS)
    forward = halves(outer)
    backward = halves(outer.T / TOTAL)
    j = np.arange(COLS, dtype=np.float64)[None, :]
    turn = 2.0 * np.pi * k1 * j / TOTAL
    turns = np.stack((np.cos(turn).reshape(GROUP, MINE, COLS), -np.sin(turn).reshape(GROUP, MINE, COLS)), 1)
    i = np.arange(QUARTER, dtype=np.float64)
    small = 2.0 * np.pi * np.arange(GROUP)[:, None] * i[None, :] / COLS
    steps = np.stack((np.cos(small), -np.sin(small)), 1).reshape(2 * GROUP, QUARTER)
    inner = 2.0 * np.pi * np.outer(i, i) / QUARTER
    inner_high, inner_low = halves(np.concatenate((np.cos(inner), -np.sin(inner)), 1))
    inner3 = np.concatenate((inner_high, inner_high, inner_low), 0)
    return forward, backward, turns.astype(np.float32), steps.astype(np.float32), inner3


def split(x):
    high = x.astype(BF)
    return high, (x - high.astype(F32)).astype(BF)


def mm(a, b):
    return jnp.dot(a, b, preferred_element_type=F32)


def pack_rows(out_ref, chan, values, base):
    for quarter in range(GROUP):
        for half in range(2):
            at = (2 * quarter + half) * LANES
            out_ref[pl.ds(16 * quarter + 2 * chan + half, 16, stride=64), :] = values[:, base + at : base + at + LANES]


def pack_filter_kernel(filter_ref, out_ref):
    for chan in range(8):
        pack_rows(out_ref, chan, filter_ref[:, chan * COLS : (chan + 1) * COLS], 0)


def feature(signal, taps, older, newer):
    lane = lax.broadcasted_iota(jnp.int32, signal.shape, 1)
    one = jnp.where(lane == 0, newer, pltpu.roll(signal, 1, 1))
    two = jnp.where(lane == 0, older, jnp.where(lane == 1, newer, pltpu.roll(signal, 2, 1)))
    return taps[0] * signal + taps[1] * one + taps[2] * two


def drive_kernel(keys_ref, values_ref, small_ref, packed_ref, drive_ref):
    for chan in range(8):
        rows = slice(16 * chan, 16 * chan + 16)
        col = lambda n: small_ref[rows, n : n + 1]
        key = feature(keys_ref[rows, :], [col(3), col(4), col(5)], col(12), col(13))
        value = feature(values_ref[rows, :], [col(6), col(7), col(8)], col(14), col(15))
        drive = key * value
        drive_ref[rows, :] = drive
        pack_rows(packed_ref, chan, drive, 0)


def gate_kernel(queries_ref, drive_ref, small_ref, gain_ref, direct_ref):
    for chan in range(8):
        rows = slice(16 * chan, 16 * chan + 16)
        col = lambda n: small_ref[rows, n : n + 1]
        query = feature(queries_ref[rows, :], [col(0), col(1), col(2)], col(10), col(11))
        gain_ref[rows, :] = query
        direct_ref[rows, :] = query * (col(9) * drive_ref[rows, :])


def finish_kernel(rows_ref, gain_ref, direct_ref, out_ref):
    for chan in range(8):
        rows = slice(16 * chan, 16 * chan + 16)
        for quarter in range(GROUP):
            for half in range(2):
                at = (2 * quarter + half) * LANES
                got = rows_ref[pl.ds(16 * quarter + 2 * chan + half, 16, stride=64), :]
                out_ref[rows, at : at + LANES] = gain_ref[rows, at : at + LANES] * got + direct_ref[rows, at : at + LANES]


def outer_kernel(me_ref, x_ref, high_ref, low_ref, *refs):
    outs, (xh_ref, xl_ref) = refs[:GROUP], refs[GROUP:]
    step = pl.program_id(0)

    @pl.when(step == 0)
    def _():
        for half in range(2):
            high, low = split(x_ref[pl.ds(half, ROWS, stride=2), :])
            xh_ref[:, half * LANES : (half + 1) * LANES] = high
            xl_ref[:, half * LANES : (half + 1) * LANES] = low

    xh = xh_ref[...]
    value = mm(high_ref[...], xh) + mm(high_ref[...], xl_ref[...]) + mm(low_ref[...], xh)
    for mask in range(GROUP):

        @pl.when(step == mask)
        def _(mask=mask):
            outs[mask][...] = value


def gather(me, pieces, held_ref):
    for mask in range(GROUP):
        held_ref[me ^ mask] = pieces[mask][...]


def butterfly(parts, sign):
    (ar, ai), (br, bi), (cr, ci), (dr, di) = parts
    er, ei, fr, fi = ar + cr, ai + ci, ar - cr, ai - ci
    gr, gi, hr, hi = br + dr, bi + di, sign * (br - dr), sign * (bi - di)
    return [(er + gr, ei + gi), (fr - hi, fi + hr), (er - gr, ei - gi), (fr + hi, fi - hr)]


def inner_product(real, imag, inner_ref):
    high, low = split(jnp.concatenate((real, imag), 0))
    result = mm(jnp.concatenate((high, low, high), 1), inner_ref[...])
    return result[:MINE, :QUARTER], result[:MINE, QUARTER:], result[MINE:, :QUARTER], result[MINE:, QUARTER:]


def spectrum(held_ref, turn_ref, step_ref, inner_ref):
    parts = []
    for s in range(GROUP):
        real, imag = held_ref[s, :MINE, :], held_ref[s, MINE:, :]
        cos, sin = turn_ref[0, 0, :, s * QUARTER : (s + 1) * QUARTER], turn_ref[0, 1, :, s * QUARTER : (s + 1) * QUARTER]
        parts.append((real * cos - imag * sin, real * sin + imag * cos))
    result = []
    for r, (real, imag) in enumerate(butterfly(parts, -1.0)):
        if r:
            cos, sin = step_ref[2 * r : 2 * r + 1, :], step_ref[2 * r + 1 : 2 * r + 2, :]
            real, imag = real * cos - imag * sin, real * sin + imag * cos
        rr, ri, ir, ii = inner_product(real, imag, inner_ref)
        result.append((rr - ii, ri + ir))
    return result


def filter_kernel(me_ref, p0, p1, p2, p3, turn_ref, step_ref, inner_ref, out_ref, held_ref):
    gather(me_ref[0], (p0, p1, p2, p3), held_ref)
    for r, (real, imag) in enumerate(spectrum(held_ref, turn_ref, step_ref, inner_ref)):
        out_ref[r, :MINE, :] = real
        out_ref[r, MINE:, :] = imag


def product_kernel(me_ref, p0, p1, p2, p3, filter_ref, turn_ref, step_ref, inner_ref, o0, o1, o2, o3, held_ref):
    me = me_ref[0]
    gather(me, (p0, p1, p2, p3), held_ref)
    parts = []
    for r, (real, imag) in enumerate(spectrum(held_ref, turn_ref, step_ref, inner_ref)):
        fr, fi = filter_ref[r, :MINE, :], filter_ref[r, MINE:, :]
        rr, ri, ir, ii = inner_product(real * fr - imag * fi, real * fi + imag * fr, inner_ref)
        real, imag = rr + ii, ir - ri
        if r:
            cos, sin = step_ref[2 * r : 2 * r + 1, :], step_ref[2 * r + 1 : 2 * r + 2, :]
            real, imag = real * cos + imag * sin, imag * cos - real * sin
        parts.append((real, imag))
    for s, (real, imag) in enumerate(butterfly(parts, 1.0)):
        cos, sin = turn_ref[0, 0, :, s * QUARTER : (s + 1) * QUARTER], turn_ref[0, 1, :, s * QUARTER : (s + 1) * QUARTER]
        held_ref[s, :MINE, :] = real * cos + imag * sin
        held_ref[s, MINE:, :] = imag * cos - real * sin
    for mask, out_ref in enumerate((o0, o1, o2, o3)):
        out_ref[...] = held_ref[me ^ mask]


def back_kernel(me_ref, p0, p1, p2, p3, high_ref, low_ref, out_ref, held_ref, zh_ref, zl_ref):
    @pl.when(pl.program_id(0) == 0)
    def _():
        gather(me_ref[0], (p0, p1, p2, p3), held_ref)
        for s in range(GROUP):
            high, low = split(held_ref[s])
            zh_ref[s * 2 * MINE : (s + 1) * 2 * MINE, :] = high
            zl_ref[s * 2 * MINE : (s + 1) * 2 * MINE, :] = low

    zh = zh_ref[...]
    value = mm(high_ref[...], zh) + mm(high_ref[...], zl_ref[...]) + mm(low_ref[...], zh)
    for half in range(2):
        out_ref[pl.ds(half, MINE, stride=2), :] = value[:, half * LANES : (half + 1) * LANES]


VMEM_LIMIT = 40 * 1024 * 1024


def call(kernel, out_shapes, args, grid=None, in_specs=None, out_specs=None, scratch=(), prefetch=0, flops=0):
    nbytes = sum(a.size * a.dtype.itemsize for a in args) + sum(int(np.prod(s.shape)) * 4 for s in out_shapes)
    single = len(out_shapes) == 1
    whole = lambda s: pl.BlockSpec(s.shape, lambda *_, n=len(s.shape): (0,) * n)
    in_specs = in_specs or [whole(a) for a in args[prefetch:]]
    out_specs = out_specs or [whole(s) for s in out_shapes]
    return pl.pallas_call(
        kernel,
        out_shape=out_shapes[0] if single else out_shapes,
        grid_spec=pltpu.PrefetchScalarGridSpec(
            num_scalar_prefetch=prefetch,
            grid=grid or (1,),
            in_specs=in_specs,
            out_specs=out_specs[0] if single else out_specs,
            scratch_shapes=list(scratch),
        ),
        compiler_params=pltpu.CompilerParams(vmem_limit_bytes=VMEM_LIMIT),
        cost_estimate=pl.CostEstimate(flops=flops, bytes_accessed=nbytes, transcendentals=0),
    )(*args)


def shape(*dims):
    return jax.ShapeDtypeStruct(dims, F32)


PIECE = (2 * MINE, QUARTER)


def exchange(pieces):
    moved = [pieces[0]]
    for mask in (2, 3, 1):
        size = lax.axis_size("seq")
        moved.append(lax.ppermute(pieces[mask], "seq", [(i, i ^ mask) for i in range(size)]))
    return [moved[0], moved[3], moved[1], moved[2]]


def outer(me, rows, forward):
    block = pl.BlockSpec((2 * MINE, ROWS), lambda i, me: (me[0] ^ i, 0))
    whole = pl.BlockSpec((2 * ROWS, LANES), lambda i, me: (0, 0))
    return call(
        outer_kernel,
        [shape(*PIECE)] * GROUP,
        (me, rows, *forward),
        grid=(GROUP,),
        in_specs=[whole, block, block],
        out_specs=[pl.BlockSpec(PIECE, lambda i, me: (0, 0))] * GROUP,
        scratch=[pltpu.VMEM((ROWS, QUARTER), BF)] * 2,
        prefetch=1,
        flops=3 * 2 * 2 * ROWS * ROWS * QUARTER,
    )


def middle(kernel, me, pieces, extra, turns, steps, inner3, outs, flops):
    whole = lambda s: pl.BlockSpec(s.shape, lambda i, me, n=len(s.shape): (0,) * n)
    turn = pl.BlockSpec((1, 2, MINE, COLS), lambda i, me: (me[0], 0, 0, 0))
    return call(
        kernel,
        outs,
        (me, *pieces, *extra, turns, steps, inner3),
        in_specs=[whole(a) for a in (*pieces, *extra)] + [turn, whole(steps), whole(inner3)],
        scratch=[pltpu.VMEM((GROUP, *PIECE), F32)],
        prefetch=1,
        flops=flops,
    )


def back(me, pieces, backward):
    block = pl.BlockSpec((MINE, 2 * ROWS), lambda i, me: (i, 0))
    piece = pl.BlockSpec(PIECE, lambda i, me: (0, 0))
    return call(
        back_kernel,
        [shape(2 * ROWS, LANES)],
        (me, *pieces, *backward),
        grid=(GROUP,),
        in_specs=[piece] * GROUP + [block, block],
        out_specs=[pl.BlockSpec((2 * MINE, LANES), lambda i, me: (i, 0))],
        scratch=[pltpu.VMEM((GROUP, *PIECE), F32)] + [pltpu.VMEM((2 * ROWS, QUARTER), BF)] * 2,
        prefetch=1,
        flops=3 * 2 * 2 * ROWS * ROWS * QUARTER,
    )


def swap(rows, axes, count):
    moved = lax.all_to_all(rows.reshape(count, -1, LANES), axes, 0, 0, tiled=True)
    return moved.reshape(2 * ROWS, LANES)


def local(queries, keys, values, short_taps, long_filter, skip_gain):
    everyone = ("seq", "chan")
    forward, backward, turns, steps, inner3 = jax.tree.map(jnp.asarray, tables())
    me = (lax.axis_index("seq") % GROUP).astype(jnp.int32).reshape(1)
    channels = queries.shape[0]

    filter_rows = call(pack_filter_kernel, [shape(2 * ROWS, LANES)], (long_filter,))
    filter_rows = swap(filter_rows, "seq", lax.axis_size("seq"))

    edges = jnp.stack((queries[:, -2], queries[:, -1], keys[:, -2], keys[:, -1], values[:, -2], values[:, -1]))
    size = lax.axis_size(everyone)
    before = lax.ppermute(edges, everyone, [(i, i + 1) for i in range(size - 1)])
    small = jnp.concatenate((short_taps.reshape(9, channels), skip_gain[None], before)).T
    packed, drive = call(drive_kernel, [shape(2 * ROWS, LANES), shape(channels, COLS)], (keys, values, small))
    drive_rows = swap(packed, everyone, size)

    middle_flops = 3 * 2 * 1024 * 256 * 512
    filter_pieces = exchange(outer(me, filter_rows, forward))
    spectra = middle(filter_kernel, me, filter_pieces, (), turns, steps, inner3, [shape(GROUP, *PIECE)], middle_flops)

    pieces = exchange(outer(me, drive_rows, forward))
    pieces = middle(
        product_kernel, me, pieces, (spectra,), turns, steps, inner3, [shape(*PIECE)] * GROUP, 2 * middle_flops
    )
    result = back(me, exchange(pieces), backward)
    gain, direct = call(gate_kernel, [shape(channels, COLS)] * 2, (queries, drive, small))
    returned = swap(result, everyone, size)
    return call(finish_kernel, [shape(channels, COLS)], (returned, gain, direct))


def solution(mesh):
    spread = P(None, ("seq", "chan"))
    in_specs = (spread, spread, spread, P(), P("chan", "seq"), P())
    return jax.shard_map(local, mesh=mesh, in_specs=in_specs, out_specs=spread, check_vma=False)
```

time: 428 us -> 156 us (0.36); the launches traced: 421 us -> 155 us
  waiting for transfers between devices: 190 us -> 49.8 us
  blocking collectives: 101 us -> 0 us
  matrix products: 39 us -> 0 us
  Pallas kernels: 0 us -> 15.5 us
  starting transfers between devices: 58.6 us -> 74.1 us
  other arithmetic: 9.29 us -> 0.66 us
  local copies, waits for them, and re-layouts: 22.6 us -> 14.4 us
    all_to_all x4 -> x3, waiting for transfers between devices: 189 us -> 28 us  [swap(): lax.all_to_all(rows.reshape(count, -1, LANES), axes, 0, 0, tiled=True)]
    all_to_all x2 -> x0, blocking collectives: 101 us -> none  [the longest x1 83.6 us: long_convolution(): lax.all_to_all(outgoing, 'seq', split_axis=2, concat_axis=2, tiled=True)]
    dot_general x20 -> x0, matrix products: 39 us -> none  [the longest x16 31.6 us: contract(): jnp.einsum(pattern, left_op, right_op, precision=lax.Precision.HIGHEST)]
    ppermute x1 -> x10, starting transfers between devices: 5.73 us -> 31.7 us  [the longest x9 28.5 us: exchange(): lax.ppermute(pieces[mask], 'seq', [(i, i ^ mask) for i in range(size)])]
    ppermute x1 -> x10, waiting for transfers between devices: 0.9 us -> 21.7 us  [the longest x9 16.4 us: exchange(): lax.ppermute(pieces[mask], 'seq', [(i, i ^ mask) for i in range(size)])]
    pallas_call x0 -> x9, Pallas kernels: none -> 15.5 us  [call(): pl.pallas_call(kernel, out_shape=out_shapes[0] if single else out_shapes,...]
    another operation x7 -> x1, local copies, waits for them, and re-layouts: 10.9 us -> 0.03 us  [local(): jnp.stack((queries[:, -2], queries[:, -1], keys[:, -2], keys[:, -1], valu...]
    all_to_all x4 -> x3, starting transfers between devices: 52.9 us -> 42.4 us  [swap(): lax.all_to_all(rows.reshape(count, -1, LANES), axes, 0, 0, tiled=True)]
  transfers between devices with their start and end apart: 5 -> 13, of which waited for: 5 -> 8; matrix products, arithmetic and copies ran while one was open for 0% -> 3% of each run, Pallas kernels for 0% -> 5%
where the time goes in v1:
time: 156 us; the launch traced here: 155 us
  starting transfers between devices  74.1 us (47%)
  waiting for transfers between devices  49.8 us (32%)
  Pallas kernels  15.5 us (10%)
  local copies, waits for them, and re-layouts  14.4 us (9%)
    all_to_all x3, starting transfers between devices, swap(): lax.all_to_all(rows.reshape(count, -1, LANES), axes, 0, 0, tiled=True)  42.4 us
    ppermute x9, starting transfers between devices, exchange(): lax.ppermute(pieces[mask], 'seq', [(i, i ^ mask) for i in range(size)])  28.5 us
    all_to_all x3, waiting for transfers between devices, swap(): lax.all_to_all(rows.reshape(count, -1, LANES), axes, 0, 0, tiled=True)  28 us
    ppermute x9, waiting for transfers between devices, exchange(): lax.ppermute(pieces[mask], 'seq', [(i, i ^ mask) for i in range(size)])  16.4 us
    pallas_call x9, Pallas kernels, call(): pl.pallas_call(kernel, out_shape=out_shapes[0] if single else out_shapes,...  15.5 us
    unnamed x28, local copies, waits for them, and re-layouts  10.2 us
    ppermute x1, waiting for transfers between devices, local(): lax.ppermute(edges, everyone, [(i, i + 1) for i in range(size - 1)])  5.32 us
  transfers between devices with their start and end apart: 13, of which 8 were waited for; matrix products, arithmetic and copies ran while one was open for 3% of the time, Pallas kernels for 5%

profile of v1, /device:TPU:1, one launch (start us, length us, event | category | flops | bytes accessed | tf_op | source)
XLA Modules:
  0.0 154.7 jit_solution(13128878643412109231)
XLA Ops:
  1.0 1.2 shard_map.129
  2.3 17.6 %all-to-all-start.1 = ((f32[64,16,128]{2,1,0:T(8,128)}), f32[64,16,128]{2,1,0:T(8,128)S(1)}, u32[]{:S(2)}, u32[]{:S(2)}) async-start(f32[64,16,128]{2,1,0:T(8,128)} %bitcast.5), calls=%async_computation.1 | async-start | bytes 1048576 | tf_op jit(solution)/shard_map/all_to_all | solution.py:290
  23.3 3.1 %collective-permute-start = (f32[6,128]{1,0:T(8,128)S(1)}, f32[6,128]{1,0:T(8,128)S(1)}, u32[]{:S(2)}, u32[]{:S(2)}) collective-permute-start(f32[6,128]{1,0:T(8,128)S(1)} %stack.3), channel_id=1, source_target_pairs={{0,1},{1,2},{2,3},{3,4},{4,5},{5,6},{6,7},{7,8},{8,9},{9,10},{10,1... | collective-permute-start | bytes 9224 | tf_op jit(solution)/shard_map/ppermute | solution.py:305
  27.1 5.3 %collective-permute-done = f32[6,128]{1,0:T(8,128)S(1)} collective-permute-done((f32[6,128]{1,0:T(8,128)S(1)}, f32[6,128]{1,0:T(8,128)S(1)}, u32[]{:S(2)}, u32[]{:S(2)}) %collective-permute-start) | collective-permute-done | bytes 3104 | tf_op jit(solution)/shard_map/ppermute | solution.py:305
  35.3 2.0 %shard_map.127 = (f32[1024,128]{1,0:T(8,128)}, f32[128,1024]{1,0:T(8,128)S(1)}) custom-call(f32[128,1024]{1,0:T(8,128)S(1)} %copy-done.5, f32[128,1024]{1,0:T(8,128)S(1)} %copy-done.6, f32[128,16]{1,0:T(8,128)S(1)} %bitcast.16), custom_call_target="tpu_custom_call" | custom-call | bytes 2105344 | tf_op jit(solution)/shard_map/pallas_call | solution.py:213
  37.3 1.3 all-to-all-done.1
  38.7 16.2 %all-to-all-start = ((f32[512,2,128]{2,1,0:T(2,128)}), f32[512,2,128]{2,1,0:T(2,128)S(1)}, u32[]{:S(2)}, u32[]{:S(2)}) async-start(f32[512,2,128]{2,1,0:T(2,128)} %bitcast.3), calls=%async_computation | async-start | bytes 1048576 | tf_op jit(solution)/shard_map/all_to_all | solution.py:290
  54.9 1.2 copy-done.10
  56.2 1.2 copy-done.12
  57.4 2.4 %shard_map.130 = (f32[256,256]{1,0:T(8,128)S(1)}, f32[256,256]{1,0:T(8,128)}, f32[256,256]{1,0:T(8,128)S(1)}, f32[256,256]{1,0:T(8,128)S(1)}) custom-call(s32[1]{0:T(128)} %bitcast.me_ref, f32[1024,128]{1,0:T(8,128)S(1)} %bitcast.18, bf16[1024,512]{1,0:T(8,128)(2,1)S(1)} %copy-done.12, bf16[1024,512]{1,0:T(8,128)(2,1)S(1)} %copy-done.10), custom_call_target="tpu_custom_call" | custom-call | flops 805306368 | bytes 3670020 | tf_op jit(solution)/shard_map/pallas_call | solution.py:213
  59.8 6.2 %collective-permute-start.4 = (f32[256,256]{1,0:T(8,128)}, f32[256,256]{1,0:T(8,128)S(1)}, u32[]{:S(2)}, u32[]{:S(2)}) collective-permute-start(f32[256,256]{1,0:T(8,128)} %get-tuple-element.27), channel_id=1, source_target_pairs={{0,8},{8,0},{16,24},{24,16},{32,40},{40,32},{48,56},{56,48},{64,72... | collective-permute-start | bytes 786440 | tf_op jit(solution)/shard_map/ppermute | solution.py:239
  66.0 1.9 %collective-permute-start.5 = (f32[256,256]{1,0:T(8,128)S(1)}, f32[256,256]{1,0:T(8,128)S(1)}, u32[]{:S(2)}, u32[]{:S(2)}) collective-permute-start(f32[256,256]{1,0:T(8,128)S(1)} %get-tuple-element.28), channel_id=1, source_target_pairs={{0,16},{8,24},{16,0},{24,8},{32,48},{40,56},{48,32},{56,40},{64,80... | collective-permute-start | bytes 786440 | tf_op jit(solution)/shard_map/ppermute | solution.py:239
  67.9 3.5 %collective-permute-start.6 = (f32[256,256]{1,0:T(8,128)S(1)}, f32[256,256]{1,0:T(8,128)S(1)}, u32[]{:S(2)}, u32[]{:S(2)}) collective-permute-start(f32[256,256]{1,0:T(8,128)S(1)} %get-tuple-element.29), channel_id=1, source_target_pairs={{0,24},{8,16},{16,8},{24,0},{32,56},{40,48},{48,40},{56,32},{64,88... | collective-permute-start | bytes 786440 | tf_op jit(solution)/shard_map/ppermute | solution.py:239
  71.5 5.3 %all-to-all-done = f32[512,2,128]{2,1,0:T(2,128)S(1)} async-done(((f32[512,2,128]{2,1,0:T(2,128)}), f32[512,2,128]{2,1,0:T(2,128)S(1)}, u32[]{:S(2)}, u32[]{:S(2)}) %all-to-all-start) | async-done | bytes 524320 | tf_op jit(solution)/shard_map/all_to_all | solution.py:290
  76.8 1.2 copy-done.11
  78.0 1.2 copy-done.13
  79.3 1.7 %shard_map.128 = (f32[256,256]{1,0:T(8,128)S(1)}, f32[256,256]{1,0:T(8,128)S(1)}, f32[256,256]{1,0:T(8,128)S(1)}, f32[256,256]{1,0:T(8,128)S(1)}) custom-call(s32[1]{0:T(128)} %bitcast.me_ref, f32[1024,128]{1,0:T(8,128)S(1)} %bitcast.19, bf16[1024,512]{1,0:T(8,128)(2,1)S(1)} %copy-done.13, bf16[1024,512]{1,0:T(8,128)(2,1)S(1)} %copy-done.11), custom_call_target="tpu_custom_call" | custom-call | flops 805306368 | bytes 3670020 | tf_op jit(solution)/shard_map/pallas_call | solution.py:213
  81.0 3.6 %collective-permute-start.1 = (f32[256,256]{1,0:T(8,128)S(1)}, f32[256,256]{1,0:T(8,128)S(1)}, u32[]{:S(2)}, u32[]{:S(2)}) collective-permute-start(f32[256,256]{1,0:T(8,128)S(1)} %get-tuple-element.23), channel_id=1, source_target_pairs={{0,8},{8,0},{16,24},{24,16},{32,40},{40,32},{48,56},{56,48},{64,72... | collective-permute-start | bytes 786440 | tf_op jit(solution)/shard_map/ppermute | solution.py:239
  84.6 2.8 %collective-permute-start.2 = (f32[256,256]{1,0:T(8,128)S(1)}, f32[256,256]{1,0:T(8,128)S(1)}, u32[]{:S(2)}, u32[]{:S(2)}) collective-permute-start(f32[256,256]{1,0:T(8,128)S(1)} %get-tuple-element.24), channel_id=1, source_target_pairs={{0,16},{8,24},{16,0},{24,8},{32,48},{40,56},{48,32},{56,40},{64,80... | collective-permute-start | bytes 786440 | tf_op jit(solution)/shard_map/ppermute | solution.py:239
  87.3 2.7 %collective-permute-start.3 = (f32[256,256]{1,0:T(8,128)S(1)}, f32[256,256]{1,0:T(8,128)S(1)}, u32[]{:S(2)}, u32[]{:S(2)}) collective-permute-start(f32[256,256]{1,0:T(8,128)S(1)} %get-tuple-element.25), channel_id=1, source_target_pairs={{0,24},{8,16},{16,8},{24,0},{32,56},{40,48},{48,40},{56,32},{64,88... | collective-permute-start | bytes 786440 | tf_op jit(solution)/shard_map/ppermute | solution.py:239
  90.1 2.2 %copy-done = f32[4,2,128,1024]{3,2,1,0:T(8,128)S(1)} copy-done((f32[4,2,128,1024]{3,2,1,0:T(8,128)S(1)}, f32[4,2,128,1024]{3,2,1,0:T(8,128)}, u32[]{:S(2)}) %copy-start) | copy-done | bytes 4194328
  92.3 1.2 shard_map.131.filter_ref
  94.4 5.7 %collective-permute-done.3.p3 = f32[256,256]{1,0:T(8,128)S(1)} collective-permute-done((f32[256,256]{1,0:T(8,128)S(1)}, f32[256,256]{1,0:T(8,128)S(1)}, u32[]{:S(2)}, u32[]{:S(2)}) %collective-permute-start.3) | collective-permute-done | bytes 262176 | tf_op jit(solution)/shard_map/ppermute | solution.py:239
  100.1 2.5 %shard_map.132 = (f32[256,256]{1,0:T(8,128)S(1)}, f32[256,256]{1,0:T(8,128)S(1)}, f32[256,256]{1,0:T(8,128)S(1)}, f32[256,256]{1,0:T(8,128)S(1)}) custom-call(s32[1]{0:T(128)} %bitcast.me_ref, f32[256,256]{1,0:T(8,128)S(1)} %get-tuple-element.22.p0, f32[256,256]{1,0:T(8,128)S(1)} %collective-permute-done.1.p1, f32[256,256]{1,0:T(8,128)S(1)} %collective-permute-done.2.p2, ...), custom_call_target="tpu_custom_call" | custom-call | flops 1610612736 | bytes 8134660 | tf_op jit(solution)/shard_map/pallas_call | solution.py:213
  102.6 2.2 %collective-permute-start.7 = (f32[256,256]{1,0:T(8,128)S(1)}, f32[256,256]{1,0:T(8,128)S(1)}, u32[]{:S(2)}, u32[]{:S(2)}) collective-permute-start(f32[256,256]{1,0:T(8,128)S(1)} %get-tuple-element.31), channel_id=1, source_target_pairs={{0,8},{8,0},{16,24},{24,16},{32,40},{40,32},{48,56},{56,48},{64,72... | collective-permute-start | bytes 786440 | tf_op jit(solution)/shard_map/ppermute | solution.py:239
  104.8 2.8 %collective-permute-start.8 = (f32[256,256]{1,0:T(8,128)S(1)}, f32[256,256]{1,0:T(8,128)S(1)}, u32[]{:S(2)}, u32[]{:S(2)}) collective-permute-start(f32[256,256]{1,0:T(8,128)S(1)} %get-tuple-element.32), channel_id=1, source_target_pairs={{0,16},{8,24},{16,0},{24,8},{32,48},{40,56},{48,32},{56,40},{64,80... | collective-permute-start | bytes 786440 | tf_op jit(solution)/shard_map/ppermute | solution.py:239
  107.6 2.9 %collective-permute-start.9 = (f32[256,256]{1,0:T(8,128)S(1)}, f32[256,256]{1,0:T(8,128)S(1)}, u32[]{:S(2)}, u32[]{:S(2)}) collective-permute-start(f32[256,256]{1,0:T(8,128)S(1)} %get-tuple-element.33), channel_id=1, source_target_pairs={{0,24},{8,16},{16,8},{24,0},{32,56},{40,48},{48,40},{56,32},{64,88... | collective-permute-start | bytes 786440 | tf_op jit(solution)/shard_map/ppermute | solution.py:239
  110.5 3.9 %collective-permute-done.8.p2 = f32[256,256]{1,0:T(8,128)S(1)} collective-permute-done((f32[256,256]{1,0:T(8,128)S(1)}, f32[256,256]{1,0:T(8,128)S(1)}, u32[]{:S(2)}, u32[]{:S(2)}) %collective-permute-start.8) | collective-permute-done | bytes 262176 | tf_op jit(solution)/shard_map/ppermute | solution.py:239
  114.4 6.0 %collective-permute-done.9.p3 = f32[256,256]{1,0:T(8,128)S(1)} collective-permute-done((f32[256,256]{1,0:T(8,128)S(1)}, f32[256,256]{1,0:T(8,128)S(1)}, u32[]{:S(2)}, u32[]{:S(2)}) %collective-permute-start.9) | collective-permute-done | bytes 262176 | tf_op jit(solution)/shard_map/ppermute | solution.py:239
  120.4 2.7 %shard_map.133 = f32[1024,128]{1,0:T(8,128)} custom-call(s32[1]{0:T(128)} %bitcast.me_ref, f32[256,256]{1,0:T(8,128)S(1)} %get-tuple-element.30.p0, f32[256,256]{1,0:T(8,128)S(1)} %collective-permute-done.7.p1, f32[256,256]{1,0:T(8,128)S(1)} %collective-permute-done.8.p2, f32[256,256]{1,0:T(8,128)S(1)} %collective-permute-done.9.p3, ...), custom_call_target="tpu_custom_call" | custom-call | flops 805306368 | bytes 3670020 | tf_op jit(solution)/shard_map/pallas_call | solution.py:213
  123.1 8.6 %all-to-all-start.2 = ((f32[512,2,128]{2,1,0:T(2,128)}), f32[512,2,128]{2,1,0:T(2,128)S(1)}, u32[]{:S(2)}, u32[]{:S(2)}) async-start(f32[512,2,128]{2,1,0:T(2,128)} %bitcast.7), calls=%async_computation.2 | async-start | bytes 1048576 | tf_op jit(solution)/shard_map/all_to_all | solution.py:290
  132.2 21.4 %all-to-all-done.2 = f32[512,2,128]{2,1,0:T(2,128)S(1)} async-done(((f32[512,2,128]{2,1,0:T(2,128)}), f32[512,2,128]{2,1,0:T(2,128)S(1)}, u32[]{:S(2)}, u32[]{:S(2)}) %all-to-all-start.2) | async-done | bytes 524320 | tf_op jit(solution)/shard_map/all_to_all | solution.py:290
  (38 shorter events, 10.5 us)
Async XLA Ops:
  0.0 1.0 copy-start.8
  2.3 36.4 %all-to-all-start.1 = ((f32[64,16,128]{2,1,0:T(8,128)}), f32[64,16,128]{2,1,0:T(8,128)S(1)}, u32[]{:S(2)}, u32[]{:S(2)}) async-start(f32[64,16,128]{2,1,0:T(8,128)} %bitcast.5), calls=%async_computation.1 | async-start | bytes 1048576 | tf_op jit(solution)/shard_map/all_to_all | solution.py:290
  21.0 69.0 %copy-start.9 = (f32[8,256]{1,0:T(8,128)S(1)}, f32[8,256]{1,0:T(8,128)}, u32[]{:S(2)}) copy-start(f32[8,256]{1,0:T(8,128)} %constant.38.clone.step_ref) | copy-start | bytes 24580
  22.1 67.9 %copy-start.2 = (bf16[768,512]{1,0:T(8,128)(2,1)S(1)}, bf16[768,512]{1,0:T(8,128)(2,1)}, u32[]{:S(2)}) copy-start(bf16[768,512]{1,0:T(8,128)(2,1)} %constant.39.clone.inner_ref) | copy-start | bytes 2359300
  23.3 9.1 %collective-permute-start = (f32[6,128]{1,0:T(8,128)S(1)}, f32[6,128]{1,0:T(8,128)S(1)}, u32[]{:S(2)}, u32[]{:S(2)}) collective-permute-start(f32[6,128]{1,0:T(8,128)S(1)} %stack.3), channel_id=1, source_target_pairs={{0,1},{1,2},{2,3},{3,4},{4,5},{5,6},{6,7},{7,8},{8,9},{9,10},{10,1... | collective-permute-start | bytes 9224 | tf_op jit(solution)/shard_map/ppermute | solution.py:305
  33.2 1.0 copy-start.5
  34.3 1.0 copy-start.6
  38.7 38.1 %all-to-all-start = ((f32[512,2,128]{2,1,0:T(2,128)}), f32[512,2,128]{2,1,0:T(2,128)S(1)}, u32[]{:S(2)}, u32[]{:S(2)}) async-start(f32[512,2,128]{2,1,0:T(2,128)} %bitcast.3), calls=%async_computation | async-start | bytes 1048576 | tf_op jit(solution)/shard_map/all_to_all | solution.py:290
  54.9 1.2 copy-start.10
  56.2 1.2 copy-start.12
  59.8 27.5 %collective-permute-start.4 = (f32[256,256]{1,0:T(8,128)}, f32[256,256]{1,0:T(8,128)S(1)}, u32[]{:S(2)}, u32[]{:S(2)}) collective-permute-start(f32[256,256]{1,0:T(8,128)} %get-tuple-element.27), channel_id=1, source_target_pairs={{0,8},{8,0},{16,24},{24,16},{32,40},{40,32},{48,56},{56,48},{64,72... | collective-permute-start | bytes 786440 | tf_op jit(solution)/shard_map/ppermute | solution.py:239
  66.0 24.0 %collective-permute-start.5 = (f32[256,256]{1,0:T(8,128)S(1)}, f32[256,256]{1,0:T(8,128)S(1)}, u32[]{:S(2)}, u32[]{:S(2)}) collective-permute-start(f32[256,256]{1,0:T(8,128)S(1)} %get-tuple-element.28), channel_id=1, source_target_pairs={{0,16},{8,24},{16,0},{24,8},{32,48},{40,56},{48,32},{56,40},{64,80... | collective-permute-start | bytes 786440 | tf_op jit(solution)/shard_map/ppermute | solution.py:239
  67.9 22.1 %collective-permute-start.6 = (f32[256,256]{1,0:T(8,128)S(1)}, f32[256,256]{1,0:T(8,128)S(1)}, u32[]{:S(2)}, u32[]{:S(2)}) collective-permute-start(f32[256,256]{1,0:T(8,128)S(1)} %get-tuple-element.29), channel_id=1, source_target_pairs={{0,24},{8,16},{16,8},{24,0},{32,56},{40,48},{48,40},{56,32},{64,88... | collective-permute-start | bytes 786440 | tf_op jit(solution)/shard_map/ppermute | solution.py:239
  76.8 1.2 copy-start.11
  78.0 1.2 copy-start.13
  81.0 12.5 %collective-permute-start.1 = (f32[256,256]{1,0:T(8,128)S(1)}, f32[256,256]{1,0:T(8,128)S(1)}, u32[]{:S(2)}, u32[]{:S(2)}) collective-permute-start(f32[256,256]{1,0:T(8,128)S(1)} %get-tuple-element.23), channel_id=1, source_target_pairs={{0,8},{8,0},{16,24},{24,16},{32,40},{40,32},{48,56},{56,48},{64,72... | collective-permute-start | bytes 786440 | tf_op jit(solution)/shard_map/ppermute | solution.py:239
  84.6 9.8 %collective-permute-start.2 = (f32[256,256]{1,0:T(8,128)S(1)}, f32[256,256]{1,0:T(8,128)S(1)}, u32[]{:S(2)}, u32[]{:S(2)}) collective-permute-start(f32[256,256]{1,0:T(8,128)S(1)} %get-tuple-element.24), channel_id=1, source_target_pairs={{0,16},{8,24},{16,0},{24,8},{32,48},{40,56},{48,32},{56,40},{64,80... | collective-permute-start | bytes 786440 | tf_op jit(solution)/shard_map/ppermute | solution.py:239
  87.3 12.8 %collective-permute-start.3 = (f32[256,256]{1,0:T(8,128)S(1)}, f32[256,256]{1,0:T(8,128)S(1)}, u32[]{:S(2)}, u32[]{:S(2)}) collective-permute-start(f32[256,256]{1,0:T(8,128)S(1)} %get-tuple-element.25), channel_id=1, source_target_pairs={{0,24},{8,16},{16,8},{24,0},{32,56},{40,48},{48,40},{56,32},{64,88... | collective-permute-start | bytes 786440 | tf_op jit(solution)/shard_map/ppermute | solution.py:239
  90.1 2.2 %copy-start = (f32[4,2,128,1024]{3,2,1,0:T(8,128)S(1)}, f32[4,2,128,1024]{3,2,1,0:T(8,128)}, u32[]{:S(2)}) copy-start(f32[4,2,128,1024]{3,2,1,0:T(8,128)} %constant.37.clone.turn_ref) | copy-start | bytes 12582916
  92.3 7.8 %copy-start.1 = (f32[4,2,128,1024]{3,2,1,0:T(8,128)S(1)}, f32[4,2,128,1024]{3,2,1,0:T(8,128)}, u32[]{:S(2)}) copy-start(f32[4,2,128,1024]{3,2,1,0:T(8,128)} %constant.37.clone.turn_ref) | copy-start | bytes 12582916
  93.5 26.9 %copy-start.3 = (bf16[512,1024]{1,0:T(8,128)(2,1)S(1)}, bf16[512,1024]{1,0:T(8,128)(2,1)}, u32[]{:S(2)}) copy-start(bf16[512,1024]{1,0:T(8,128)(2,1)} %constant.36.clone.low_ref) | copy-start | bytes 3145732
  93.5 26.9 %copy-start.4 = (bf16[512,1024]{1,0:T(8,128)(2,1)S(1)}, bf16[512,1024]{1,0:T(8,128)(2,1)}, u32[]{:S(2)}) copy-start(bf16[512,1024]{1,0:T(8,128)(2,1)} %constant.35.clone.high_ref) | copy-start | bytes 3145732
  100.1 31.6 %copy-start.7 = (f32[128,1024]{1,0:T(8,128)S(1)}, f32[128,1024]{1,0:T(8,128)}, u32[]{:S(2)}) copy-start(f32[128,1024]{1,0:T(8,128)} %queries_ref.1) | copy-start | bytes 1572868
  102.6 7.9 %collective-permute-start.7 = (f32[256,256]{1,0:T(8,128)S(1)}, f32[256,256]{1,0:T(8,128)S(1)}, u32[]{:S(2)}, u32[]{:S(2)}) collective-permute-start(f32[256,256]{1,0:T(8,128)S(1)} %get-tuple-element.31), channel_id=1, source_target_pairs={{0,8},{8,0},{16,24},{24,16},{32,40},{40,32},{48,56},{56,48},{64,72... | collective-permute-start | bytes 786440 | tf_op jit(solution)/shard_map/ppermute | solution.py:239
  104.8 9.6 %collective-permute-start.8 = (f32[256,256]{1,0:T(8,128)S(1)}, f32[256,256]{1,0:T(8,128)S(1)}, u32[]{:S(2)}, u32[]{:S(2)}) collective-permute-start(f32[256,256]{1,0:T(8,128)S(1)} %get-tuple-element.32), channel_id=1, source_target_pairs={{0,16},{8,24},{16,0},{24,8},{32,48},{40,56},{48,32},{56,40},{64,80... | collective-permute-start | bytes 786440 | tf_op jit(solution)/shard_map/ppermute | solution.py:239
  107.6 12.8 %collective-permute-start.9 = (f32[256,256]{1,0:T(8,128)S(1)}, f32[256,256]{1,0:T(8,128)S(1)}, u32[]{:S(2)}, u32[]{:S(2)}) collective-permute-start(f32[256,256]{1,0:T(8,128)S(1)} %get-tuple-element.33), channel_id=1, source_target_pairs={{0,24},{8,16},{16,8},{24,0},{32,56},{40,48},{48,40},{56,32},{64,88... | collective-permute-start | bytes 786440 | tf_op jit(solution)/shard_map/ppermute | solution.py:239
  123.1 30.5 %all-to-all-start.2 = ((f32[512,2,128]{2,1,0:T(2,128)}), f32[512,2,128]{2,1,0:T(2,128)S(1)}, u32[]{:S(2)}, u32[]{:S(2)}) async-start(f32[512,2,128]{2,1,0:T(2,128)} %bitcast.7), calls=%async_computation.2 | async-start | bytes 1048576 | tf_op jit(solution)/shard_map/all_to_all | solution.py:290

commit v2 on v1

v2 whole, which is shorter than its diff:
```python
import functools

import jax
import jax.numpy as jnp
import numpy as np
from jax import lax
from jax.experimental import pallas as pl
from jax.experimental.pallas import tpu as pltpu
from jax.sharding import PartitionSpec as P


BF = jnp.bfloat16
F32 = jnp.float32
GROUP = 4
ROWS = 512
COLS = 1024
Q = 256
LANES = 128
TILES = 8
CHUNK = 16
TOTAL = ROWS * COLS
ROOT = float(np.sqrt(0.5))


def halves(values):
    high = np.asarray(values, np.float32).astype(jnp.bfloat16)
    low = (np.asarray(values, np.float64) - high.astype(np.float64)).astype(np.float32).astype(jnp.bfloat16)
    return high, low


@functools.lru_cache(maxsize=None)
def tables():
    i = np.arange(LANES, dtype=np.float64)
    grid = 2.0 * np.pi * np.outer(i, i) / LANES
    cos, sin = np.cos(grid), np.sin(grid)
    ahead = np.block([[cos, -sin], [sin, cos]])
    matrices = np.stack((*halves(ahead), *halves(ahead.T)))
    steps = np.zeros((2, 2 * TILES, LANES))
    for r in range(TILES):
        angle = 2.0 * np.pi * r * i / COLS
        for chip in range(2):
            sign = -1.0 if chip and r % 2 else 1.0
            steps[chip, 2 * r], steps[chip, 2 * r + 1] = sign * np.cos(angle), -sign * np.sin(angle)
    turns = np.zeros((2, 2, Q, LANES))
    columns = np.zeros((GROUP, Q, LANES))
    mixes = np.zeros((2, LANES, LANES))
    for member in range(GROUP):
        chip, core = divmod(member, 2)
        k1 = np.concatenate((4.0 * i + core, 4.0 * i + 2.0 + core)) + 0.25
        angle = 2.0 * np.pi * np.outer(k1, i) / TOTAL
        turns[core, 0], turns[core, 1] = np.cos(angle), -np.sin(angle)
        for s in range(TILES):
            angle = 2.0 * np.pi * s * LANES * k1 / TOTAL
            columns[member, :, 2 * s], columns[member, :, 2 * s + 1] = np.cos(angle), -np.sin(angle)
        columns[member, :, 16:24] = columns[member, :, 8 * chip : 8 * chip + 8]
        for a in range(4):
            for q in range(2):
                angle = 2.0 * np.pi * (a * LANES + i) * (2.0 * q + core + 0.25) / ROWS
                at = 4 * a + 2 * q
                mixes[core, :, at], mixes[core, :, at + 1] = np.cos(angle), -np.sin(angle)
                mixes[core, :, 16 + at], mixes[core, :, 17 + at] = np.cos(angle) / TOTAL, -np.sin(angle) / TOTAL
    pages = []
    for member in range(GROUP):
        chip, core = divmod(member, 2)
        pages.append(
            np.concatenate((columns[member], turns[core, 0], turns[core, 1], mixes[core], mixes[1 - core], steps[chip], steps[0]))
        )
    return matrices, np.stack(pages).astype(np.float32)


def split(x):
    high = x.astype(BF)
    return high, (x - high.astype(F32)).astype(BF)


def mm(a, b):
    return jnp.dot(a, b, preferred_element_type=F32)


def pack_filter_kernel(filter_rows, out_ref, held_ref, sem_ref):
    width = filter_rows.shape[1] // 4
    pieces = [filter_rows.at[:, pl.ds(n * width, width)] for n in range(4)]
    loads = Loads(sem_ref, [(piece, held_ref.at[n]) for n, piece in enumerate(pieces)])
    for n in range(4):
        loads.wait(n)
        for tile in range(width // LANES):
            out_ref[pl.ds(n * (width // LANES) + tile, 16, stride=64), :] = held_ref[n, :, tile * LANES : (tile + 1) * LANES]


def feature(signal, taps, older, newer):
    lane = lax.broadcasted_iota(jnp.int32, signal.shape, 1)
    one = jnp.where(lane == 0, newer, pltpu.roll(signal, 1, 1))
    two = jnp.where(lane == 0, older, jnp.where(lane == 1, newer, pltpu.roll(signal, 2, 1)))
    return taps[0] * signal + taps[1] * one + taps[2] * two


def drive_kernel(keys_ref, values_ref, small_ref, packed_ref, drive_ref, token_ref):
    token_ref[...] = small_ref[:8, :16]
    for chan in range(8):
        rows = slice(16 * chan, 16 * chan + 16)
        col = lambda n: small_ref[rows, n : n + 1]
        key = feature(keys_ref[rows, :], [col(3), col(4), col(5)], col(12), col(13))
        value = feature(values_ref[rows, :], [col(6), col(7), col(8)], col(14), col(15))
        drive = key * value
        drive_ref[rows, :] = drive
        for member in range(GROUP):
            for half in range(2):
                at = (2 * member + half) * LANES
                packed_ref[pl.ds(16 * member + 2 * chan + half, 16, stride=64), :] = drive[:, at : at + LANES]


def gate_kernel(queries_ref, drive_ref, small_ref, gain_ref, direct_ref):
    for chan in range(8):
        rows = slice(16 * chan, 16 * chan + 16)
        col = lambda n: small_ref[rows, n : n + 1]
        query = feature(queries_ref[rows, :], [col(0), col(1), col(2)], col(10), col(11))
        gain_ref[rows, :] = query
        direct_ref[rows, :] = query * (col(9) * drive_ref[rows, :])


def finish_kernel(rows_ref, gain_ref, direct_ref, out_ref):
    for chan in range(8):
        rows = slice(16 * chan, 16 * chan + 16)
        for core in range(2):
            for tile in range(4):
                at = (4 * core + tile) * LANES
                first = rows_ref[pl.ds(32 * core + 4 * chan + tile, 16, stride=128), :]
                second = rows_ref[pl.ds(32 * (2 + core) + 4 * chan + tile, 16, stride=128), :]
                out_ref[rows, at : at + LANES] = (
                    gain_ref[rows, at : at + LANES] * (first + second) + direct_ref[rows, at : at + LANES]
                )


def times(a, b, conjugate=False):
    (ar, ai), (br, bi) = a, b
    if conjugate:
        return ar * br + ai * bi, ai * br - ar * bi
    return ar * br - ai * bi, ar * bi + ai * br


def mixed(weights, values):
    (w0, w1, w2, w3), (v0, v1, v2, v3) = weights, values
    return (w0 * v0 + w1 * v1) + (w2 * v2 + w3 * v3)


def plus(a, b):
    return a[0] + b[0], a[1] + b[1]


def minus(a, b):
    return a[0] - b[0], a[1] - b[1]


def turned(a, sign):
    return (-a[1], a[0]) if sign > 0 else (a[1], -a[0])


def eighth(a, power, sign):
    if power >= 2:
        a = turned(a, sign)
    if power % 2:
        real, imag = a
        a = ((real - sign * imag) * ROOT, (imag + sign * real) * ROOT)
    return a


def four(parts, sign):
    e, f = plus(parts[0], parts[2]), minus(parts[0], parts[2])
    g, h = plus(parts[1], parts[3]), turned(minus(parts[1], parts[3]), sign)
    return [plus(e, g), plus(f, h), minus(e, g), minus(f, h)]


TURN, MIX, STEP, PAGE = Q, 3 * Q, 4 * Q, 4 * Q + 4 * TILES


def column(page_ref, rows, n):
    return page_ref[rows, n : n + 1], page_ref[rows, n + 1 : n + 2]


def turn(page_ref, rows):
    return tuple(page_ref[TURN + part * Q + rows.start : TURN + part * Q + rows.stop, :] for part in range(2))


def mixes(page_ref, other, rows, first):
    at = MIX + other * LANES
    return [page_ref[at + rows.start : at + rows.stop, n : n + 1] for n in range(first, first + 16)]


def step(page_ref, plain, r):
    at = STEP + plain * 2 * TILES + 2 * r
    return page_ref[at : at + 1, :], page_ref[at + 1 : at + 2, :]


class Loads:
    def __init__(self, sem_ref, pairs):
        self.copies = [pltpu.make_async_copy(src, dst, sem_ref.at[n]) for n, (src, dst) in enumerate(pairs)]
        for copy in self.copies:
            copy.start()

    def wait(self, *which):
        for n in which:
            self.copies[n].wait()


def matrix(ref, transposed, axis):
    high, low = ref[2 * transposed], ref[2 * transposed + 1]
    return jnp.concatenate((high, high, low), axis)


def left_product(matrix_ref, transposed, high, low):
    return mm(matrix(matrix_ref, transposed, 1), jnp.concatenate((high, low, high), 0))


def right_product(matrix_ref, transposed, high, low):
    return mm(jnp.concatenate((high, low, high), 1), matrix(matrix_ref, transposed, 0))


def outer_transform(x_ref, count, other, page_ref, matrix_ref, f_ref, high_ref, low_ref):
    for chunk in range(LANES // CHUNK):
        rows = slice(chunk * CHUNK, (chunk + 1) * CHUNK)
        mix = mixes(page_ref, other, rows, 0)
        for s in range(count):
            x = [x_ref[s, a * LANES + rows.start : a * LANES + rows.stop, :] for a in range(4)]
            for q in range(2):
                for part in range(2):
                    u = mixed([mix[4 * a + 2 * q + part] for a in range(4)], x)
                    at = slice(part * LANES + rows.start, part * LANES + rows.stop), slice(q * LANES, (q + 1) * LANES)
                    high_ref[s, *at], low_ref[s, *at] = split(u)
    for s in range(count):
        result = left_product(matrix_ref, 1, high_ref[s], low_ref[s])
        for part in range(2):
            for q in range(2):
                f_ref[s, part, q * LANES : (q + 1) * LANES, :] = result[
                    part * LANES : (part + 1) * LANES, q * LANES : (q + 1) * LANES
                ]


def inner_transform(f_ref, count, plain, first, page_ref, high_ref, low_ref):
    for chunk in range(Q // CHUNK):
        rows = slice(chunk * CHUNK, (chunk + 1) * CHUNK)
        angle = turn(page_ref, rows)
        parts = [
            times(times((f_ref[s, 0, rows, :], f_ref[s, 1, rows, :]), angle), column(page_ref, rows, first + 2 * s))
            for s in range(count)
        ]
        if count == TILES:
            even = [plus(parts[s], parts[s + 4]) for s in range(4)]
            odd = [minus(parts[s], parts[s + 4]) for s in range(4)]
        else:
            even = odd = parts
        even, odd = four(even, -1), four([eighth(odd[s], s, -1) for s in range(4)], -1)
        for r in range(TILES):
            value = (odd if r % 2 else even)[r // 2]
            if r:
                value = times(value, step(page_ref, plain, r))
            for part in range(2):
                at = rows, slice(part * LANES, (part + 1) * LANES)
                high_ref[r, *at], low_ref[r, *at] = split(value[part])


def filter_kernel(
    me_ref, pages, matrices, p0, p1, p2, p3, out_ref, token_ref, page_ref, matrix_ref, sem_ref, held_ref, x_ref, f_ref, high_ref, low_ref
):
    me = me_ref[0]
    pieces = [(piece, held_ref.at[mask]) for mask, piece in enumerate((p0, p1, p2, p3))]
    loads = Loads(sem_ref, [(pages.at[me], page_ref), (matrices, matrix_ref), *pieces])
    for mask in range(GROUP):
        loads.wait(2 + mask)
        at = (me ^ mask) * 8
        for a in range(16):
            for tile in range(TILES):
                rows = pl.ds(pl.multiple_of(a * 32 + at, 8), 8)
                x_ref[tile, rows, :] = held_ref[mask, pl.ds(a * 64 + tile, 8, stride=8), :]
    loads.wait(0, 1)
    token_ref[...] = page_ref[:8, :]
    outer_transform(x_ref, TILES, 0, page_ref, matrix_ref, f_ref, high_ref, low_ref)
    inner_transform(f_ref, TILES, 1, 0, page_ref, high_ref, low_ref)
    for r in range(TILES):
        out_ref[r] = right_product(matrix_ref, 0, high_ref[r], low_ref[r])


def drive_outer_kernel(
    me_ref, pages, matrices, own_ref, _, mine_ref, other_ref, page_ref, matrix_ref, sem_ref, x_ref, high_ref, low_ref
):
    loads = Loads(sem_ref, [(pages.at[me_ref[0]], page_ref), (matrices, matrix_ref)])
    for half in range(2):
        x_ref[half] = own_ref[pl.ds(half, ROWS, stride=2), :]
    loads.wait(0, 1)
    outer_transform(x_ref, 2, 1, page_ref, matrix_ref, other_ref, high_ref, low_ref)
    outer_transform(x_ref, 2, 0, page_ref, matrix_ref, mine_ref, high_ref, low_ref)


def product_kernel(
    me_ref,
    pages,
    matrices,
    own,
    peer,
    spectrum,
    mine_ref,
    other_ref,
    page_ref,
    matrix_ref,
    sem_ref,
    f_ref,
    filter_ref,
    d_ref,
    high_ref,
    low_ref,
):
    me = me_ref[0]
    core = me & 1
    pieces = [(own, f_ref.at[pl.ds(2 * core, 2)]), (peer, f_ref.at[pl.ds(2 * (1 - core), 2)])]
    loads = Loads(sem_ref, [(pages.at[me], page_ref), (matrices, matrix_ref), *pieces, (spectrum, filter_ref)])
    loads.wait(0, 2, 3)
    inner_transform(f_ref, 4, 0, 16, page_ref, high_ref, low_ref)
    loads.wait(1, 4)
    for r in range(TILES):
        x, h = right_product(matrix_ref, 0, high_ref[r], low_ref[r]), filter_ref[r]
        value = times((x[:, :LANES], x[:, LANES:]), (h[:, :LANES], h[:, LANES:]))
        d_ref[r] = right_product(matrix_ref, 1, *split(jnp.concatenate(value, 1)))
    for chunk in range(Q // CHUNK):
        rows = slice(chunk * CHUNK, (chunk + 1) * CHUNK)
        q, kappa = divmod(chunk * CHUNK, LANES)
        angle = turn(page_ref, rows)
        parts = []
        for r in range(TILES):
            value = d_ref[r, rows, :LANES], d_ref[r, rows, LANES:]
            if r:
                value = times(value, step(page_ref, 1, r), True)
            parts.append(value)
        even, odd = four(parts[0::2], 1), four(parts[1::2], 1)
        odd = [eighth(odd[s], s, 1) for s in range(4)]
        for s in range(TILES):
            value = (minus if s >= 4 else plus)(even[s % 4], odd[s % 4])
            value = times(times(value, angle, True), column(page_ref, rows, 2 * s), True)
            for part in range(2):
                at = slice(part * LANES + kappa, part * LANES + kappa + CHUNK), slice(q * LANES, (q + 1) * LANES)
                high_ref[s, *at], low_ref[s, *at] = split(value[part])
    for s in range(TILES):
        d_ref[s] = left_product(matrix_ref, 0, high_ref[s], low_ref[s])
    for chunk in range(LANES // CHUNK):
        rows = slice(chunk * CHUNK, (chunk + 1) * CHUNK)
        mix = mixes(page_ref, 0, rows, 16)
        for owner, out_ref in ((core, mine_ref), (1 - core, other_ref)):
            for t in range(4):
                s = 4 * owner + t
                v = [
                    d_ref[s, part * LANES + rows.start : part * LANES + rows.stop, q * LANES : (q + 1) * LANES]
                    for q in range(2)
                    for part in range(2)
                ]
                for a in range(4):
                    value = mixed(mix[4 * a : 4 * a + 4], v)
                    out_ref[pl.ds((a * LANES + rows.start) * 4 + t, CHUNK, stride=4), :] = value


VMEM_LIMIT = 32 * 1024 * 1024
VMEM_ALL = 60 * 1024 * 1024
FILTER_FLOPS = 3 * 2 * 256 * 256 * 256 * 16


def whole(s):
    return pl.BlockSpec(s.shape, lambda *_, n=len(s.shape): (0,) * n)


def call(kernel, out_shapes, args, in_specs=None, scratch=(), prefetch=0, flops=0, limit=VMEM_LIMIT):
    nbytes = sum(a.size * a.dtype.itemsize for a in args) + sum(int(np.prod(s.shape)) * 4 for s in out_shapes)
    single = len(out_shapes) == 1
    out_specs = [whole(s) for s in out_shapes]
    return pl.pallas_call(
        kernel,
        out_shape=out_shapes[0] if single else out_shapes,
        grid_spec=pltpu.PrefetchScalarGridSpec(
            num_scalar_prefetch=prefetch,
            grid=(1,),
            in_specs=in_specs or [whole(a) for a in args[prefetch:]],
            out_specs=out_specs[0] if single else out_specs,
            scratch_shapes=list(scratch),
        ),
        compiler_params=pltpu.CompilerParams(vmem_limit_bytes=limit),
        cost_estimate=pl.CostEstimate(flops=flops, bytes_accessed=nbytes, transcendentals=0),
    )(*args)


def shape(*dims):
    return jax.ShapeDtypeStruct(dims, F32)


HBM = pl.BlockSpec(memory_space=pltpu.HBM)


def transform(kernel, me, arrays, specs, outs, scratch, flops):
    matrices, pages = map(jnp.asarray, tables())
    fixed = [
        pltpu.VMEM((PAGE, LANES), F32),
        pltpu.VMEM(matrices.shape, BF),
        pltpu.SemaphoreType.DMA((2 + specs.count(HBM),)),
    ]
    count = 2 if kernel is drive_outer_kernel else TILES
    scratch = fixed + [pltpu.VMEM(s, F32) for s in scratch] + [pltpu.VMEM((count, Q, Q), BF)] * 2
    limit = VMEM_ALL if kernel is filter_kernel else VMEM_LIMIT
    return call(kernel, outs, (me, pages, matrices, *arrays), [HBM, HBM, *specs], scratch, 1, flops, limit)


def tie_kernel(rows_ref, _, out_ref):
    pass


def after(rows, other):
    return pl.pallas_call(
        tie_kernel,
        out_shape=shape(*rows.shape),
        grid=(1,),
        in_specs=[pl.BlockSpec(memory_space=pl.ANY), whole(other)],
        out_specs=pl.BlockSpec(memory_space=pl.ANY),
        input_output_aliases={0: 0},
        compiler_params=pltpu.CompilerParams(vmem_limit_bytes=VMEM_LIMIT),
    )(rows, other)


def across(rows, mask):
    size = lax.axis_size("seq")
    return lax.ppermute(rows, "seq", [(i, i ^ mask) for i in range(size)])


def local(queries, keys, values, short_taps, long_filter, skip_gain):
    everyone = ("seq", "chan")
    size = lax.axis_size(everyone)
    seq_size = lax.axis_size("seq")
    me = (lax.axis_index("seq") % GROUP).astype(jnp.int32).reshape(1)
    channels = queries.shape[0]

    held = [pltpu.VMEM((4, 16, 2 * COLS), F32), pltpu.SemaphoreType.DMA((4,))]
    filter_rows = call(pack_filter_kernel, [shape(2 * ROWS, LANES)], (long_filter,), [HBM], held, limit=VMEM_ALL)
    alike = [list(range(member, seq_size, GROUP)) for member in range(GROUP)]
    filter_rows = lax.all_to_all(
        filter_rows.reshape(16, 64, LANES), "seq", 0, 0, tiled=True, axis_index_groups=alike
    ).reshape(2 * ROWS, LANES)

    edges = jnp.stack((queries[:, -2], queries[:, -1], keys[:, -2], keys[:, -1], values[:, -2], values[:, -1]))
    before = lax.ppermute(edges, everyone, [(i, i + 1) for i in range(size - 1)])
    small = jnp.concatenate((short_taps.reshape(9, channels), skip_gain[None], before)).T
    outs = [shape(2 * ROWS, LANES), shape(channels, COLS), shape(8, 16)]
    packed, drive, token = call(drive_kernel, outs, (keys, values, small))
    filter_rows = after(filter_rows, token)
    filter_far = across(filter_rows, 2)
    own = lax.all_to_all(packed.reshape(size, -1, LANES), everyone, 0, 0, tiled=True).reshape(2 * ROWS, LANES)

    flops = 3 * 2 * 256 * 256 * 256 * 8
    pieces = (filter_rows, across(filter_rows, 1), filter_far, across(filter_far, 1))
    filter_spectrum, token = transform(
        filter_kernel,
        me,
        pieces,
        [HBM] * GROUP,
        [shape(TILES, Q, Q), shape(8, LANES)],
        [(GROUP, 2 * ROWS, LANES), (TILES, ROWS, LANES), (TILES, 2, Q, LANES)],
        FILTER_FLOPS,
    )
    mine, other = transform(
        drive_outer_kernel,
        me,
        (own, token),
        [whole(own), whole(token)],
        [shape(2, 2, Q, LANES)] * 2,
        [(2, ROWS, LANES)],
        flops,
    )
    mine, other = transform(
        product_kernel,
        me,
        (mine, across(other, 1), filter_spectrum),
        [HBM] * 3,
        [shape(4 * ROWS, LANES)] * 2,
        [(4, 2, Q, LANES), (TILES, Q, Q), (TILES, Q, Q)],
        3 * flops,
    )
    result = mine + across(other, 1)
    gain, direct = call(gate_kernel, [shape(channels, COLS)] * 2, (queries, drive, small))
    returned = lax.all_to_all(result.reshape(size, -1, LANES), everyone, 0, 0, tiled=True).reshape(4 * ROWS, LANES)
    return call(finish_kernel, [shape(channels, COLS)], (returned, gain, direct))


def solution(mesh):
    spread = P(None, ("seq", "chan"))
    in_specs = (spread, spread, spread, P(), P("chan", "seq"), P())
    return jax.shard_map(local, mesh=mesh, in_specs=in_specs, out_specs=spread, check_vma=False)
```

time: 156 us -> 142 us (0.910)
  starting transfers between devices: 74.1 us -> 58.8 us
  local copies, waits for them, and re-layouts: 14.4 us -> 5.99 us
  Pallas kernels: 15.5 us -> 21.2 us
  waiting for transfers between devices: 49.8 us -> 54.4 us
    all_to_all x3, waiting for transfers between devices: 28 us -> 40.6 us  [the longest x1 32.5 us: local(): lax.all_to_all(result.reshape(size, -1, LANES), everyone, 0, 0, tiled=True)]
    ppermute x9 -> x5, starting transfers between devices: 28.5 us -> 16.8 us  [across(): return lax.ppermute(rows, 'seq', [(i, i ^ mask) for i in range(size)])]
    ppermute x9 -> x5, waiting for transfers between devices: 16.4 us -> 5.45 us  [across(): return lax.ppermute(rows, 'seq', [(i, i ^ mask) for i in range(size)])]
    unnamed x28 -> x32, local copies, waits for them, and re-layouts: 10.2 us -> 4.4 us
    pallas_call x9 -> x7, Pallas kernels: 15.5 us -> 21.2 us  [call(): pl.pallas_call(kernel, out_shape=out_shapes[0] if single else out_shapes,...]
    all_to_all x3, starting transfers between devices: 42.4 us -> 38.9 us  [the longest x1 16.2 us: local(): lax.all_to_all(filter_rows.reshape(16, 64, LANES), 'seq', 0, 0, tiled=Tru...]
    ppermute x1, waiting for transfers between devices: 5.32 us -> 8.32 us  [local(): lax.ppermute(edges, everyone, [(i, i + 1) for i in range(size - 1)])]
  transfers between devices with their start and end apart: 13 -> 9, of which waited for: 8 -> 7; matrix products, arithmetic and copies ran while one was open for 3% -> 1% of each run, Pallas kernels for 5% -> 7%
where the time goes in v2:
time: 142 us
  starting transfers between devices  58.8 us (41%)
  waiting for transfers between devices  54.4 us (38%)
  Pallas kernels  21.2 us (15%)
  local copies, waits for them, and re-layouts  5.99 us (4%)
    all_to_all x1, waiting for transfers between devices, local(): lax.all_to_all(result.reshape(size, -1, LANES), everyone, 0, 0, tiled=True)  32.5 us
    pallas_call x7, Pallas kernels, call(): pl.pallas_call(kernel, out_shape=out_shapes[0] if single else out_shapes,...  21.2 us
    ppermute x5, starting transfers between devices, across(): return lax.ppermute(rows, 'seq', [(i, i ^ mask) for i in range(size)])  16.8 us
    all_to_all x1, starting transfers between devices, local(): lax.all_to_all(filter_rows.reshape(16, 64, LANES), 'seq', 0, 0, tiled=Tru...  16.2 us
    all_to_all x1, starting transfers between devices, local(): lax.all_to_all(packed.reshape(size, -1, LANES), everyone, 0, 0, tiled=True)  12.4 us
    all_to_all x1, starting transfers between devices, local(): lax.all_to_all(result.reshape(size, -1, LANES), everyone, 0, 0, tiled=True)  10.3 us
    ppermute x1, waiting for transfers between devices, local(): lax.ppermute(edges, everyone, [(i, i + 1) for i in range(size - 1)])  8.32 us
    ppermute x5, waiting for transfers between devices, across(): return lax.ppermute(rows, 'seq', [(i, i ^ mask) for i in range(size)])  5.45 us
  transfers between devices with their start and end apart: 9, of which 7 were waited for; matrix products, arithmetic and copies ran while one was open for 1% of the time, Pallas kernels for 7%

profile of v2, /device:TPU:1, one launch (start us, length us, event | category | flops | bytes accessed | tf_op | source)
XLA Modules:
  0.0 141.8 jit_solution(15027275935333177754)
XLA Ops:
  0.0 2.3 %shard_map.83 = f32[1024,128]{1,0:T(8,128)} custom-call(f32[16,8192]{1,0:T(8,128)} %filter_rows.1), custom_call_target="tpu_custom_call" | custom-call | bytes 1048576 | tf_op jit(solution)/shard_map/pallas_call | solution.py:371
  2.3 16.2 %all-to-all-start.1 = ((f32[16,64,128]{2,1,0:T(8,128)}), f32[16,64,128]{2,1,0:T(8,128)S(1)}, u32[]{:S(2)}, u32[]{:S(2)}) async-start(f32[16,64,128]{2,1,0:T(8,128)} %bitcast.20), calls=%async_computation.1 | async-start | bytes 1048576 | tf_op jit(solution)/shard_map/all_to_all | solution.py:437
  18.5 1.1 slice_reduce_fusion.4
  19.7 0.2 slice_reduce_fusion.2
  19.8 0.2 slice_reduce_fusion
  20.1 3.1 %collective-permute-start = (f32[6,128]{1,0:T(8,128)S(1)}, f32[6,128]{1,0:T(8,128)S(1)}, u32[]{:S(2)}, u32[]{:S(2)}) collective-permute-start(f32[6,128]{1,0:T(8,128)S(1)} %stack.3), channel_id=1, source_target_pairs={{0,1},{1,2},{2,3},{3,4},{4,5},{5,6},{6,7},{7,8},{8,9},{9,10},{10,1... | collective-permute-start | bytes 9224 | tf_op jit(solution)/shard_map/ppermute | solution.py:442
  23.2 8.3 %collective-permute-done = f32[6,128]{1,0:T(8,128)S(1)} collective-permute-done((f32[6,128]{1,0:T(8,128)S(1)}, f32[6,128]{1,0:T(8,128)S(1)}, u32[]{:S(2)}, u32[]{:S(2)}) %collective-permute-start) | collective-permute-done | bytes 3104 | tf_op jit(solution)/shard_map/ppermute | solution.py:442
  31.6 2.0 %shard_map.82 = (f32[1024,128]{1,0:T(8,128)}, f32[128,1024]{1,0:T(8,128)S(1)}, f32[8,16]{1,0:T(8,128)S(1)}) custom-call(f32[128,1024]{1,0:T(8,128)S(1)} %copy-done.2, f32[128,1024]{1,0:T(8,128)S(1)} %copy-done.3, f32[128,16]{1,0:T(8,128)S(1)} %bitcast.18), custom_call_target="tpu_custom_call" | custom-call | bytes 2105856 | tf_op jit(solution)/shard_map/pallas_call | solution.py:371
  33.7 0.8 copy-done.5
  34.5 4.5 %all-to-all-done.1 = f32[16,64,128]{2,1,0:T(8,128)S(1)} async-done(((f32[16,64,128]{2,1,0:T(8,128)}), f32[16,64,128]{2,1,0:T(8,128)S(1)}, u32[]{:S(2)}, u32[]{:S(2)}) %all-to-all-start.1) | async-done | bytes 524320 | tf_op jit(solution)/shard_map/all_to_all | solution.py:437
  39.0 2.6 %collective-permute-start.2 = (f32[1024,128]{1,0:T(8,128)S(1)}, f32[1024,128]{1,0:T(8,128)S(1)}, u32[]{:S(2)}, u32[]{:S(2)}) collective-permute-start(f32[1024,128]{1,0:T(8,128)S(1)} %shard_map.84.p0), channel_id=1, source_target_pairs={{0,16},{8,24},{16,0},{24,8},{32,48},{40,56},{48,32},{56,40},{64,80... | collective-permute-start | bytes 1572872 | tf_op jit(solution)/shard_map/ppermute | solution.py:424
  41.6 12.4 %all-to-all-start = ((f32[512,2,128]{2,1,0:T(2,128)}), f32[512,2,128]{2,1,0:T(2,128)S(1)}, u32[]{:S(2)}, u32[]{:S(2)}) async-start(f32[512,2,128]{2,1,0:T(2,128)} %bitcast.3), calls=%async_computation | async-start | bytes 1048576 | tf_op jit(solution)/shard_map/all_to_all | solution.py:448
  54.0 6.2 %collective-permute-start.1 = (f32[1024,128]{1,0:T(8,128)S(1)}, f32[1024,128]{1,0:T(8,128)S(1)}, u32[]{:S(2)}, u32[]{:S(2)}) collective-permute-start(f32[1024,128]{1,0:T(8,128)S(1)} %shard_map.84.p0), channel_id=1, source_target_pairs={{0,8},{8,0},{16,24},{24,16},{32,40},{40,32},{48,56},{56,48},{64,72... | collective-permute-start | bytes 1572872 | tf_op jit(solution)/shard_map/ppermute | solution.py:424
  60.2 1.9 %collective-permute-start.3 = (f32[1024,128]{1,0:T(8,128)S(1)}, f32[1024,128]{1,0:T(8,128)S(1)}, u32[]{:S(2)}, u32[]{:S(2)}) collective-permute-start(f32[1024,128]{1,0:T(8,128)S(1)} %collective-permute-done.2.p2), channel_id=1, source_target_pairs={{0,8},{8,0},{16,24},{24,16},{32,40},{40,32},{48,56},{56,48},{64,72... | collective-permute-start | bytes 1572872 | tf_op jit(solution)/shard_map/ppermute | solution.py:424
  62.2 1.8 %collective-permute-done.3.p3 = f32[1024,128]{1,0:T(8,128)S(1)} collective-permute-done((f32[1024,128]{1,0:T(8,128)S(1)}, f32[1024,128]{1,0:T(8,128)S(1)}, u32[]{:S(2)}, u32[]{:S(2)}) %collective-permute-start.3) | collective-permute-done | bytes 524320 | tf_op jit(solution)/shard_map/ppermute | solution.py:424
  64.0 0.8 copy-done.15
  64.9 7.4 %shard_map.85 = (f32[8,256,256]{2,1,0:T(8,128)}, f32[8,128]{1,0:T(8,128)}) custom-call(s32[1]{0:T(128)} %bitcast.me_ref, f32[4,1056,128]{2,1,0:T(8,128)} %constant.24.clone.pages, bf16[4,256,256]{2,1,0:T(8,128)(2,1)} %constant.23.clone.matrices, f32[1024,128]{1,0:T(8,128)} %copy-done.1, f32[1024,128]{1,0:T(8,128)} %copy-done.14, f32[1024,128]{1,0:T(8,128)} %copy-done.13, ...), custom_call_target="tpu_custom_call" | custom-call | flops 1610612736 | bytes 6885380 | tf_op jit(solution)/shard_map/pallas_call | solution.py:371
  72.2 3.6 %all-to-all-done = f32[512,2,128]{2,1,0:T(2,128)S(1)} async-done(((f32[512,2,128]{2,1,0:T(2,128)}), f32[512,2,128]{2,1,0:T(2,128)S(1)}, u32[]{:S(2)}, u32[]{:S(2)}) %all-to-all-start) | async-done | bytes 524320 | tf_op jit(solution)/shard_map/all_to_all | solution.py:448
  75.9 1.0 copy-done.7
  76.9 0.7 copy-done.9
  77.6 1.5 %shard_map.86 = (f32[2,2,256,128]{3,2,1,0:T(8,128)S(1)}, f32[2,2,256,128]{3,2,1,0:T(8,128)S(1)}) custom-call(s32[1]{0:T(128)} %bitcast.me_ref, f32[4,1056,128]{2,1,0:T(8,128)S(1)} %copy-done, bf16[4,256,256]{2,1,0:T(8,128)(2,1)S(1)} %copy-done.7, f32[1024,128]{1,0:T(8,128)S(1)} %bitcast.17, f32[8,128]{1,0:T(8,128)S(1)} %copy-done.9), custom_call_target="tpu_custom_call" | custom-call | flops 805306368 | bytes 4263940 | tf_op jit(solution)/shard_map/pallas_call | solution.py:371
  79.1 3.7 %collective-permute-start.4 = (f32[2,2,256,128]{3,2,1,0:T(8,128)S(1)}, f32[2,2,256,128]{3,2,1,0:T(8,128)S(1)}, u32[]{:S(2)}, u32[]{:S(2)}) collective-permute-start(f32[2,2,256,128]{3,2,1,0:T(8,128)S(1)} %get-tuple-element.20), channel_id=1, source_target_pairs={{0,8},{8,0},{16,24},{24,16},{32,40},{40,32},{48,56},{56,48},{64,72... | collective-permute-start | bytes 1572872 | tf_op jit(solution)/shard_map/ppermute | solution.py:424
  82.8 1.3 collective-permute-done.4.peer
  84.2 1.0 copy-done.8
  85.2 6.1 %shard_map.87 = (f32[2048,128]{1,0:T(8,128)S(1)}, f32[2048,128]{1,0:T(8,128)S(1)}) custom-call(s32[1]{0:T(128)} %bitcast.me_ref, f32[4,1056,128]{2,1,0:T(8,128)S(1)} %copy-done, bf16[4,256,256]{2,1,0:T(8,128)(2,1)S(1)} %copy-done.8, f32[2,2,256,128]{3,2,1,0:T(8,128)S(1)} %get-tuple-element.19.own, f32[2,2,256,128]{3,2,1,0:T(8,128)S(1)} %collective-permute-done.4.peer, ...), custom_call_target="tpu_custom_call" | custom-call | flops 2415919104 | bytes 7929860 | tf_op jit(solution)/shard_map/pallas_call | solution.py:371
  91.3 2.3 %collective-permute-start.5 = (f32[2048,128]{1,0:T(8,128)S(1)}, f32[2048,128]{1,0:T(8,128)S(1)}, u32[]{:S(2)}, u32[]{:S(2)}) collective-permute-start(f32[2048,128]{1,0:T(8,128)S(1)} %get-tuple-element.23), channel_id=1, source_target_pairs={{0,8},{8,0},{16,24},{24,16},{32,40},{40,32},{48,56},{56,48},{64,72... | collective-permute-start | bytes 3145736 | tf_op jit(solution)/shard_map/ppermute | solution.py:424
  93.6 2.3 %collective-permute-done.5 = f32[2048,128]{1,0:T(8,128)S(1)} collective-permute-done((f32[2048,128]{1,0:T(8,128)S(1)}, f32[2048,128]{1,0:T(8,128)S(1)}, u32[]{:S(2)}, u32[]{:S(2)}) %collective-permute-start.5) | collective-permute-done | bytes 1048608 | tf_op jit(solution)/shard_map/ppermute | solution.py:424
  95.9 1.1 add.8
  97.0 10.3 %all-to-all-start.2 = ((f32[512,4,128]{2,1,0:T(4,128)}), f32[512,4,128]{2,1,0:T(4,128)S(1)}, u32[]{:S(2)}, u32[]{:S(2)}) async-start(f32[512,4,128]{2,1,0:T(4,128)} %bitcast.7), calls=%async_computation.2 | async-start | bytes 2097152 | tf_op jit(solution)/shard_map/all_to_all | solution.py:481
  107.3 0.5 shard_map.88
  107.9 32.5 %all-to-all-done.2 = f32[512,4,128]{2,1,0:T(4,128)S(1)} async-done(((f32[512,4,128]{2,1,0:T(4,128)}), f32[512,4,128]{2,1,0:T(4,128)S(1)}, u32[]{:S(2)}, u32[]{:S(2)}) %all-to-all-start.2) | async-done | bytes 1048608 | tf_op jit(solution)/shard_map/all_to_all | solution.py:481
  140.4 1.4 shard_map.89
  (34 shorter events, 0.2 us)
Async XLA Ops:
  0.0 19.6 %copy-start.2 = (f32[128,1024]{1,0:T(8,128)S(1)}, f32[128,1024]{1,0:T(8,128)}, u32[]{:S(2)}) copy-start(f32[128,1024]{1,0:T(8,128)} %keys_ref.1) | copy-start | bytes 1572868
  0.0 19.8 %copy-start.3 = (f32[128,1024]{1,0:T(8,128)S(1)}, f32[128,1024]{1,0:T(8,128)}, u32[]{:S(2)}) copy-start(f32[128,1024]{1,0:T(8,128)} %values_ref.1) | copy-start | bytes 1572868
  0.0 23.2 %copy-start.11 = (f32[3,3,128]{2,1,0:T(4,128)S(1)}, f32[3,3,128]{2,1,0:T(4,128)}, u32[]{:S(2)}) copy-start(f32[3,3,128]{2,1,0:T(4,128)} %param.11) | copy-start | bytes 13828
  0.0 31.5 %copy-start.12 = (f32[128]{0:T(128)S(1)}, f32[128]{0:T(128)}, u32[]{:S(2)}) copy-start(f32[128]{0:T(128)} %param.13) | copy-start | bytes 1540
  2.3 36.7 %all-to-all-start.1 = ((f32[16,64,128]{2,1,0:T(8,128)}), f32[16,64,128]{2,1,0:T(8,128)S(1)}, u32[]{:S(2)}, u32[]{:S(2)}) async-start(f32[16,64,128]{2,1,0:T(8,128)} %bitcast.20), calls=%async_computation.1 | async-start | bytes 1048576 | tf_op jit(solution)/shard_map/all_to_all | solution.py:437
  20.1 11.5 %collective-permute-start = (f32[6,128]{1,0:T(8,128)S(1)}, f32[6,128]{1,0:T(8,128)S(1)}, u32[]{:S(2)}, u32[]{:S(2)}) collective-permute-start(f32[6,128]{1,0:T(8,128)S(1)} %stack.3), channel_id=1, source_target_pairs={{0,1},{1,2},{2,3},{3,4},{4,5},{5,6},{6,7},{7,8},{8,9},{9,10},{10,1... | collective-permute-start | bytes 9224 | tf_op jit(solution)/shard_map/ppermute | solution.py:442
  33.7 0.8 copy-start.5
  39.0 25.9 %copy-start.1 = (f32[1024,128]{1,0:T(8,128)}, f32[1024,128]{1,0:T(8,128)S(1)}, u32[]{:S(2)}) copy-start(f32[1024,128]{1,0:T(8,128)S(1)} %shard_map.84.p0) | copy-start | bytes 1572868
  39.0 21.3 %collective-permute-start.2 = (f32[1024,128]{1,0:T(8,128)S(1)}, f32[1024,128]{1,0:T(8,128)S(1)}, u32[]{:S(2)}, u32[]{:S(2)}) collective-permute-start(f32[1024,128]{1,0:T(8,128)S(1)} %shard_map.84.p0), channel_id=1, source_target_pairs={{0,16},{8,24},{16,0},{24,8},{32,48},{40,56},{48,32},{56,40},{64,80... | collective-permute-start | bytes 1572872 | tf_op jit(solution)/shard_map/ppermute | solution.py:424
  41.6 34.3 %all-to-all-start = ((f32[512,2,128]{2,1,0:T(2,128)}), f32[512,2,128]{2,1,0:T(2,128)S(1)}, u32[]{:S(2)}, u32[]{:S(2)}) async-start(f32[512,2,128]{2,1,0:T(2,128)} %bitcast.3), calls=%async_computation | async-start | bytes 1048576 | tf_op jit(solution)/shard_map/all_to_all | solution.py:448
  54.0 8.2 %collective-permute-start.1 = (f32[1024,128]{1,0:T(8,128)S(1)}, f32[1024,128]{1,0:T(8,128)S(1)}, u32[]{:S(2)}, u32[]{:S(2)}) collective-permute-start(f32[1024,128]{1,0:T(8,128)S(1)} %shard_map.84.p0), channel_id=1, source_target_pairs={{0,8},{8,0},{16,24},{24,16},{32,40},{40,32},{48,56},{56,48},{64,72... | collective-permute-start | bytes 1572872 | tf_op jit(solution)/shard_map/ppermute | solution.py:424
  60.2 3.8 %copy-start.13 = (f32[1024,128]{1,0:T(8,128)}, f32[1024,128]{1,0:T(8,128)S(1)}, u32[]{:S(2)}) copy-start(f32[1024,128]{1,0:T(8,128)S(1)} %collective-permute-done.2.p2) | copy-start | bytes 1572868
  60.2 3.8 %collective-permute-start.3 = (f32[1024,128]{1,0:T(8,128)S(1)}, f32[1024,128]{1,0:T(8,128)S(1)}, u32[]{:S(2)}, u32[]{:S(2)}) collective-permute-start(f32[1024,128]{1,0:T(8,128)S(1)} %collective-permute-done.2.p2), channel_id=1, source_target_pairs={{0,8},{8,0},{16,24},{24,16},{32,40},{40,32},{48,56},{56,48},{64,72... | collective-permute-start | bytes 1572872 | tf_op jit(solution)/shard_map/ppermute | solution.py:424
  62.2 1.9 %copy-start.14 = (f32[1024,128]{1,0:T(8,128)}, f32[1024,128]{1,0:T(8,128)S(1)}, u32[]{:S(2)}) copy-start(f32[1024,128]{1,0:T(8,128)S(1)} %collective-permute-done.1.p1) | copy-start | bytes 1572868
  64.0 0.8 copy-start.15
  64.9 11.0 %copy-start = (f32[4,1056,128]{2,1,0:T(8,128)S(1)}, f32[4,1056,128]{2,1,0:T(8,128)}, u32[]{:S(2)}) copy-start(f32[4,1056,128]{2,1,0:T(8,128)} %constant.24.clone.pages) | copy-start | bytes 6488068
  75.9 1.0 copy-start.7
  76.9 0.7 copy-start.9
  77.6 6.6 %copy-start.10 = (f32[8,256,256]{2,1,0:T(8,128)S(1)}, f32[8,256,256]{2,1,0:T(8,128)}, u32[]{:S(2)}) copy-start(f32[8,256,256]{2,1,0:T(8,128)} %get-tuple-element.21.spectrum) | copy-start | bytes 6291460
  79.1 5.1 %collective-permute-start.4 = (f32[2,2,256,128]{3,2,1,0:T(8,128)S(1)}, f32[2,2,256,128]{3,2,1,0:T(8,128)S(1)}, u32[]{:S(2)}, u32[]{:S(2)}) collective-permute-start(f32[2,2,256,128]{3,2,1,0:T(8,128)S(1)} %get-tuple-element.20), channel_id=1, source_target_pairs={{0,8},{8,0},{16,24},{24,16},{32,40},{40,32},{48,56},{56,48},{64,72... | collective-permute-start | bytes 1572872 | tf_op jit(solution)/shard_map/ppermute | solution.py:424
  84.2 1.0 copy-start.8
  91.3 4.6 %collective-permute-start.5 = (f32[2048,128]{1,0:T(8,128)S(1)}, f32[2048,128]{1,0:T(8,128)S(1)}, u32[]{:S(2)}, u32[]{:S(2)}) collective-permute-start(f32[2048,128]{1,0:T(8,128)S(1)} %get-tuple-element.23), channel_id=1, source_target_pairs={{0,8},{8,0},{16,24},{24,16},{32,40},{40,32},{48,56},{56,48},{64,72... | collective-permute-start | bytes 3145736 | tf_op jit(solution)/shard_map/ppermute | solution.py:424
  95.9 11.4 %copy-start.4 = (f32[128,1024]{1,0:T(8,128)S(1)}, f32[128,1024]{1,0:T(8,128)}, u32[]{:S(2)}) copy-start(f32[128,1024]{1,0:T(8,128)} %queries_ref.1) | copy-start | bytes 1572868
  95.9 11.4 %copy-start.6 = (f32[128,1024]{1,0:T(8,128)S(1)}, f32[128,1024]{1,0:T(8,128)}, u32[]{:S(2)}) copy-start(f32[128,1024]{1,0:T(8,128)} %copy-done.5) | copy-start | bytes 1572868
  97.0 43.4 %all-to-all-start.2 = ((f32[512,4,128]{2,1,0:T(4,128)}), f32[512,4,128]{2,1,0:T(4,128)S(1)}, u32[]{:S(2)}, u32[]{:S(2)}) async-start(f32[512,4,128]{2,1,0:T(4,128)} %bitcast.7), calls=%async_computation.2 | async-start | bytes 2097152 | tf_op jit(solution)/shard_map/all_to_all | solution.py:481

commit v3 on v2

--- a/solution.py
+++ b/solution.py
@@ -181,8 +181,8 @@
     return tuple(page_ref[TURN + part * Q + rows.start : TURN + part * Q + rows.stop, :] for part in range(2))
 
 
-def mixes(page_ref, other, rows, first):
-    at = MIX + other * LANES
+def mixes(page_ref, other, rows, first, base=MIX):
+    at = base + other * LANES
     return [page_ref[at + rows.start : at + rows.stop, n : n + 1] for n in range(first, first + 16)]
 
 
@@ -215,10 +215,10 @@
     return mm(jnp.concatenate((high, low, high), 1), matrix(matrix_ref, transposed, 0))
 
 
-def outer_transform(x_ref, count, other, page_ref, matrix_ref, f_ref, high_ref, low_ref):
+def outer_transform(x_ref, count, other, page_ref, base, matrix_ref, transposed, f_ref, high_ref, low_ref):
     for chunk in range(LANES // CHUNK):
         rows = slice(chunk * CHUNK, (chunk + 1) * CHUNK)
-        mix = mixes(page_ref, other, rows, 0)
+        mix = mixes(page_ref, other, rows, 0, base)
         for s in range(count):
             x = [x_ref[s, a * LANES + rows.start : a * LANES + rows.stop, :] for a in range(4)]
             for q in range(2):
@@ -227,7 +227,7 @@
                     at = slice(part * LANES + rows.start, part * LANES + rows.stop), slice(q * LANES, (q + 1) * LANES)
                     high_ref[s, *at], low_ref[s, *at] = split(u)
     for s in range(count):
-        result = left_product(matrix_ref, 1, high_ref[s], low_ref[s])
+        result = left_product(matrix_ref, transposed, high_ref[s], low_ref[s])
         for part in range(2):
             for q in range(2):
                 f_ref[s, part, q * LANES : (q + 1) * LANES, :] = result[
@@ -259,7 +259,7 @@
 
 
 def filter_kernel(
-    me_ref, pages, matrices, p0, p1, p2, p3, out_ref, token_ref, page_ref, matrix_ref, sem_ref, held_ref, x_ref, f_ref, high_ref, low_ref
+    me_ref, pages, matrices, p0, p1, p2, p3, out_ref, page_ref, matrix_ref, sem_ref, held_ref, x_ref, f_ref, high_ref, low_ref
 ):
     me = me_ref[0]
     pieces = [(piece, held_ref.at[mask]) for mask, piece in enumerate((p0, p1, p2, p3))]
@@ -272,49 +272,49 @@
                 rows = pl.ds(pl.multiple_of(a * 32 + at, 8), 8)
                 x_ref[tile, rows, :] = held_ref[mask, pl.ds(a * 64 + tile, 8, stride=8), :]
     loads.wait(0, 1)
-    token_ref[...] = page_ref[:8, :]
-    outer_transform(x_ref, TILES, 0, page_ref, matrix_ref, f_ref, high_ref, low_ref)
+    outer_transform(x_ref, TILES, 0, page_ref, MIX, matrix_ref, 1, f_ref, high_ref, low_ref)
     inner_transform(f_ref, TILES, 1, 0, page_ref, high_ref, low_ref)
     for r in range(TILES):
         out_ref[r] = right_product(matrix_ref, 0, high_ref[r], low_ref[r])
 
 
 def drive_outer_kernel(
-    me_ref, pages, matrices, own_ref, _, mine_ref, other_ref, page_ref, matrix_ref, sem_ref, x_ref, high_ref, low_ref
-):
-    loads = Loads(sem_ref, [(pages.at[me_ref[0]], page_ref), (matrices, matrix_ref)])
-    for half in range(2):
-        x_ref[half] = own_ref[pl.ds(half, ROWS, stride=2), :]
-    loads.wait(0, 1)
-    outer_transform(x_ref, 2, 1, page_ref, matrix_ref, other_ref, high_ref, low_ref)
-    outer_transform(x_ref, 2, 0, page_ref, matrix_ref, mine_ref, high_ref, low_ref)
-
-
-def product_kernel(
     me_ref,
     pages,
     matrices,
-    own,
-    peer,
+    own_ref,
     spectrum,
     mine_ref,
     other_ref,
     page_ref,
     matrix_ref,
+    filter_ref,
+    mix_ref,
+    ahead_ref,
     sem_ref,
-    f_ref,
-    filter_ref,
-    d_ref,
+    x_ref,
     high_ref,
     low_ref,
 ):
-    me = me_ref[0]
-    core = me & 1
-    pieces = [(own, f_ref.at[pl.ds(2 * core, 2)]), (peer, f_ref.at[pl.ds(2 * (1 - core), 2)])]
-    loads = Loads(sem_ref, [(pages.at[me], page_ref), (matrices, matrix_ref), *pieces, (spectrum, filter_ref)])
-    loads.wait(0, 2, 3)
+    page = pages.at[me_ref[0]]
+    first = [(page.at[pl.ds(MIX, 2 * LANES)], mix_ref), (matrices.at[pl.ds(2, 2)], ahead_ref)]
+    loads = Loads(sem_ref, [*first, (page, page_ref), (matrices, matrix_ref), (spectrum, filter_ref)])
+    for half in range(2):
+        x_ref[half] = own_ref[pl.ds(half, ROWS, stride=2), :]
+    loads.wait(0, 1)
+    outer_transform(x_ref, 2, 1, mix_ref, 0, ahead_ref, 0, other_ref, high_ref, low_ref)
+    outer_transform(x_ref, 2, 0, mix_ref, 0, ahead_ref, 0, mine_ref, high_ref, low_ref)
+    loads.wait(2, 3, 4)
+
+
+def product_kernel(
+    me_ref, own_ref, peer_ref, page_ref, matrix_ref, filter_ref, mine_ref, other_ref, f_ref, d_ref, high_ref, low_ref
+):
+    core = me_ref[0] & 1
+    for which, piece_ref in ((core, own_ref), (1 - core, peer_ref)):
+        for half in range(2):
+            f_ref[2 * which + half] = piece_ref[half]
     inner_transform(f_ref, 4, 0, 16, page_ref, high_ref, low_ref)
-    loads.wait(1, 4)
     for r in range(TILES):
         x, h = right_product(matrix_ref, 0, high_ref[r], low_ref[r]), filter_ref[r]
         value = times((x[:, :LANES], x[:, LANES:]), (h[:, :LANES], h[:, LANES:]))
@@ -390,17 +390,12 @@
 HBM = pl.BlockSpec(memory_space=pltpu.HBM)
 
 
-def transform(kernel, me, arrays, specs, outs, scratch, flops):
-    matrices, pages = map(jnp.asarray, tables())
-    fixed = [
-        pltpu.VMEM((PAGE, LANES), F32),
-        pltpu.VMEM(matrices.shape, BF),
-        pltpu.SemaphoreType.DMA((2 + specs.count(HBM),)),
-    ]
-    count = 2 if kernel is drive_outer_kernel else TILES
-    scratch = fixed + [pltpu.VMEM(s, F32) for s in scratch] + [pltpu.VMEM((count, Q, Q), BF)] * 2
-    limit = VMEM_ALL if kernel is filter_kernel else VMEM_LIMIT
-    return call(kernel, outs, (me, pages, matrices, *arrays), [HBM, HBM, *specs], scratch, 1, flops, limit)
+def stay(x):
+    return pltpu.with_memory_space_constraint(x, pltpu.HBM)
+
+
+def work(count):
+    return [pltpu.VMEM((count, Q, Q), BF)] * 2
 
 
 def tie_kernel(rows_ref, _, out_ref):
@@ -448,32 +443,39 @@
     own = lax.all_to_all(packed.reshape(size, -1, LANES), everyone, 0, 0, tiled=True).reshape(2 * ROWS, LANES)
 
     flops = 3 * 2 * 256 * 256 * 256 * 8
-    pieces = (filter_rows, across(filter_rows, 1), filter_far, across(filter_far, 1))
-    filter_spectrum, token = transform(
+    pieces = tuple(map(stay, (filter_rows, across(filter_rows, 1), filter_far, across(filter_far, 1))))
+    matrices, pages = (stay(jnp.asarray(t)) for t in tables())
+    page, table = shape(PAGE, LANES), jax.ShapeDtypeStruct(matrices.shape, BF)
+    vmem = lambda s: pltpu.VMEM(s.shape, s.dtype)
+    f32 = lambda *dims: pltpu.VMEM(dims, F32)
+    sems = lambda count: pltpu.SemaphoreType.DMA((count,))
+    spectrum = call(
         filter_kernel,
-        me,
-        pieces,
-        [HBM] * GROUP,
-        [shape(TILES, Q, Q), shape(8, LANES)],
-        [(GROUP, 2 * ROWS, LANES), (TILES, ROWS, LANES), (TILES, 2, Q, LANES)],
+        [shape(TILES, Q, Q)],
+        (me, pages, matrices, *pieces),
+        [HBM] * 6,
+        [vmem(page), vmem(table), sems(6), f32(GROUP, 2 * ROWS, LANES), f32(TILES, ROWS, LANES), f32(TILES, 2, Q, LANES)]
+        + work(TILES),
+        1,
         FILTER_FLOPS,
+        VMEM_ALL,
     )
-    mine, other = transform(
+    mine, other, *loaded = call(
         drive_outer_kernel,
-        me,
-        (own, token),
-        [whole(own), whole(token)],
-        [shape(2, 2, Q, LANES)] * 2,
-        [(2, ROWS, LANES)],
+        [shape(2, 2, Q, LANES), shape(2, 2, Q, LANES), page, table, shape(TILES, Q, Q)],
+        (me, pages, matrices, own, stay(spectrum)),
+        [HBM, HBM, whole(own), HBM],
+        [f32(2 * LANES, LANES), pltpu.VMEM((2, Q, Q), BF), sems(5), f32(2, ROWS, LANES)] + work(2),
+        1,
         flops,
     )
-    mine, other = transform(
+    mine, other = call(
         product_kernel,
-        me,
-        (mine, across(other, 1), filter_spectrum),
-        [HBM] * 3,
         [shape(4 * ROWS, LANES)] * 2,
-        [(4, 2, Q, LANES), (TILES, Q, Q), (TILES, Q, Q)],
+        (me, mine, across(other, 1), *loaded),
+        None,
+        [f32(4, 2, Q, LANES), f32(TILES, Q, Q)] + work(TILES),
+        1,
         3 * flops,
     )
     result = mine + across(other, 1)

time: 142 us -> 138 us (0.972)
  local copies, waits for them, and re-layouts: 5.99 us -> 0.7 us
  waiting for transfers between devices: 54.4 us -> 57.1 us
  starting transfers between devices: 58.8 us -> 57.3 us
    unnamed x32 -> x16, local copies, waits for them, and re-layouts: 4.4 us -> 0.03 us
  transfers between devices with their start and end apart: 9 -> 9, of which waited for: 7 -> 7; matrix products, arithmetic and copies ran while one was open for 1% -> 0% of each run, Pallas kernels for 7% -> 7%
where the time goes in v3:
time: 138 us
  starting transfers between devices  57.3 us (42%)
  waiting for transfers between devices  57.1 us (41%)
  Pallas kernels  21.5 us (16%)
    all_to_all x1, waiting for transfers between devices, local(): lax.all_to_all(result.reshape(size, -1, LANES), everyone, 0, 0, tiled=True)  32.5 us
    pallas_call x7, Pallas kernels, call(): pl.pallas_call(kernel, out_shape=out_shapes[0] if single else out_shapes,...  21.5 us
    ppermute x5, starting transfers between devices, across(): return lax.ppermute(rows, 'seq', [(i, i ^ mask) for i in range(size)])  16.8 us
    all_to_all x1, starting transfers between devices, local(): lax.all_to_all(filter_rows.reshape(16, 64, LANES), 'seq', 0, 0, tiled=Tru...  16.2 us
    all_to_all x1, starting transfers between devices, local(): lax.all_to_all(packed.reshape(size, -1, LANES), everyone, 0, 0, tiled=True)  11.6 us
    all_to_all x1, starting transfers between devices, local(): lax.all_to_all(result.reshape(size, -1, LANES), everyone, 0, 0, tiled=True)  9.51 us
    ppermute x1, waiting for transfers between devices, local(): lax.ppermute(edges, everyone, [(i, i + 1) for i in range(size - 1)])  9.23 us
    ppermute x5, waiting for transfers between devices, across(): return lax.ppermute(rows, 'seq', [(i, i ^ mask) for i in range(size)])  5.58 us
  transfers between devices with their start and end apart: 9, of which 7 were waited for; matrix products, arithmetic and copies ran while one was open for 0% of the time, Pallas kernels for 7%

profile of v3, /device:TPU:1, one launch (start us, length us, event | category | flops | bytes accessed | tf_op | source)
XLA Modules:
  0.0 137.9 jit_solution(4669258259535136188)
XLA Ops:
  0.0 0.0 copy-start.6
  0.0 2.3 %shard_map.83 = f32[1024,128]{1,0:T(8,128)} custom-call(f32[16,8192]{1,0:T(8,128)} %filter_rows.1), custom_call_target="tpu_custom_call" | custom-call | bytes 1048576 | tf_op jit(solution)/shard_map/pallas_call | solution.py:371
  2.3 16.2 %all-to-all-start.1 = ((f32[16,64,128]{2,1,0:T(8,128)}), f32[16,64,128]{2,1,0:T(8,128)S(1)}, u32[]{:S(2)}, u32[]{:S(2)}) async-start(f32[16,64,128]{2,1,0:T(8,128)} %bitcast.21), calls=%async_computation.1 | async-start | bytes 1048576 | tf_op jit(solution)/shard_map/all_to_all | solution.py:432
  18.6 0.2 slice_reduce_fusion.4
  18.8 0.2 slice_reduce_fusion.2
  19.0 0.2 slice_reduce_fusion
  19.2 3.1 %collective-permute-start = (f32[6,128]{1,0:T(8,128)S(1)}, f32[6,128]{1,0:T(8,128)S(1)}, u32[]{:S(2)}, u32[]{:S(2)}) collective-permute-start(f32[6,128]{1,0:T(8,128)S(1)} %stack.3), channel_id=1, source_target_pairs={{0,1},{1,2},{2,3},{3,4},{4,5},{5,6},{6,7},{7,8},{8,9},{9,10},{10,1... | collective-permute-start | bytes 9224 | tf_op jit(solution)/shard_map/ppermute | solution.py:437
  22.3 9.2 %collective-permute-done = f32[6,128]{1,0:T(8,128)S(1)} collective-permute-done((f32[6,128]{1,0:T(8,128)S(1)}, f32[6,128]{1,0:T(8,128)S(1)}, u32[]{:S(2)}, u32[]{:S(2)}) %collective-permute-start) | collective-permute-done | bytes 3104 | tf_op jit(solution)/shard_map/ppermute | solution.py:437
  31.6 0.0 copy-done.7
  31.6 0.1 copy.26
  31.7 2.0 %shard_map.82 = (f32[1024,128]{1,0:T(8,128)}, f32[128,1024]{1,0:T(8,128)S(1)}, f32[8,16]{1,0:T(8,128)S(1)}) custom-call(f32[128,1024]{1,0:T(8,128)S(1)} %copy-done.1, f32[128,1024]{1,0:T(8,128)S(1)} %copy-done.2, f32[128,16]{1,0:T(8,128)S(1)} %bitcast.18), custom_call_target="tpu_custom_call" | custom-call | bytes 2105856 | tf_op jit(solution)/shard_map/pallas_call | solution.py:371
  33.7 5.3 %all-to-all-done.1 = f32[16,64,128]{2,1,0:T(8,128)S(1)} async-done(((f32[16,64,128]{2,1,0:T(8,128)}), f32[16,64,128]{2,1,0:T(8,128)S(1)}, u32[]{:S(2)}, u32[]{:S(2)}) %all-to-all-start.1) | async-done | bytes 524320 | tf_op jit(solution)/shard_map/all_to_all | solution.py:432
  39.0 2.6 %collective-permute-start.2 = (f32[1024,128]{1,0:T(8,128)S(1)}, f32[1024,128]{1,0:T(8,128)S(1)}, u32[]{:S(2)}, u32[]{:S(2)}) collective-permute-start(f32[1024,128]{1,0:T(8,128)S(1)} %shard_map.84.p0), channel_id=1, source_target_pairs={{0,16},{8,24},{16,0},{24,8},{32,48},{40,56},{48,32},{56,40},{64,80... | collective-permute-start | bytes 1572872 | tf_op jit(solution)/shard_map/ppermute | solution.py:419
  41.6 11.6 %all-to-all-start = ((f32[512,2,128]{2,1,0:T(2,128)}), f32[512,2,128]{2,1,0:T(2,128)S(1)}, u32[]{:S(2)}, u32[]{:S(2)}) async-start(f32[512,2,128]{2,1,0:T(2,128)} %bitcast.3), calls=%async_computation | async-start | bytes 1048576 | tf_op jit(solution)/shard_map/all_to_all | solution.py:443
  53.3 6.2 %collective-permute-start.1 = (f32[1024,128]{1,0:T(8,128)S(1)}, f32[1024,128]{1,0:T(8,128)S(1)}, u32[]{:S(2)}, u32[]{:S(2)}) collective-permute-start(f32[1024,128]{1,0:T(8,128)S(1)} %shard_map.84.p0), channel_id=1, source_target_pairs={{0,8},{8,0},{16,24},{24,16},{32,40},{40,32},{48,56},{56,48},{64,72... | collective-permute-start | bytes 1572872 | tf_op jit(solution)/shard_map/ppermute | solution.py:419
  59.5 0.0 collective-permute-done.2.p2
  59.5 1.9 %collective-permute-start.3 = (f32[1024,128]{1,0:T(8,128)S(1)}, f32[1024,128]{1,0:T(8,128)}, u32[]{:S(2)}, u32[]{:S(2)}) collective-permute-start(f32[1024,128]{1,0:T(8,128)S(1)} %collective-permute-done.2.p2), channel_id=1, source_target_pairs={{0,8},{8,0},{16,24},{24,16},{32,40},{40,32},{48,56},{56,48},{64,72... | collective-permute-start | bytes 1572872 | tf_op jit(solution)/shard_map/ppermute | solution.py:419
  61.5 0.0 collective-permute-done.1.p1
  61.5 2.0 %collective-permute-done.3.p3 = f32[1024,128]{1,0:T(8,128)} collective-permute-done((f32[1024,128]{1,0:T(8,128)S(1)}, f32[1024,128]{1,0:T(8,128)}, u32[]{:S(2)}, u32[]{:S(2)}) %collective-permute-start.3) | collective-permute-done | bytes 524320 | tf_op jit(solution)/shard_map/ppermute | solution.py:419
  63.5 7.2 %shard_map.85.spectrum = f32[8,256,256]{2,1,0:T(8,128)} custom-call(s32[1]{0:T(128)} %bitcast.me_ref, f32[4,1056,128]{2,1,0:T(8,128)} %constant.24.clone.pages, bf16[4,256,256]{2,1,0:T(8,128)(2,1)} %constant.23.clone.matrices, f32[1024,128]{1,0:T(8,128)} %copy-done, f32[1024,128]{1,0:T(8,128)} %copy-done.5, f32[1024,128]{1,0:T(8,128)} %copy-done.4, ...), custom_call_target="tpu_custom_call" | custom-call | flops 1610612736 | bytes 6881284 | tf_op jit(solution)/shard_map/pallas_call | solution.py:371
  70.7 4.4 %all-to-all-done = f32[512,2,128]{2,1,0:T(2,128)S(1)} async-done(((f32[512,2,128]{2,1,0:T(2,128)}), f32[512,2,128]{2,1,0:T(2,128)S(1)}, u32[]{:S(2)}, u32[]{:S(2)}) %all-to-all-start) | async-done | bytes 524320 | tf_op jit(solution)/shard_map/all_to_all | solution.py:443
  75.2 2.4 %shard_map.86 = (f32[2,2,256,128]{3,2,1,0:T(8,128)S(1)}, f32[2,2,256,128]{3,2,1,0:T(8,128)S(1)}, f32[1056,128]{1,0:T(8,128)S(1)}, bf16[4,256,256]{2,1,0:T(8,128)(2,1)S(1)}, f32[8,256,256]{2,1,0:T(8,128)S(1)}) custom-call(s32[1]{0:T(128)} %bitcast.me_ref, f32[4,1056,128]{2,1,0:T(8,128)} %constant.24.clone.pages, ...), custom_call_target="tpu_custom_call" | custom-call | flops 805306368 | bytes 10043396 | tf_op jit(solution)/shard_map/pallas_call | solution.py:371
  77.6 3.7 %collective-permute-start.4 = (f32[2,2,256,128]{3,2,1,0:T(8,128)S(1)}, f32[2,2,256,128]{3,2,1,0:T(8,128)S(1)}, u32[]{:S(2)}, u32[]{:S(2)}) collective-permute-start(f32[2,2,256,128]{3,2,1,0:T(8,128)S(1)} %get-tuple-element.20), channel_id=1, source_target_pairs={{0,8},{8,0},{16,24},{24,16},{32,40},{40,32},{48,56},{56,48},{64,72... | collective-permute-start | bytes 1572872 | tf_op jit(solution)/shard_map/ppermute | solution.py:419
  81.3 1.3 collective-permute-done.4.peer_ref
  82.7 5.6 %shard_map.87 = (f32[2048,128]{1,0:T(8,128)S(1)}, f32[2048,128]{1,0:T(8,128)S(1)}) custom-call(s32[1]{0:T(128)} %bitcast.me_ref, f32[2,2,256,128]{3,2,1,0:T(8,128)S(1)} %get-tuple-element.19.own_ref, f32[2,2,256,128]{3,2,1,0:T(8,128)S(1)} %collective-permute-done.4.peer_ref, f32[1056,128]{1,0:T(8,128)S(1)} %get-tuple-element.21.page_ref, ...), custom_call_target="tpu_custom_call" | custom-call | flops 2415919104 | bytes 6307844 | tf_op jit(solution)/shard_map/pallas_call | solution.py:371
  88.3 2.3 %collective-permute-start.5 = (f32[2048,128]{1,0:T(8,128)S(1)}, f32[2048,128]{1,0:T(8,128)S(1)}, u32[]{:S(2)}, u32[]{:S(2)}) collective-permute-start(f32[2048,128]{1,0:T(8,128)S(1)} %get-tuple-element.25), channel_id=1, source_target_pairs={{0,8},{8,0},{16,24},{24,16},{32,40},{40,32},{48,56},{56,48},{64,72... | collective-permute-start | bytes 3145736 | tf_op jit(solution)/shard_map/ppermute | solution.py:419
  90.6 2.3 %collective-permute-done.5 = f32[2048,128]{1,0:T(8,128)S(1)} collective-permute-done((f32[2048,128]{1,0:T(8,128)S(1)}, f32[2048,128]{1,0:T(8,128)S(1)}, u32[]{:S(2)}, u32[]{:S(2)}) %collective-permute-start.5) | collective-permute-done | bytes 1048608 | tf_op jit(solution)/shard_map/ppermute | solution.py:419
  92.8 1.1 add.8
  93.9 9.5 %all-to-all-start.2 = ((f32[512,4,128]{2,1,0:T(4,128)}), f32[512,4,128]{2,1,0:T(4,128)S(1)}, u32[]{:S(2)}, u32[]{:S(2)}) async-start(f32[512,4,128]{2,1,0:T(4,128)} %bitcast.20), calls=%async_computation.2 | async-start | bytes 2097152 | tf_op jit(solution)/shard_map/all_to_all | solution.py:483
  103.4 0.5 shard_map.88
  103.9 32.5 %all-to-all-done.2 = f32[512,4,128]{2,1,0:T(4,128)S(1)} async-done(((f32[512,4,128]{2,1,0:T(4,128)}), f32[512,4,128]{2,1,0:T(4,128)S(1)}, u32[]{:S(2)}, u32[]{:S(2)}) %all-to-all-start.2) | async-done | bytes 1048608 | tf_op jit(solution)/shard_map/all_to_all | solution.py:483
  136.5 1.4 %shard_map.89 = f32[128,1024]{1,0:T(8,128)} custom-call(f32[2048,128]{1,0:T(8,128)S(1)} %bitcast.16, f32[128,1024]{1,0:T(8,128)S(1)} %get-tuple-element.27.gain_ref, f32[128,1024]{1,0:T(8,128)S(1)} %get-tuple-element.28.direct_ref), custom_call_target="tpu_custom_call" | custom-call | bytes 2621440 | tf_op jit(solution)/shard_map/pallas_call | solution.py:371
  (18 shorter events, 0.1 us)
Async XLA Ops:
  0.0 18.6 %copy-start.3 = (f32[128,1024]{1,0:T(8,128)S(1)}, f32[128,1024]{1,0:T(8,128)}, u32[]{:S(2)}) copy-start(f32[128,1024]{1,0:T(8,128)} %queries_ref.1) | copy-start | bytes 1572868
  0.0 18.8 %copy-start.1 = (f32[128,1024]{1,0:T(8,128)S(1)}, f32[128,1024]{1,0:T(8,128)}, u32[]{:S(2)}) copy-start(f32[128,1024]{1,0:T(8,128)} %keys_ref.1) | copy-start | bytes 1572868
  0.0 19.0 %copy-start.2 = (f32[128,1024]{1,0:T(8,128)S(1)}, f32[128,1024]{1,0:T(8,128)}, u32[]{:S(2)}) copy-start(f32[128,1024]{1,0:T(8,128)} %values_ref.1) | copy-start | bytes 1572868
  0.0 22.3 %copy-start.6 = (f32[3,3,128]{2,1,0:T(4,128)S(1)}, f32[3,3,128]{2,1,0:T(4,128)}, u32[]{:S(2)}) copy-start(f32[3,3,128]{2,1,0:T(4,128)} %param.11) | copy-start | bytes 13828
  0.0 31.5 %copy-start.7 = (f32[128]{0:T(128)S(1)}, f32[128]{0:T(128)}, u32[]{:S(2)}) copy-start(f32[128]{0:T(128)} %param.13) | copy-start | bytes 1540
  2.3 36.7 %all-to-all-start.1 = ((f32[16,64,128]{2,1,0:T(8,128)}), f32[16,64,128]{2,1,0:T(8,128)S(1)}, u32[]{:S(2)}, u32[]{:S(2)}) async-start(f32[16,64,128]{2,1,0:T(8,128)} %bitcast.21), calls=%async_computation.1 | async-start | bytes 1048576 | tf_op jit(solution)/shard_map/all_to_all | solution.py:432
  19.2 12.4 %collective-permute-start = (f32[6,128]{1,0:T(8,128)S(1)}, f32[6,128]{1,0:T(8,128)S(1)}, u32[]{:S(2)}, u32[]{:S(2)}) collective-permute-start(f32[6,128]{1,0:T(8,128)S(1)} %stack.3), channel_id=1, source_target_pairs={{0,1},{1,2},{2,3},{3,4},{4,5},{5,6},{6,7},{7,8},{8,9},{9,10},{10,1... | collective-permute-start | bytes 9224 | tf_op jit(solution)/shard_map/ppermute | solution.py:437
  39.0 24.5 %copy-start = (f32[1024,128]{1,0:T(8,128)}, f32[1024,128]{1,0:T(8,128)S(1)}, u32[]{:S(2)}) copy-start(f32[1024,128]{1,0:T(8,128)S(1)} %shard_map.84.p0) | copy-start | bytes 1572868
  39.0 20.5 %collective-permute-start.2 = (f32[1024,128]{1,0:T(8,128)S(1)}, f32[1024,128]{1,0:T(8,128)S(1)}, u32[]{:S(2)}, u32[]{:S(2)}) collective-permute-start(f32[1024,128]{1,0:T(8,128)S(1)} %shard_map.84.p0), channel_id=1, source_target_pairs={{0,16},{8,24},{16,0},{24,8},{32,48},{40,56},{48,32},{56,40},{64,80... | collective-permute-start | bytes 1572872 | tf_op jit(solution)/shard_map/ppermute | solution.py:419
  41.6 33.5 %all-to-all-start = ((f32[512,2,128]{2,1,0:T(2,128)}), f32[512,2,128]{2,1,0:T(2,128)S(1)}, u32[]{:S(2)}, u32[]{:S(2)}) async-start(f32[512,2,128]{2,1,0:T(2,128)} %bitcast.3), calls=%async_computation | async-start | bytes 1048576 | tf_op jit(solution)/shard_map/all_to_all | solution.py:443
  53.3 8.2 %collective-permute-start.1 = (f32[1024,128]{1,0:T(8,128)S(1)}, f32[1024,128]{1,0:T(8,128)S(1)}, u32[]{:S(2)}, u32[]{:S(2)}) collective-permute-start(f32[1024,128]{1,0:T(8,128)S(1)} %shard_map.84.p0), channel_id=1, source_target_pairs={{0,8},{8,0},{16,24},{24,16},{32,40},{40,32},{48,56},{56,48},{64,72... | collective-permute-start | bytes 1572872 | tf_op jit(solution)/shard_map/ppermute | solution.py:419
  59.5 4.0 %copy-start.4 = (f32[1024,128]{1,0:T(8,128)}, f32[1024,128]{1,0:T(8,128)S(1)}, u32[]{:S(2)}) copy-start(f32[1024,128]{1,0:T(8,128)S(1)} %collective-permute-done.2.p2) | copy-start | bytes 1572868
  59.5 3.9 %collective-permute-start.3 = (f32[1024,128]{1,0:T(8,128)S(1)}, f32[1024,128]{1,0:T(8,128)}, u32[]{:S(2)}, u32[]{:S(2)}) collective-permute-start(f32[1024,128]{1,0:T(8,128)S(1)} %collective-permute-done.2.p2), channel_id=1, source_target_pairs={{0,8},{8,0},{16,24},{24,16},{32,40},{40,32},{48,56},{56,48},{64,72... | collective-permute-start | bytes 1572872 | tf_op jit(solution)/shard_map/ppermute | solution.py:419
  61.5 2.0 %copy-start.5 = (f32[1024,128]{1,0:T(8,128)}, f32[1024,128]{1,0:T(8,128)S(1)}, u32[]{:S(2)}) copy-start(f32[1024,128]{1,0:T(8,128)S(1)} %collective-permute-done.1.p1) | copy-start | bytes 1572868
  77.6 5.1 %collective-permute-start.4 = (f32[2,2,256,128]{3,2,1,0:T(8,128)S(1)}, f32[2,2,256,128]{3,2,1,0:T(8,128)S(1)}, u32[]{:S(2)}, u32[]{:S(2)}) collective-permute-start(f32[2,2,256,128]{3,2,1,0:T(8,128)S(1)} %get-tuple-element.20), channel_id=1, source_target_pairs={{0,8},{8,0},{16,24},{24,16},{32,40},{40,32},{48,56},{56,48},{64,72... | collective-permute-start | bytes 1572872 | tf_op jit(solution)/shard_map/ppermute | solution.py:419
  88.3 4.6 %collective-permute-start.5 = (f32[2048,128]{1,0:T(8,128)S(1)}, f32[2048,128]{1,0:T(8,128)S(1)}, u32[]{:S(2)}, u32[]{:S(2)}) collective-permute-start(f32[2048,128]{1,0:T(8,128)S(1)} %get-tuple-element.25), channel_id=1, source_target_pairs={{0,8},{8,0},{16,24},{24,16},{32,40},{40,32},{48,56},{56,48},{64,72... | collective-permute-start | bytes 3145736 | tf_op jit(solution)/shard_map/ppermute | solution.py:419
  93.9 42.6 %all-to-all-start.2 = ((f32[512,4,128]{2,1,0:T(4,128)}), f32[512,4,128]{2,1,0:T(4,128)S(1)}, u32[]{:S(2)}, u32[]{:S(2)}) async-start(f32[512,4,128]{2,1,0:T(4,128)} %bitcast.20), calls=%async_computation.2 | async-start | bytes 2097152 | tf_op jit(solution)/shard_map/all_to_all | solution.py:483

commit v4 on v3

--- a/solution.py
+++ b/solution.py
@@ -77,14 +77,20 @@
     return jnp.dot(a, b, preferred_element_type=F32)
 
 
-def pack_filter_kernel(filter_rows, out_ref, held_ref, sem_ref):
+def pack_filter_kernel(filter_rows, out, held_ref, packed_ref, sem_ref):
     width = filter_rows.shape[1] // 4
-    pieces = [filter_rows.at[:, pl.ds(n * width, width)] for n in range(4)]
-    loads = Loads(sem_ref, [(piece, held_ref.at[n]) for n, piece in enumerate(pieces)])
+    tiles = width // LANES
+    ins = [(filter_rows.at[:, pl.ds(n * width, width)], held_ref.at[n]) for n in range(4)]
+    loads = Loads(sem_ref.at[pl.ds(0, 4)], ins)
+    stores = []
     for n in range(4):
         loads.wait(n)
-        for tile in range(width // LANES):
-            out_ref[pl.ds(n * (width // LANES) + tile, 16, stride=64), :] = held_ref[n, :, tile * LANES : (tile + 1) * LANES]
+        for tile in range(tiles):
+            packed_ref[n, pl.ds(tile, 16, stride=tiles), :] = held_ref[n, :, tile * LANES : (tile + 1) * LANES]
+        piece = packed_ref.at[n].reshape(16, tiles, LANES)
+        stores.append(Loads(sem_ref.at[pl.ds(4 + n, 1)], [(piece, out.at[:, pl.ds(n * tiles, tiles), :])]))
+    for store in stores:
+        store.wait(0)
 
 
 def feature(signal, taps, older, newer):
@@ -278,43 +284,52 @@
         out_ref[r] = right_product(matrix_ref, 0, high_ref[r], low_ref[r])
 
 
-def drive_outer_kernel(
+def drive_tiles(own_ref, x_ref):
+    for half in range(2):
+        x_ref[half] = own_ref[pl.ds(half, ROWS, stride=2), :]
+
+
+def drive_other_kernel(me_ref, pages, matrices, own_ref, _, other_ref, mix_ref, ahead_ref, sem_ref, x_ref, high_ref, low_ref):
+    mix, ahead = pages.at[me_ref[0], pl.ds(MIX, 2 * LANES)], matrices.at[pl.ds(2, 2)]
+    loads = Loads(sem_ref, [(mix, mix_ref), (ahead, ahead_ref)])
+    drive_tiles(own_ref, x_ref)
+    loads.wait(0, 1)
+    outer_transform(x_ref, 2, 1, mix_ref, 0, ahead_ref, 0, other_ref, high_ref, low_ref)
+
+
+def drive_mine_kernel(
+    me_ref, pages, matrices, own_ref, mix_ref, ahead_ref, mine_ref, page_ref, matrix_ref, sem_ref, x_ref, high_ref, low_ref
+):
+    loads = Loads(sem_ref, [(pages.at[me_ref[0]], page_ref), (matrices, matrix_ref)])
+    drive_tiles(own_ref, x_ref)
+    outer_transform(x_ref, 2, 0, mix_ref, 0, ahead_ref, 0, mine_ref, high_ref, low_ref)
+    loads.wait(0, 1)
+
+
+def product_kernel(
     me_ref,
-    pages,
-    matrices,
     own_ref,
-    spectrum,
-    mine_ref,
-    other_ref,
+    peer_ref,
     page_ref,
     matrix_ref,
+    spectrum,
+    other_ref,
+    left_high_ref,
+    left_low_ref,
+    sem_ref,
     filter_ref,
-    mix_ref,
-    ahead_ref,
-    sem_ref,
-    x_ref,
+    f_ref,
+    d_ref,
     high_ref,
     low_ref,
 ):
-    page = pages.at[me_ref[0]]
-    first = [(page.at[pl.ds(MIX, 2 * LANES)], mix_ref), (matrices.at[pl.ds(2, 2)], ahead_ref)]
-    loads = Loads(sem_ref, [*first, (page, page_ref), (matrices, matrix_ref), (spectrum, filter_ref)])
-    for half in range(2):
-        x_ref[half] = own_ref[pl.ds(half, ROWS, stride=2), :]
-    loads.wait(0, 1)
-    outer_transform(x_ref, 2, 1, mix_ref, 0, ahead_ref, 0, other_ref, high_ref, low_ref)
-    outer_transform(x_ref, 2, 0, mix_ref, 0, ahead_ref, 0, mine_ref, high_ref, low_ref)
-    loads.wait(2, 3, 4)
-
-
-def product_kernel(
-    me_ref, own_ref, peer_ref, page_ref, matrix_ref, filter_ref, mine_ref, other_ref, f_ref, d_ref, high_ref, low_ref
-):
     core = me_ref[0] & 1
+    loads = Loads(sem_ref, [(spectrum, filter_ref)])
     for which, piece_ref in ((core, own_ref), (1 - core, peer_ref)):
         for half in range(2):
             f_ref[2 * which + half] = piece_ref[half]
     inner_transform(f_ref, 4, 0, 16, page_ref, high_ref, low_ref)
+    loads.wait(0)
     for r in range(TILES):
         x, h = right_product(matrix_ref, 0, high_ref[r], low_ref[r]), filter_ref[r]
         value = times((x[:, :LANES], x[:, LANES:]), (h[:, :LANES], h[:, LANES:]))
@@ -337,22 +352,33 @@
             for part in range(2):
                 at = slice(part * LANES + kappa, part * LANES + kappa + CHUNK), slice(q * LANES, (q + 1) * LANES)
                 high_ref[s, *at], low_ref[s, *at] = split(value[part])
-    for s in range(TILES):
-        d_ref[s] = left_product(matrix_ref, 0, high_ref[s], low_ref[s])
+    for t in range(4):
+        left_high_ref[t] = high_ref[4 * core + t]
+        left_low_ref[t] = low_ref[4 * core + t]
+        high, low = high_ref[4 * (1 - core) + t], low_ref[4 * (1 - core) + t]
+        d_ref[t] = left_product(matrix_ref, 0, high, low)
+    blend(d_ref, page_ref, other_ref)
+
+
+def blend(d_ref, page_ref, out_ref):
     for chunk in range(LANES // CHUNK):
         rows = slice(chunk * CHUNK, (chunk + 1) * CHUNK)
         mix = mixes(page_ref, 0, rows, 16)
-        for owner, out_ref in ((core, mine_ref), (1 - core, other_ref)):
-            for t in range(4):
-                s = 4 * owner + t
-                v = [
-                    d_ref[s, part * LANES + rows.start : part * LANES + rows.stop, q * LANES : (q + 1) * LANES]
-                    for q in range(2)
-                    for part in range(2)
-                ]
-                for a in range(4):
-                    value = mixed(mix[4 * a : 4 * a + 4], v)
-                    out_ref[pl.ds((a * LANES + rows.start) * 4 + t, CHUNK, stride=4), :] = value
+        for t in range(4):
+            v = [
+                d_ref[t, part * LANES + rows.start : part * LANES + rows.stop, q * LANES : (q + 1) * LANES]
+                for q in range(2)
+                for part in range(2)
+            ]
+            for a in range(4):
+                value = mixed(mix[4 * a : 4 * a + 4], v)
+                out_ref[pl.ds((a * LANES + rows.start) * 4 + t, CHUNK, stride=4), :] = value
+
+
+def mine_kernel(high_ref, low_ref, page_ref, matrix_ref, out_ref, d_ref):
+    for t in range(4):
+        d_ref[t] = left_product(matrix_ref, 0, high_ref[t], low_ref[t])
+    blend(d_ref, page_ref, out_ref)
 
 
 VMEM_LIMIT = 32 * 1024 * 1024
@@ -364,10 +390,10 @@
     return pl.BlockSpec(s.shape, lambda *_, n=len(s.shape): (0,) * n)
 
 
-def call(kernel, out_shapes, args, in_specs=None, scratch=(), prefetch=0, flops=0, limit=VMEM_LIMIT):
+def call(kernel, out_shapes, args, in_specs=None, scratch=(), prefetch=0, flops=0, limit=VMEM_LIMIT, out_specs=None):
     nbytes = sum(a.size * a.dtype.itemsize for a in args) + sum(int(np.prod(s.shape)) * 4 for s in out_shapes)
     single = len(out_shapes) == 1
-    out_specs = [whole(s) for s in out_shapes]
+    out_specs = out_specs or [whole(s) for s in out_shapes]
     return pl.pallas_call(
         kernel,
         out_shape=out_shapes[0] if single else out_shapes,
@@ -426,11 +452,11 @@
     me = (lax.axis_index("seq") % GROUP).astype(jnp.int32).reshape(1)
     channels = queries.shape[0]
 
-    held = [pltpu.VMEM((4, 16, 2 * COLS), F32), pltpu.SemaphoreType.DMA((4,))]
-    filter_rows = call(pack_filter_kernel, [shape(2 * ROWS, LANES)], (long_filter,), [HBM], held, limit=VMEM_ALL)
+    held = [pltpu.VMEM((4, 16, 2 * COLS), F32), pltpu.VMEM((4, 2 * LANES, LANES), F32), pltpu.SemaphoreType.DMA((8,))]
+    filter_rows = call(pack_filter_kernel, [shape(16, 64, LANES)], (long_filter,), [HBM], held, limit=VMEM_ALL, out_specs=[HBM])
     alike = [list(range(member, seq_size, GROUP)) for member in range(GROUP)]
     filter_rows = lax.all_to_all(
-        filter_rows.reshape(16, 64, LANES), "seq", 0, 0, tiled=True, axis_index_groups=alike
+        filter_rows, "seq", 0, 0, tiled=True, axis_index_groups=alike
     ).reshape(2 * ROWS, LANES)
 
     edges = jnp.stack((queries[:, -2], queries[:, -1], keys[:, -2], keys[:, -1], values[:, -2], values[:, -1]))
@@ -460,24 +486,38 @@
         FILTER_FLOPS,
         VMEM_ALL,
     )
-    mine, other, *loaded = call(
-        drive_outer_kernel,
-        [shape(2, 2, Q, LANES), shape(2, 2, Q, LANES), page, table, shape(TILES, Q, Q)],
-        (me, pages, matrices, own, stay(spectrum)),
+    half, mix, ahead = shape(2, 2, Q, LANES), shape(2 * LANES, LANES), jax.ShapeDtypeStruct((2, Q, Q), BF)
+    spectrum = stay(spectrum)
+    other, mix, ahead = call(
+        drive_other_kernel,
+        [half, mix, ahead],
+        (me, pages, matrices, own, spectrum),
         [HBM, HBM, whole(own), HBM],
-        [f32(2 * LANES, LANES), pltpu.VMEM((2, Q, Q), BF), sems(5), f32(2, ROWS, LANES)] + work(2),
+        [sems(2), f32(2, ROWS, LANES)] + work(2),
         1,
-        flops,
+        flops // 2,
     )
-    mine, other = call(
+    mine, page, table = call(
+        drive_mine_kernel,
+        [half, page, table],
+        (me, pages, matrices, own, mix, ahead),
+        [HBM, HBM, whole(own), whole(mix), whole(ahead)],
+        [sems(2), f32(2, ROWS, LANES)] + work(2),
+        1,
+        flops // 2,
+    )
+    peer = across(other, 1)
+    left = jax.ShapeDtypeStruct((4, Q, Q), BF)
+    other, *left = call(
         product_kernel,
-        [shape(4 * ROWS, LANES)] * 2,
-        (me, mine, across(other, 1), *loaded),
-        None,
-        [f32(4, 2, Q, LANES), f32(TILES, Q, Q)] + work(TILES),
+        [shape(4 * ROWS, LANES), left, left],
+        (me, mine, peer, page, table, spectrum),
+        [whole(mine), whole(peer), whole(page), whole(table), HBM],
+        [sems(1), f32(TILES, Q, Q), f32(4, 2, Q, LANES), f32(TILES, Q, Q)] + work(TILES),
         1,
         3 * flops,
     )
+    mine = call(mine_kernel, [shape(4 * ROWS, LANES)], (*left, page, table), None, [f32(4, Q, Q)], 0, flops)
     result = mine + across(other, 1)
     gain, direct = call(gate_kernel, [shape(channels, COLS)] * 2, (queries, drive, small))
     returned = lax.all_to_all(result.reshape(size, -1, LANES), everyone, 0, 0, tiled=True).reshape(4 * ROWS, LANES)

time: 138 us -> 138 us (level)
  waiting for transfers between devices: 57.1 us -> 55.4 us
  Pallas kernels: 21.5 us -> 23.2 us
    pallas_call x7 -> x9, Pallas kernels: 21.5 us -> 23.2 us  [call(): pl.pallas_call(kernel, out_shape=out_shapes[0] if single else out_shapes,...]
    ppermute x5, waiting for transfers between devices: 5.58 us -> 3.87 us  [across(): return lax.ppermute(rows, 'seq', [(i, i ^ mask) for i in range(size)])]
  transfers between devices with their start and end apart: 9 -> 9, of which waited for: 7 -> 6; matrix products, arithmetic and copies ran while one was open for 0% -> 0% of each run, Pallas kernels for 7% -> 9%
where the time goes in v4:
time: 138 us; the launch traced here: 137 us
  starting transfers between devices  56.8 us (41%)
  waiting for transfers between devices  55.4 us (40%)
  Pallas kernels  23.2 us (17%)
    all_to_all x1, waiting for transfers between devices, local(): lax.all_to_all(result.reshape(size, -1, LANES), everyone, 0, 0, tiled=True)  32.5 us
    pallas_call x9, Pallas kernels, call(): pl.pallas_call(kernel, out_shape=out_shapes[0] if single else out_shapes,...  23.2 us
    ppermute x5, starting transfers between devices, across(): return lax.ppermute(rows, 'seq', [(i, i ^ mask) for i in range(size)])  16.4 us
    all_to_all x1, starting transfers between devices, local(): lax.all_to_all(filter_rows, 'seq', 0, 0, tiled=True, axis_index_groups=al...  16.2 us
    all_to_all x1, starting transfers between devices, local(): lax.all_to_all(packed.reshape(size, -1, LANES), everyone, 0, 0, tiled=True)  11.6 us
    all_to_all x1, starting transfers between devices, local(): lax.all_to_all(result.reshape(size, -1, LANES), everyone, 0, 0, tiled=True)  9.43 us
    ppermute x1, waiting for transfers between devices, local(): lax.ppermute(edges, everyone, [(i, i + 1) for i in range(size - 1)])  9.23 us
    all_to_all x1, waiting for transfers between devices, local(): lax.all_to_all(filter_rows, 'seq', 0, 0, tiled=True, axis_index_groups=al...  5.3 us
  transfers between devices with their start and end apart: 9, of which 6 were waited for; matrix products, arithmetic and copies ran while one was open for 0% of the time, Pallas kernels for 9%

profile of v4, /device:TPU:1, one launch (start us, length us, event | category | flops | bytes accessed | tf_op | source)
XLA Modules:
  0.0 137.5 jit_solution(12244433216470933677)
XLA Ops:
  0.0 2.0 %shard_map.83 = f32[16,64,128]{2,1,0:T(8,128)} custom-call(f32[16,8192]{1,0:T(8,128)} %filter_rows.1), custom_call_target="tpu_custom_call" | custom-call | bytes 1048576 | tf_op jit(solution)/shard_map/pallas_call | solution.py:397
  2.0 16.2 %all-to-all-start.1 = ((f32[16,64,128]{2,1,0:T(8,128)}), f32[16,64,128]{2,1,0:T(8,128)S(1)}, u32[]{:S(2)}, u32[]{:S(2)}) async-start(f32[16,64,128]{2,1,0:T(8,128)} %shard_map.83), calls=%async_computation.1 | async-start | bytes 1048576 | tf_op jit(solution)/shard_map/all_to_all | solution.py:458
  18.3 0.2 slice_reduce_fusion.4
  18.5 0.2 slice_reduce_fusion.2
  18.7 0.2 slice_reduce_fusion
  18.9 3.1 %collective-permute-start = (f32[6,128]{1,0:T(8,128)S(1)}, f32[6,128]{1,0:T(8,128)S(1)}, u32[]{:S(2)}, u32[]{:S(2)}) collective-permute-start(f32[6,128]{1,0:T(8,128)S(1)} %stack.3), channel_id=1, source_target_pairs={{0,1},{1,2},{2,3},{3,4},{4,5},{5,6},{6,7},{7,8},{8,9},{9,10},{10,1... | collective-permute-start | bytes 9224 | tf_op jit(solution)/shard_map/ppermute | solution.py:463
  22.0 9.2 %collective-permute-done = f32[6,128]{1,0:T(8,128)S(1)} collective-permute-done((f32[6,128]{1,0:T(8,128)S(1)}, f32[6,128]{1,0:T(8,128)S(1)}, u32[]{:S(2)}, u32[]{:S(2)}) %collective-permute-start) | collective-permute-done | bytes 3104 | tf_op jit(solution)/shard_map/ppermute | solution.py:463
  31.3 0.1 copy.26
  31.4 2.0 %shard_map.82 = (f32[1024,128]{1,0:T(8,128)}, f32[128,1024]{1,0:T(8,128)S(1)}, f32[8,16]{1,0:T(8,128)S(1)}) custom-call(f32[128,1024]{1,0:T(8,128)S(1)} %copy-done.1, f32[128,1024]{1,0:T(8,128)S(1)} %copy-done.2, f32[128,16]{1,0:T(8,128)S(1)} %bitcast.18), custom_call_target="tpu_custom_call" | custom-call | bytes 2105856 | tf_op jit(solution)/shard_map/pallas_call | solution.py:397
  33.4 5.3 %all-to-all-done.1 = f32[16,64,128]{2,1,0:T(8,128)S(1)} async-done(((f32[16,64,128]{2,1,0:T(8,128)}), f32[16,64,128]{2,1,0:T(8,128)S(1)}, u32[]{:S(2)}, u32[]{:S(2)}) %all-to-all-start.1) | async-done | bytes 524320 | tf_op jit(solution)/shard_map/all_to_all | solution.py:458
  38.7 2.6 %collective-permute-start.2 = (f32[1024,128]{1,0:T(8,128)S(1)}, f32[1024,128]{1,0:T(8,128)S(1)}, u32[]{:S(2)}, u32[]{:S(2)}) collective-permute-start(f32[1024,128]{1,0:T(8,128)S(1)} %shard_map.84.p0), channel_id=1, source_target_pairs={{0,16},{8,24},{16,0},{24,8},{32,48},{40,56},{48,32},{56,40},{64,80... | collective-permute-start | bytes 1572872 | tf_op jit(solution)/shard_map/ppermute | solution.py:445
  41.4 11.6 %all-to-all-start = ((f32[512,2,128]{2,1,0:T(2,128)}), f32[512,2,128]{2,1,0:T(2,128)S(1)}, u32[]{:S(2)}, u32[]{:S(2)}) async-start(f32[512,2,128]{2,1,0:T(2,128)} %bitcast.3), calls=%async_computation | async-start | bytes 1048576 | tf_op jit(solution)/shard_map/all_to_all | solution.py:469
  53.0 6.2 %collective-permute-start.1 = (f32[1024,128]{1,0:T(8,128)S(1)}, f32[1024,128]{1,0:T(8,128)S(1)}, u32[]{:S(2)}, u32[]{:S(2)}) collective-permute-start(f32[1024,128]{1,0:T(8,128)S(1)} %shard_map.84.p0), channel_id=1, source_target_pairs={{0,8},{8,0},{16,24},{24,16},{32,40},{40,32},{48,56},{56,48},{64,72... | collective-permute-start | bytes 1572872 | tf_op jit(solution)/shard_map/ppermute | solution.py:445
  59.2 0.0 collective-permute-done.2.p2
  59.2 1.9 %collective-permute-start.3 = (f32[1024,128]{1,0:T(8,128)S(1)}, f32[1024,128]{1,0:T(8,128)}, u32[]{:S(2)}, u32[]{:S(2)}) collective-permute-start(f32[1024,128]{1,0:T(8,128)S(1)} %collective-permute-done.2.p2), channel_id=1, source_target_pairs={{0,8},{8,0},{16,24},{24,16},{32,40},{40,32},{48,56},{56,48},{64,72... | collective-permute-start | bytes 1572872 | tf_op jit(solution)/shard_map/ppermute | solution.py:445
  61.2 0.0 collective-permute-done.1.p1
  61.2 2.0 %collective-permute-done.3.p3 = f32[1024,128]{1,0:T(8,128)} collective-permute-done((f32[1024,128]{1,0:T(8,128)S(1)}, f32[1024,128]{1,0:T(8,128)}, u32[]{:S(2)}, u32[]{:S(2)}) %collective-permute-start.3) | collective-permute-done | bytes 524320 | tf_op jit(solution)/shard_map/ppermute | solution.py:445
  63.2 7.2 %shard_map.85._.spectrum = f32[8,256,256]{2,1,0:T(8,128)} custom-call(s32[1]{0:T(128)} %bitcast.me_ref, f32[4,1056,128]{2,1,0:T(8,128)} %constant.24.clone.pages, bf16[4,256,256]{2,1,0:T(8,128)(2,1)} %constant.23.clone.matrices, f32[1024,128]{1,0:T(8,128)} %copy-done, f32[1024,128]{1,0:T(8,128)} %copy-done.5, f32[1024,128]{1,0:T(8,128)} %copy-done.4, ...), custom_call_target="tpu_custom_call" | custom-call | flops 1610612736 | bytes 6881284 | tf_op jit(solution)/shard_map/pallas_call | solution.py:397
  70.4 4.4 %all-to-all-done = f32[512,2,128]{2,1,0:T(2,128)S(1)} async-done(((f32[512,2,128]{2,1,0:T(2,128)}), f32[512,2,128]{2,1,0:T(2,128)S(1)}, u32[]{:S(2)}, u32[]{:S(2)}) %all-to-all-start) | async-done | bytes 524320 | tf_op jit(solution)/shard_map/all_to_all | solution.py:469
  74.9 1.9 %shard_map.86 = (f32[2,2,256,128]{3,2,1,0:T(8,128)S(1)}, f32[256,128]{1,0:T(8,128)S(1)}, bf16[2,256,256]{2,1,0:T(8,128)(2,1)S(1)}) custom-call(s32[1]{0:T(128)} %bitcast.me_ref, f32[4,1056,128]{2,1,0:T(8,128)} %constant.24.clone.pages, bf16[4,256,256]{2,1,0:T(8,128)(2,1)} %constant.23.clone.matrices, f32[1024,128]{1,0:T(8,128)S(1)} %bitcast.15, ...), custom_call_target="tpu_custom_call" | custom-call | flops 402653184 | bytes 6488068 | tf_op jit(solution)/shard_map/pallas_call | solution.py:397
  76.8 3.7 %collective-permute-start.4 = (f32[2,2,256,128]{3,2,1,0:T(8,128)S(1)}, f32[2,2,256,128]{3,2,1,0:T(8,128)S(1)}, u32[]{:S(2)}, u32[]{:S(2)}) collective-permute-start(f32[2,2,256,128]{3,2,1,0:T(8,128)S(1)} %get-tuple-element.24), channel_id=1, source_target_pairs={{0,8},{8,0},{16,24},{24,16},{32,40},{40,32},{48,56},{56,48},{64,72... | collective-permute-start | bytes 1572872 | tf_op jit(solution)/shard_map/ppermute | solution.py:445
  80.5 1.9 %shard_map.87 = (f32[2,2,256,128]{3,2,1,0:T(8,128)S(1)}, f32[1056,128]{1,0:T(8,128)S(1)}, bf16[4,256,256]{2,1,0:T(8,128)(2,1)S(1)}) custom-call(s32[1]{0:T(128)} %bitcast.me_ref, f32[4,1056,128]{2,1,0:T(8,128)} %constant.24.clone.pages, bf16[4,256,256]{2,1,0:T(8,128)(2,1)} %constant.23.clone.matrices, f32[1024,128]{1,0:T(8,128)S(1)} %bitcast.16, ...), custom_call_target="tpu_custom_call" | custom-call | flops 402653184 | bytes 5718020 | tf_op jit(solution)/shard_map/pallas_call | solution.py:397
  82.4 0.0 collective-permute-done.4.peer_ref
  82.5 5.5 %shard_map.88 = (f32[2048,128]{1,0:T(8,128)S(1)}, bf16[4,256,256]{2,1,0:T(8,128)(2,1)S(1)}, bf16[4,256,256]{2,1,0:T(8,128)(2,1)S(1)}) custom-call(s32[1]{0:T(128)} %bitcast.me_ref, f32[2,2,256,128]{3,2,1,0:T(8,128)S(1)} %get-tuple-element.23.own_ref, f32[2,2,256,128]{3,2,1,0:T(8,128)S(1)} %collective-permute-done.4.peer_ref, ...), custom_call_target="tpu_custom_call" | custom-call | flops 2415919104 | bytes 7356420 | tf_op jit(solution)/shard_map/pallas_call | solution.py:397
  87.9 1.9 %collective-permute-start.5 = (f32[2048,128]{1,0:T(8,128)S(1)}, f32[2048,128]{1,0:T(8,128)S(1)}, u32[]{:S(2)}, u32[]{:S(2)}) collective-permute-start(f32[2048,128]{1,0:T(8,128)S(1)} %get-tuple-element.29), channel_id=1, source_target_pairs={{0,8},{8,0},{16,24},{24,16},{32,40},{40,32},{48,56},{56,48},{64,72... | collective-permute-start | bytes 3145736 | tf_op jit(solution)/shard_map/ppermute | solution.py:445
  89.9 0.7 shard_map.89
  90.6 1.9 %collective-permute-done.5 = f32[2048,128]{1,0:T(8,128)S(1)} collective-permute-done((f32[2048,128]{1,0:T(8,128)S(1)}, f32[2048,128]{1,0:T(8,128)S(1)}, u32[]{:S(2)}, u32[]{:S(2)}) %collective-permute-start.5) | collective-permute-done | bytes 1048608 | tf_op jit(solution)/shard_map/ppermute | solution.py:445
  92.5 1.1 add.8
  93.6 9.4 %all-to-all-start.2 = ((f32[512,4,128]{2,1,0:T(4,128)}), f32[512,4,128]{2,1,0:T(4,128)S(1)}, u32[]{:S(2)}, u32[]{:S(2)}) async-start(f32[512,4,128]{2,1,0:T(4,128)} %bitcast.20), calls=%async_computation.2 | async-start | bytes 2097152 | tf_op jit(solution)/shard_map/all_to_all | solution.py:523
  103.0 0.5 shard_map.90
  103.5 32.5 %all-to-all-done.2 = f32[512,4,128]{2,1,0:T(4,128)S(1)} async-done(((f32[512,4,128]{2,1,0:T(4,128)}), f32[512,4,128]{2,1,0:T(4,128)S(1)}, u32[]{:S(2)}, u32[]{:S(2)}) %all-to-all-start.2) | async-done | bytes 1048608 | tf_op jit(solution)/shard_map/all_to_all | solution.py:523
  136.1 1.4 %shard_map.91 = f32[128,1024]{1,0:T(8,128)} custom-call(f32[2048,128]{1,0:T(8,128)S(1)} %bitcast.17, f32[128,1024]{1,0:T(8,128)S(1)} %get-tuple-element.31.gain_ref, f32[128,1024]{1,0:T(8,128)S(1)} %get-tuple-element.32.direct_ref), custom_call_target="tpu_custom_call" | custom-call | bytes 2621440 | tf_op jit(solution)/shard_map/pallas_call | solution.py:397
  (20 shorter events, 0.1 us)
Async XLA Ops:
  0.0 18.3 %copy-start.3 = (f32[128,1024]{1,0:T(8,128)S(1)}, f32[128,1024]{1,0:T(8,128)}, u32[]{:S(2)}) copy-start(f32[128,1024]{1,0:T(8,128)} %queries_ref.1) | copy-start | bytes 1572868
  0.0 18.5 %copy-start.1 = (f32[128,1024]{1,0:T(8,128)S(1)}, f32[128,1024]{1,0:T(8,128)}, u32[]{:S(2)}) copy-start(f32[128,1024]{1,0:T(8,128)} %keys_ref.1) | copy-start | bytes 1572868
  0.0 18.7 %copy-start.2 = (f32[128,1024]{1,0:T(8,128)S(1)}, f32[128,1024]{1,0:T(8,128)}, u32[]{:S(2)}) copy-start(f32[128,1024]{1,0:T(8,128)} %values_ref.1) | copy-start | bytes 1572868
  0.0 22.0 %copy-start.6 = (f32[3,3,128]{2,1,0:T(4,128)S(1)}, f32[3,3,128]{2,1,0:T(4,128)}, u32[]{:S(2)}) copy-start(f32[3,3,128]{2,1,0:T(4,128)} %param.11) | copy-start | bytes 13828
  0.0 31.2 %copy-start.7 = (f32[128]{0:T(128)S(1)}, f32[128]{0:T(128)}, u32[]{:S(2)}) copy-start(f32[128]{0:T(128)} %param.13) | copy-start | bytes 1540
  2.0 36.7 %all-to-all-start.1 = ((f32[16,64,128]{2,1,0:T(8,128)}), f32[16,64,128]{2,1,0:T(8,128)S(1)}, u32[]{:S(2)}, u32[]{:S(2)}) async-start(f32[16,64,128]{2,1,0:T(8,128)} %shard_map.83), calls=%async_computation.1 | async-start | bytes 1048576 | tf_op jit(solution)/shard_map/all_to_all | solution.py:458
  18.9 12.4 %collective-permute-start = (f32[6,128]{1,0:T(8,128)S(1)}, f32[6,128]{1,0:T(8,128)S(1)}, u32[]{:S(2)}, u32[]{:S(2)}) collective-permute-start(f32[6,128]{1,0:T(8,128)S(1)} %stack.3), channel_id=1, source_target_pairs={{0,1},{1,2},{2,3},{3,4},{4,5},{5,6},{6,7},{7,8},{8,9},{9,10},{10,1... | collective-permute-start | bytes 9224 | tf_op jit(solution)/shard_map/ppermute | solution.py:463
  38.7 24.5 %copy-start = (f32[1024,128]{1,0:T(8,128)}, f32[1024,128]{1,0:T(8,128)S(1)}, u32[]{:S(2)}) copy-start(f32[1024,128]{1,0:T(8,128)S(1)} %shard_map.84.p0) | copy-start | bytes 1572868
  38.7 20.5 %collective-permute-start.2 = (f32[1024,128]{1,0:T(8,128)S(1)}, f32[1024,128]{1,0:T(8,128)S(1)}, u32[]{:S(2)}, u32[]{:S(2)}) collective-permute-start(f32[1024,128]{1,0:T(8,128)S(1)} %shard_map.84.p0), channel_id=1, source_target_pairs={{0,16},{8,24},{16,0},{24,8},{32,48},{40,56},{48,32},{56,40},{64,80... | collective-permute-start | bytes 1572872 | tf_op jit(solution)/shard_map/ppermute | solution.py:445
  41.4 33.5 %all-to-all-start = ((f32[512,2,128]{2,1,0:T(2,128)}), f32[512,2,128]{2,1,0:T(2,128)S(1)}, u32[]{:S(2)}, u32[]{:S(2)}) async-start(f32[512,2,128]{2,1,0:T(2,128)} %bitcast.3), calls=%async_computation | async-start | bytes 1048576 | tf_op jit(solution)/shard_map/all_to_all | solution.py:469
  53.0 8.2 %collective-permute-start.1 = (f32[1024,128]{1,0:T(8,128)S(1)}, f32[1024,128]{1,0:T(8,128)S(1)}, u32[]{:S(2)}, u32[]{:S(2)}) collective-permute-start(f32[1024,128]{1,0:T(8,128)S(1)} %shard_map.84.p0), channel_id=1, source_target_pairs={{0,8},{8,0},{16,24},{24,16},{32,40},{40,32},{48,56},{56,48},{64,72... | collective-permute-start | bytes 1572872 | tf_op jit(solution)/shard_map/ppermute | solution.py:445
  59.2 4.0 %copy-start.4 = (f32[1024,128]{1,0:T(8,128)}, f32[1024,128]{1,0:T(8,128)S(1)}, u32[]{:S(2)}) copy-start(f32[1024,128]{1,0:T(8,128)S(1)} %collective-permute-done.2.p2) | copy-start | bytes 1572868
  59.2 3.9 %collective-permute-start.3 = (f32[1024,128]{1,0:T(8,128)S(1)}, f32[1024,128]{1,0:T(8,128)}, u32[]{:S(2)}, u32[]{:S(2)}) collective-permute-start(f32[1024,128]{1,0:T(8,128)S(1)} %collective-permute-done.2.p2), channel_id=1, source_target_pairs={{0,8},{8,0},{16,24},{24,16},{32,40},{40,32},{48,56},{56,48},{64,72... | collective-permute-start | bytes 1572872 | tf_op jit(solution)/shard_map/ppermute | solution.py:445
  61.2 2.0 %copy-start.5 = (f32[1024,128]{1,0:T(8,128)}, f32[1024,128]{1,0:T(8,128)S(1)}, u32[]{:S(2)}) copy-start(f32[1024,128]{1,0:T(8,128)S(1)} %collective-permute-done.1.p1) | copy-start | bytes 1572868
  76.8 5.7 %collective-permute-start.4 = (f32[2,2,256,128]{3,2,1,0:T(8,128)S(1)}, f32[2,2,256,128]{3,2,1,0:T(8,128)S(1)}, u32[]{:S(2)}, u32[]{:S(2)}) collective-permute-start(f32[2,2,256,128]{3,2,1,0:T(8,128)S(1)} %get-tuple-element.24), channel_id=1, source_target_pairs={{0,8},{8,0},{16,24},{24,16},{32,40},{40,32},{48,56},{56,48},{64,72... | collective-permute-start | bytes 1572872 | tf_op jit(solution)/shard_map/ppermute | solution.py:445
  87.9 4.6 %collective-permute-start.5 = (f32[2048,128]{1,0:T(8,128)S(1)}, f32[2048,128]{1,0:T(8,128)S(1)}, u32[]{:S(2)}, u32[]{:S(2)}) collective-permute-start(f32[2048,128]{1,0:T(8,128)S(1)} %get-tuple-element.29), channel_id=1, source_target_pairs={{0,8},{8,0},{16,24},{24,16},{32,40},{40,32},{48,56},{56,48},{64,72... | collective-permute-start | bytes 3145736 | tf_op jit(solution)/shard_map/ppermute | solution.py:445
  93.6 42.5 %all-to-all-start.2 = ((f32[512,4,128]{2,1,0:T(4,128)}), f32[512,4,128]{2,1,0:T(4,128)S(1)}, u32[]{:S(2)}, u32[]{:S(2)}) async-start(f32[512,4,128]{2,1,0:T(4,128)} %bitcast.20), calls=%async_computation.2 | async-start | bytes 2097152 | tf_op jit(solution)/shard_map/all_to_all | solution.py:523

commit v5 on v4

--- a/solution.py
+++ b/solution.py
@@ -284,26 +284,33 @@
         out_ref[r] = right_product(matrix_ref, 0, high_ref[r], low_ref[r])
 
 
-def drive_tiles(own_ref, x_ref):
+def drive_outer_kernel(
+    me_ref,
+    pages,
+    matrices,
+    own_ref,
+    spectrum,
+    mine_ref,
+    other_ref,
+    page_ref,
+    matrix_ref,
+    filter_ref,
+    mix_ref,
+    ahead_ref,
+    sem_ref,
+    x_ref,
+    high_ref,
+    low_ref,
+):
+    page = pages.at[me_ref[0]]
+    first = [(page.at[pl.ds(MIX, 2 * LANES)], mix_ref), (matrices.at[pl.ds(2, 2)], ahead_ref)]
+    loads = Loads(sem_ref, [*first, (page, page_ref), (matrices, matrix_ref), (spectrum, filter_ref)])
     for half in range(2):
         x_ref[half] = own_ref[pl.ds(half, ROWS, stride=2), :]
-
-
-def drive_other_kernel(me_ref, pages, matrices, own_ref, _, other_ref, mix_ref, ahead_ref, sem_ref, x_ref, high_ref, low_ref):
-    mix, ahead = pages.at[me_ref[0], pl.ds(MIX, 2 * LANES)], matrices.at[pl.ds(2, 2)]
-    loads = Loads(sem_ref, [(mix, mix_ref), (ahead, ahead_ref)])
-    drive_tiles(own_ref, x_ref)
     loads.wait(0, 1)
     outer_transform(x_ref, 2, 1, mix_ref, 0, ahead_ref, 0, other_ref, high_ref, low_ref)
-
-
-def drive_mine_kernel(
-    me_ref, pages, matrices, own_ref, mix_ref, ahead_ref, mine_ref, page_ref, matrix_ref, sem_ref, x_ref, high_ref, low_ref
-):
-    loads = Loads(sem_ref, [(pages.at[me_ref[0]], page_ref), (matrices, matrix_ref)])
-    drive_tiles(own_ref, x_ref)
     outer_transform(x_ref, 2, 0, mix_ref, 0, ahead_ref, 0, mine_ref, high_ref, low_ref)
-    loads.wait(0, 1)
+    loads.wait(2, 3, 4)
 
 
 def product_kernel(
@@ -312,24 +319,20 @@
     peer_ref,
     page_ref,
     matrix_ref,
-    spectrum,
+    filter_ref,
     other_ref,
     left_high_ref,
     left_low_ref,
-    sem_ref,
-    filter_ref,
     f_ref,
     d_ref,
     high_ref,
     low_ref,
 ):
     core = me_ref[0] & 1
-    loads = Loads(sem_ref, [(spectrum, filter_ref)])
     for which, piece_ref in ((core, own_ref), (1 - core, peer_ref)):
         for half in range(2):
             f_ref[2 * which + half] = piece_ref[half]
     inner_transform(f_ref, 4, 0, 16, page_ref, high_ref, low_ref)
-    loads.wait(0)
     for r in range(TILES):
         x, h = right_product(matrix_ref, 0, high_ref[r], low_ref[r]), filter_ref[r]
         value = times((x[:, :LANES], x[:, LANES:]), (h[:, :LANES], h[:, LANES:]))
@@ -486,34 +489,23 @@
         FILTER_FLOPS,
         VMEM_ALL,
     )
-    half, mix, ahead = shape(2, 2, Q, LANES), shape(2 * LANES, LANES), jax.ShapeDtypeStruct((2, Q, Q), BF)
-    spectrum = stay(spectrum)
-    other, mix, ahead = call(
-        drive_other_kernel,
-        [half, mix, ahead],
-        (me, pages, matrices, own, spectrum),
+    mine, other, *loaded = call(
+        drive_outer_kernel,
+        [shape(2, 2, Q, LANES), shape(2, 2, Q, LANES), page, table, shape(TILES, Q, Q)],
+        (me, pages, matrices, own, stay(spectrum)),
         [HBM, HBM, whole(own), HBM],
-        [sems(2), f32(2, ROWS, LANES)] + work(2),
+        [f32(2 * LANES, LANES), pltpu.VMEM((2, Q, Q), BF), sems(5), f32(2, ROWS, LANES)] + work(2),
         1,
-        flops // 2,
+        flops,
     )
-    mine, page, table = call(
-        drive_mine_kernel,
-        [half, page, table],
-        (me, pages, matrices, own, mix, ahead),
-        [HBM, HBM, whole(own), whole(mix), whole(ahead)],
-        [sems(2), f32(2, ROWS, LANES)] + work(2),
-        1,
-        flops // 2,
-    )
-    peer = across(other, 1)
     left = jax.ShapeDtypeStruct((4, Q, Q), BF)
+    page, table, _ = loaded
     other, *left = call(
         product_kernel,
         [shape(4 * ROWS, LANES), left, left],
-        (me, mine, peer, page, table, spectrum),
-        [whole(mine), whole(peer), whole(page), whole(table), HBM],
-        [sems(1), f32(TILES, Q, Q), f32(4, 2, Q, LANES), f32(TILES, Q, Q)] + work(TILES),
+        (me, mine, across(other, 1), *loaded),
+        None,
+        [f32(4, 2, Q, LANES), f32(TILES, Q, Q)] + work(TILES),
         1,
         3 * flops,
     )

time: 138 us -> 137 us (level)
  Pallas kernels: 23.2 us -> 21.2 us
    pallas_call x9 -> x8, Pallas kernels: 23.2 us -> 21.2 us  [call(): pl.pallas_call(kernel, out_shape=out_shapes[0] if single else out_shapes,...]
  transfers between devices with their start and end apart: 9 -> 9, of which waited for: 6 -> 7; matrix products, arithmetic and copies ran while one was open for 0% -> 0% of each run, Pallas kernels for 9% -> 8%
where the time goes in v5:
time: 137 us
  starting transfers between devices  57.2 us (42%)
  waiting for transfers between devices  56.4 us (41%)
  Pallas kernels  21.2 us (15%)
    all_to_all x1, waiting for transfers between devices, local(): lax.all_to_all(result.reshape(size, -1, LANES), everyone, 0, 0, tiled=True)  32.5 us
    pallas_call x8, Pallas kernels, call(): pl.pallas_call(kernel, out_shape=out_shapes[0] if single else out_shapes,...  21.2 us
    ppermute x5, starting transfers between devices, across(): return lax.ppermute(rows, 'seq', [(i, i ^ mask) for i in range(size)])  16.7 us
    all_to_all x1, starting transfers between devices, local(): lax.all_to_all(filter_rows, 'seq', 0, 0, tiled=True, axis_index_groups=al...  16.2 us
    all_to_all x1, starting transfers between devices, local(): lax.all_to_all(packed.reshape(size, -1, LANES), everyone, 0, 0, tiled=True)  11.6 us
    all_to_all x1, starting transfers between devices, local(): lax.all_to_all(result.reshape(size, -1, LANES), everyone, 0, 0, tiled=True)  9.5 us
    ppermute x1, waiting for transfers between devices, local(): lax.ppermute(edges, everyone, [(i, i + 1) for i in range(size - 1)])  9.23 us
    all_to_all x1, waiting for transfers between devices, local(): lax.all_to_all(filter_rows, 'seq', 0, 0, tiled=True, axis_index_groups=al...  5.3 us
  transfers between devices with their start and end apart: 9, of which 7 were waited for; matrix products, arithmetic and copies ran while one was open for 0% of the time, Pallas kernels for 8%

profile of v5, /device:TPU:1, one launch (start us, length us, event | category | flops | bytes accessed | tf_op | source)
XLA Modules:
  0.0 136.8 jit_solution(10277711430927047634)
XLA Ops:
  0.0 2.0 %shard_map.83 = f32[16,64,128]{2,1,0:T(8,128)} custom-call(f32[16,8192]{1,0:T(8,128)} %filter_rows.1), custom_call_target="tpu_custom_call" | custom-call | bytes 1048576 | tf_op jit(solution)/shard_map/pallas_call | solution.py:400
  2.1 16.2 %all-to-all-start.1 = ((f32[16,64,128]{2,1,0:T(8,128)}), f32[16,64,128]{2,1,0:T(8,128)S(1)}, u32[]{:S(2)}, u32[]{:S(2)}) async-start(f32[16,64,128]{2,1,0:T(8,128)} %shard_map.83), calls=%async_computation.1 | async-start | bytes 1048576 | tf_op jit(solution)/shard_map/all_to_all | solution.py:461
  18.3 0.0 copy-done.1
  18.3 0.2 slice_reduce_fusion.2
  18.5 0.2 slice_reduce_fusion
  18.7 0.2 slice_reduce_fusion.4
  18.9 3.1 %collective-permute-start = (f32[6,128]{1,0:T(8,128)S(1)}, f32[6,128]{1,0:T(8,128)S(1)}, u32[]{:S(2)}, u32[]{:S(2)}) collective-permute-start(f32[6,128]{1,0:T(8,128)S(1)} %stack.3), channel_id=1, source_target_pairs={{0,1},{1,2},{2,3},{3,4},{4,5},{5,6},{6,7},{7,8},{8,9},{9,10},{10,1... | collective-permute-start | bytes 9224 | tf_op jit(solution)/shard_map/ppermute | solution.py:466
  22.1 9.2 %collective-permute-done = f32[6,128]{1,0:T(8,128)S(1)} collective-permute-done((f32[6,128]{1,0:T(8,128)S(1)}, f32[6,128]{1,0:T(8,128)S(1)}, u32[]{:S(2)}, u32[]{:S(2)}) %collective-permute-start) | collective-permute-done | bytes 3104 | tf_op jit(solution)/shard_map/ppermute | solution.py:466
  31.3 0.1 copy.26
  31.4 2.0 %shard_map.82 = (f32[1024,128]{1,0:T(8,128)}, f32[128,1024]{1,0:T(8,128)S(1)}, f32[8,16]{1,0:T(8,128)S(1)}) custom-call(f32[128,1024]{1,0:T(8,128)S(1)} %copy-done.1, f32[128,1024]{1,0:T(8,128)S(1)} %copy-done.2, f32[128,16]{1,0:T(8,128)S(1)} %bitcast.17), custom_call_target="tpu_custom_call" | custom-call | bytes 2105856 | tf_op jit(solution)/shard_map/pallas_call | solution.py:400
  33.4 5.3 %all-to-all-done.1 = f32[16,64,128]{2,1,0:T(8,128)S(1)} async-done(((f32[16,64,128]{2,1,0:T(8,128)}), f32[16,64,128]{2,1,0:T(8,128)S(1)}, u32[]{:S(2)}, u32[]{:S(2)}) %all-to-all-start.1) | async-done | bytes 524320 | tf_op jit(solution)/shard_map/all_to_all | solution.py:461
  38.7 2.6 %collective-permute-start.2 = (f32[1024,128]{1,0:T(8,128)S(1)}, f32[1024,128]{1,0:T(8,128)S(1)}, u32[]{:S(2)}, u32[]{:S(2)}) collective-permute-start(f32[1024,128]{1,0:T(8,128)S(1)} %shard_map.84.p0), channel_id=1, source_target_pairs={{0,16},{8,24},{16,0},{24,8},{32,48},{40,56},{48,32},{56,40},{64,80... | collective-permute-start | bytes 1572872 | tf_op jit(solution)/shard_map/ppermute | solution.py:448
  41.4 11.6 %all-to-all-start = ((f32[512,2,128]{2,1,0:T(2,128)}), f32[512,2,128]{2,1,0:T(2,128)S(1)}, u32[]{:S(2)}, u32[]{:S(2)}) async-start(f32[512,2,128]{2,1,0:T(2,128)} %bitcast.3), calls=%async_computation | async-start | bytes 1048576 | tf_op jit(solution)/shard_map/all_to_all | solution.py:472
  53.0 6.2 %collective-permute-start.1 = (f32[1024,128]{1,0:T(8,128)S(1)}, f32[1024,128]{1,0:T(8,128)S(1)}, u32[]{:S(2)}, u32[]{:S(2)}) collective-permute-start(f32[1024,128]{1,0:T(8,128)S(1)} %shard_map.84.p0), channel_id=1, source_target_pairs={{0,8},{8,0},{16,24},{24,16},{32,40},{40,32},{48,56},{56,48},{64,72... | collective-permute-start | bytes 1572872 | tf_op jit(solution)/shard_map/ppermute | solution.py:448
  59.2 0.0 collective-permute-done.2.p2
  59.3 1.9 %collective-permute-start.3 = (f32[1024,128]{1,0:T(8,128)S(1)}, f32[1024,128]{1,0:T(8,128)}, u32[]{:S(2)}, u32[]{:S(2)}) collective-permute-start(f32[1024,128]{1,0:T(8,128)S(1)} %collective-permute-done.2.p2), channel_id=1, source_target_pairs={{0,8},{8,0},{16,24},{24,16},{32,40},{40,32},{48,56},{56,48},{64,72... | collective-permute-start | bytes 1572872 | tf_op jit(solution)/shard_map/ppermute | solution.py:448
  61.2 0.0 collective-permute-done.1.p1
  61.2 2.0 %collective-permute-done.3.p3 = f32[1024,128]{1,0:T(8,128)} collective-permute-done((f32[1024,128]{1,0:T(8,128)S(1)}, f32[1024,128]{1,0:T(8,128)}, u32[]{:S(2)}, u32[]{:S(2)}) %collective-permute-start.3) | collective-permute-done | bytes 524320 | tf_op jit(solution)/shard_map/ppermute | solution.py:448
  63.2 7.2 %shard_map.85.spectrum = f32[8,256,256]{2,1,0:T(8,128)} custom-call(s32[1]{0:T(128)} %bitcast.me_ref, f32[4,1056,128]{2,1,0:T(8,128)} %constant.24.clone.pages, bf16[4,256,256]{2,1,0:T(8,128)(2,1)} %constant.23.clone.matrices, f32[1024,128]{1,0:T(8,128)} %copy-done, f32[1024,128]{1,0:T(8,128)} %copy-done.5, f32[1024,128]{1,0:T(8,128)} %copy-done.4, ...), custom_call_target="tpu_custom_call" | custom-call | flops 1610612736 | bytes 6881284 | tf_op jit(solution)/shard_map/pallas_call | solution.py:400
  70.5 4.4 %all-to-all-done = f32[512,2,128]{2,1,0:T(2,128)S(1)} async-done(((f32[512,2,128]{2,1,0:T(2,128)}), f32[512,2,128]{2,1,0:T(2,128)S(1)}, u32[]{:S(2)}, u32[]{:S(2)}) %all-to-all-start) | async-done | bytes 524320 | tf_op jit(solution)/shard_map/all_to_all | solution.py:472
  74.9 2.4 %shard_map.86 = (f32[2,2,256,128]{3,2,1,0:T(8,128)S(1)}, f32[2,2,256,128]{3,2,1,0:T(8,128)S(1)}, f32[1056,128]{1,0:T(8,128)S(1)}, bf16[4,256,256]{2,1,0:T(8,128)(2,1)S(1)}, f32[8,256,256]{2,1,0:T(8,128)S(1)}) custom-call(s32[1]{0:T(128)} %bitcast.me_ref, f32[4,1056,128]{2,1,0:T(8,128)} %constant.24.clone.pages, ...), custom_call_target="tpu_custom_call" | custom-call | flops 805306368 | bytes 10043396 | tf_op jit(solution)/shard_map/pallas_call | solution.py:400
  77.3 3.7 %collective-permute-start.4 = (f32[2,2,256,128]{3,2,1,0:T(8,128)S(1)}, f32[2,2,256,128]{3,2,1,0:T(8,128)S(1)}, u32[]{:S(2)}, u32[]{:S(2)}) collective-permute-start(f32[2,2,256,128]{3,2,1,0:T(8,128)S(1)} %get-tuple-element.21), channel_id=1, source_target_pairs={{0,8},{8,0},{16,24},{24,16},{32,40},{40,32},{48,56},{56,48},{64,72... | collective-permute-start | bytes 1572872 | tf_op jit(solution)/shard_map/ppermute | solution.py:448
  81.1 1.3 collective-permute-done.4.peer_ref
  82.4 4.8 %shard_map.87 = (f32[2048,128]{1,0:T(8,128)S(1)}, bf16[4,256,256]{2,1,0:T(8,128)(2,1)S(1)}, bf16[4,256,256]{2,1,0:T(8,128)(2,1)S(1)}) custom-call(s32[1]{0:T(128)} %bitcast.me_ref, f32[2,2,256,128]{3,2,1,0:T(8,128)S(1)} %get-tuple-element.20.own_ref, f32[2,2,256,128]{3,2,1,0:T(8,128)S(1)} %collective-permute-done.4.peer_ref, ...), custom_call_target="tpu_custom_call" | custom-call | flops 2415919104 | bytes 7356420 | tf_op jit(solution)/shard_map/pallas_call | solution.py:400
  87.2 2.2 %collective-permute-start.5 = (f32[2048,128]{1,0:T(8,128)S(1)}, f32[2048,128]{1,0:T(8,128)S(1)}, u32[]{:S(2)}, u32[]{:S(2)}) collective-permute-start(f32[2048,128]{1,0:T(8,128)S(1)} %get-tuple-element.27), channel_id=1, source_target_pairs={{0,8},{8,0},{16,24},{24,16},{32,40},{40,32},{48,56},{56,48},{64,72... | collective-permute-start | bytes 3145736 | tf_op jit(solution)/shard_map/ppermute | solution.py:448
  89.5 0.7 shard_map.88
  90.2 1.6 %collective-permute-done.5 = f32[2048,128]{1,0:T(8,128)S(1)} collective-permute-done((f32[2048,128]{1,0:T(8,128)S(1)}, f32[2048,128]{1,0:T(8,128)S(1)}, u32[]{:S(2)}, u32[]{:S(2)}) %collective-permute-start.5) | collective-permute-done | bytes 1048608 | tf_op jit(solution)/shard_map/ppermute | solution.py:448
  91.8 1.1 add.8
  92.9 9.5 %all-to-all-start.2 = ((f32[512,4,128]{2,1,0:T(4,128)}), f32[512,4,128]{2,1,0:T(4,128)S(1)}, u32[]{:S(2)}, u32[]{:S(2)}) async-start(f32[512,4,128]{2,1,0:T(4,128)} %bitcast.19), calls=%async_computation.2 | async-start | bytes 2097152 | tf_op jit(solution)/shard_map/all_to_all | solution.py:515
  102.4 0.5 shard_map.89
  102.9 32.5 %all-to-all-done.2 = f32[512,4,128]{2,1,0:T(4,128)S(1)} async-done(((f32[512,4,128]{2,1,0:T(4,128)}), f32[512,4,128]{2,1,0:T(4,128)S(1)}, u32[]{:S(2)}, u32[]{:S(2)}) %all-to-all-start.2) | async-done | bytes 1048608 | tf_op jit(solution)/shard_map/all_to_all | solution.py:515
  135.4 1.4 %shard_map.90 = f32[128,1024]{1,0:T(8,128)} custom-call(f32[2048,128]{1,0:T(8,128)S(1)} %bitcast.15, f32[128,1024]{1,0:T(8,128)S(1)} %get-tuple-element.29.gain_ref, f32[128,1024]{1,0:T(8,128)S(1)} %get-tuple-element.30.direct_ref), custom_call_target="tpu_custom_call" | custom-call | bytes 2621440 | tf_op jit(solution)/shard_map/pallas_call | solution.py:400
  (19 shorter events, 0.1 us)
Async XLA Ops:
  0.0 18.3 %copy-start.1 = (f32[128,1024]{1,0:T(8,128)S(1)}, f32[128,1024]{1,0:T(8,128)}, u32[]{:S(2)}) copy-start(f32[128,1024]{1,0:T(8,128)} %keys_ref.1) | copy-start | bytes 1572868
  0.0 18.5 %copy-start.2 = (f32[128,1024]{1,0:T(8,128)S(1)}, f32[128,1024]{1,0:T(8,128)}, u32[]{:S(2)}) copy-start(f32[128,1024]{1,0:T(8,128)} %values_ref.1) | copy-start | bytes 1572868
  0.0 18.7 %copy-start.3 = (f32[128,1024]{1,0:T(8,128)S(1)}, f32[128,1024]{1,0:T(8,128)}, u32[]{:S(2)}) copy-start(f32[128,1024]{1,0:T(8,128)} %queries_ref.1) | copy-start | bytes 1572868
  0.0 22.0 %copy-start.6 = (f32[3,3,128]{2,1,0:T(4,128)S(1)}, f32[3,3,128]{2,1,0:T(4,128)}, u32[]{:S(2)}) copy-start(f32[3,3,128]{2,1,0:T(4,128)} %param.11) | copy-start | bytes 13828
  0.0 31.3 %copy-start.7 = (f32[128]{0:T(128)S(1)}, f32[128]{0:T(128)}, u32[]{:S(2)}) copy-start(f32[128]{0:T(128)} %param.13) | copy-start | bytes 1540
  2.1 36.7 %all-to-all-start.1 = ((f32[16,64,128]{2,1,0:T(8,128)}), f32[16,64,128]{2,1,0:T(8,128)S(1)}, u32[]{:S(2)}, u32[]{:S(2)}) async-start(f32[16,64,128]{2,1,0:T(8,128)} %shard_map.83), calls=%async_computation.1 | async-start | bytes 1048576 | tf_op jit(solution)/shard_map/all_to_all | solution.py:461
  18.9 12.4 %collective-permute-start = (f32[6,128]{1,0:T(8,128)S(1)}, f32[6,128]{1,0:T(8,128)S(1)}, u32[]{:S(2)}, u32[]{:S(2)}) collective-permute-start(f32[6,128]{1,0:T(8,128)S(1)} %stack.3), channel_id=1, source_target_pairs={{0,1},{1,2},{2,3},{3,4},{4,5},{5,6},{6,7},{7,8},{8,9},{9,10},{10,1... | collective-permute-start | bytes 9224 | tf_op jit(solution)/shard_map/ppermute | solution.py:466
  38.7 24.5 %copy-start = (f32[1024,128]{1,0:T(8,128)}, f32[1024,128]{1,0:T(8,128)S(1)}, u32[]{:S(2)}) copy-start(f32[1024,128]{1,0:T(8,128)S(1)} %shard_map.84.p0) | copy-start | bytes 1572868
  38.7 20.5 %collective-permute-start.2 = (f32[1024,128]{1,0:T(8,128)S(1)}, f32[1024,128]{1,0:T(8,128)S(1)}, u32[]{:S(2)}, u32[]{:S(2)}) collective-permute-start(f32[1024,128]{1,0:T(8,128)S(1)} %shard_map.84.p0), channel_id=1, source_target_pairs={{0,16},{8,24},{16,0},{24,8},{32,48},{40,56},{48,32},{56,40},{64,80... | collective-permute-start | bytes 1572872 | tf_op jit(solution)/shard_map/ppermute | solution.py:448
  41.4 33.5 %all-to-all-start = ((f32[512,2,128]{2,1,0:T(2,128)}), f32[512,2,128]{2,1,0:T(2,128)S(1)}, u32[]{:S(2)}, u32[]{:S(2)}) async-start(f32[512,2,128]{2,1,0:T(2,128)} %bitcast.3), calls=%async_computation | async-start | bytes 1048576 | tf_op jit(solution)/shard_map/all_to_all | solution.py:472
  53.0 8.2 %collective-permute-start.1 = (f32[1024,128]{1,0:T(8,128)S(1)}, f32[1024,128]{1,0:T(8,128)S(1)}, u32[]{:S(2)}, u32[]{:S(2)}) collective-permute-start(f32[1024,128]{1,0:T(8,128)S(1)} %shard_map.84.p0), channel_id=1, source_target_pairs={{0,8},{8,0},{16,24},{24,16},{32,40},{40,32},{48,56},{56,48},{64,72... | collective-permute-start | bytes 1572872 | tf_op jit(solution)/shard_map/ppermute | solution.py:448
  59.2 4.0 %copy-start.4 = (f32[1024,128]{1,0:T(8,128)}, f32[1024,128]{1,0:T(8,128)S(1)}, u32[]{:S(2)}) copy-start(f32[1024,128]{1,0:T(8,128)S(1)} %collective-permute-done.2.p2) | copy-start | bytes 1572868
  59.3 3.9 %collective-permute-start.3 = (f32[1024,128]{1,0:T(8,128)S(1)}, f32[1024,128]{1,0:T(8,128)}, u32[]{:S(2)}, u32[]{:S(2)}) collective-permute-start(f32[1024,128]{1,0:T(8,128)S(1)} %collective-permute-done.2.p2), channel_id=1, source_target_pairs={{0,8},{8,0},{16,24},{24,16},{32,40},{40,32},{48,56},{56,48},{64,72... | collective-permute-start | bytes 1572872 | tf_op jit(solution)/shard_map/ppermute | solution.py:448
  61.2 2.0 %copy-start.5 = (f32[1024,128]{1,0:T(8,128)}, f32[1024,128]{1,0:T(8,128)S(1)}, u32[]{:S(2)}) copy-start(f32[1024,128]{1,0:T(8,128)S(1)} %collective-permute-done.1.p1) | copy-start | bytes 1572868
  77.3 5.1 %collective-permute-start.4 = (f32[2,2,256,128]{3,2,1,0:T(8,128)S(1)}, f32[2,2,256,128]{3,2,1,0:T(8,128)S(1)}, u32[]{:S(2)}, u32[]{:S(2)}) collective-permute-start(f32[2,2,256,128]{3,2,1,0:T(8,128)S(1)} %get-tuple-element.21), channel_id=1, source_target_pairs={{0,8},{8,0},{16,24},{24,16},{32,40},{40,32},{48,56},{56,48},{64,72... | collective-permute-start | bytes 1572872 | tf_op jit(solution)/shard_map/ppermute | solution.py:448
  87.2 4.6 %collective-permute-start.5 = (f32[2048,128]{1,0:T(8,128)S(1)}, f32[2048,128]{1,0:T(8,128)S(1)}, u32[]{:S(2)}, u32[]{:S(2)}) collective-permute-start(f32[2048,128]{1,0:T(8,128)S(1)} %get-tuple-element.27), channel_id=1, source_target_pairs={{0,8},{8,0},{16,24},{24,16},{32,40},{40,32},{48,56},{56,48},{64,72... | collective-permute-start | bytes 3145736 | tf_op jit(solution)/shard_map/ppermute | solution.py:448
  92.9 42.6 %all-to-all-start.2 = ((f32[512,4,128]{2,1,0:T(4,128)}), f32[512,4,128]{2,1,0:T(4,128)S(1)}, u32[]{:S(2)}, u32[]{:S(2)}) async-start(f32[512,4,128]{2,1,0:T(4,128)} %bitcast.19), calls=%async_computation.2 | async-start | bytes 2097152 | tf_op jit(solution)/shard_map/all_to_all | solution.py:515

commit v6 on v5

--- a/solution.py
+++ b/solution.py
@@ -304,13 +304,14 @@
 ):
     page = pages.at[me_ref[0]]
     first = [(page.at[pl.ds(MIX, 2 * LANES)], mix_ref), (matrices.at[pl.ds(2, 2)], ahead_ref)]
-    loads = Loads(sem_ref, [*first, (page, page_ref), (matrices, matrix_ref), (spectrum, filter_ref)])
+    tables_here = Loads(sem_ref.at[pl.ds(0, 2)], first)
     for half in range(2):
         x_ref[half] = own_ref[pl.ds(half, ROWS, stride=2), :]
-    loads.wait(0, 1)
+    tables_here.wait(0, 1)
+    loads = Loads(sem_ref.at[pl.ds(2, 3)], [(page, page_ref), (matrices, matrix_ref), (spectrum, filter_ref)])
     outer_transform(x_ref, 2, 1, mix_ref, 0, ahead_ref, 0, other_ref, high_ref, low_ref)
     outer_transform(x_ref, 2, 0, mix_ref, 0, ahead_ref, 0, mine_ref, high_ref, low_ref)
-    loads.wait(2, 3, 4)
+    loads.wait(0, 1, 2)
 
 
 def product_kernel(

time: 137 us -> 138 us (level)
  no operation moved by 1% of the time
where the time goes in v6:
time: 138 us; the launch traced here: 137 us
  starting transfers between devices  57.2 us (41%)
  waiting for transfers between devices  56.4 us (41%)
  Pallas kernels  21.8 us (16%)
    all_to_all x1, waiting for transfers between devices, local(): lax.all_to_all(result.reshape(size, -1, LANES), everyone, 0, 0, tiled=True)  32.5 us
    pallas_call x8, Pallas kernels, call(): pl.pallas_call(kernel, out_shape=out_shapes[0] if single else out_shapes,...  21.8 us
    ppermute x5, starting transfers between devices, across(): return lax.ppermute(rows, 'seq', [(i, i ^ mask) for i in range(size)])  16.7 us
    all_to_all x1, starting transfers between devices, local(): lax.all_to_all(filter_rows, 'seq', 0, 0, tiled=True, axis_index_groups=al...  16.2 us
    all_to_all x1, starting transfers between devices, local(): lax.all_to_all(packed.reshape(size, -1, LANES), everyone, 0, 0, tiled=True)  11.6 us
    all_to_all x1, starting transfers between devices, local(): lax.all_to_all(result.reshape(size, -1, LANES), everyone, 0, 0, tiled=True)  9.5 us
    ppermute x1, waiting for transfers between devices, local(): lax.ppermute(edges, everyone, [(i, i + 1) for i in range(size - 1)])  9.23 us
    all_to_all x1, waiting for transfers between devices, local(): lax.all_to_all(filter_rows, 'seq', 0, 0, tiled=True, axis_index_groups=al...  5.3 us
  transfers between devices with their start and end apart: 9, of which 7 were waited for; matrix products, arithmetic and copies ran while one was open for 0% of the time, Pallas kernels for 8%

profile of v6, /device:TPU:1, one launch (start us, length us, event | category | flops | bytes accessed | tf_op | source)
XLA Modules:
  0.0 137.4 jit_solution(1257205562581845606)
XLA Ops:
  0.0 2.0 %shard_map.83 = f32[16,64,128]{2,1,0:T(8,128)} custom-call(f32[16,8192]{1,0:T(8,128)} %filter_rows.1), custom_call_target="tpu_custom_call" | custom-call | bytes 1048576 | tf_op jit(solution)/shard_map/pallas_call | solution.py:401
  2.1 16.2 %all-to-all-start.1 = ((f32[16,64,128]{2,1,0:T(8,128)}), f32[16,64,128]{2,1,0:T(8,128)S(1)}, u32[]{:S(2)}, u32[]{:S(2)}) async-start(f32[16,64,128]{2,1,0:T(8,128)} %shard_map.83), calls=%async_computation.1 | async-start | bytes 1048576 | tf_op jit(solution)/shard_map/all_to_all | solution.py:462
  18.3 0.0 copy-done.1
  18.3 0.2 slice_reduce_fusion.2
  18.5 0.2 slice_reduce_fusion
  18.7 0.2 slice_reduce_fusion.4
  18.9 3.1 %collective-permute-start = (f32[6,128]{1,0:T(8,128)S(1)}, f32[6,128]{1,0:T(8,128)S(1)}, u32[]{:S(2)}, u32[]{:S(2)}) collective-permute-start(f32[6,128]{1,0:T(8,128)S(1)} %stack.3), channel_id=1, source_target_pairs={{0,1},{1,2},{2,3},{3,4},{4,5},{5,6},{6,7},{7,8},{8,9},{9,10},{10,1... | collective-permute-start | bytes 9224 | tf_op jit(solution)/shard_map/ppermute | solution.py:467
  22.1 9.2 %collective-permute-done = f32[6,128]{1,0:T(8,128)S(1)} collective-permute-done((f32[6,128]{1,0:T(8,128)S(1)}, f32[6,128]{1,0:T(8,128)S(1)}, u32[]{:S(2)}, u32[]{:S(2)}) %collective-permute-start) | collective-permute-done | bytes 3104 | tf_op jit(solution)/shard_map/ppermute | solution.py:467
  31.3 0.1 copy.26
  31.4 2.0 %shard_map.82 = (f32[1024,128]{1,0:T(8,128)}, f32[128,1024]{1,0:T(8,128)S(1)}, f32[8,16]{1,0:T(8,128)S(1)}) custom-call(f32[128,1024]{1,0:T(8,128)S(1)} %copy-done.1, f32[128,1024]{1,0:T(8,128)S(1)} %copy-done.2, f32[128,16]{1,0:T(8,128)S(1)} %bitcast.17), custom_call_target="tpu_custom_call" | custom-call | bytes 2105856 | tf_op jit(solution)/shard_map/pallas_call | solution.py:401
  33.4 5.3 %all-to-all-done.1 = f32[16,64,128]{2,1,0:T(8,128)S(1)} async-done(((f32[16,64,128]{2,1,0:T(8,128)}), f32[16,64,128]{2,1,0:T(8,128)S(1)}, u32[]{:S(2)}, u32[]{:S(2)}) %all-to-all-start.1) | async-done | bytes 524320 | tf_op jit(solution)/shard_map/all_to_all | solution.py:462
  38.7 2.6 %collective-permute-start.2 = (f32[1024,128]{1,0:T(8,128)S(1)}, f32[1024,128]{1,0:T(8,128)S(1)}, u32[]{:S(2)}, u32[]{:S(2)}) collective-permute-start(f32[1024,128]{1,0:T(8,128)S(1)} %shard_map.84.p0), channel_id=1, source_target_pairs={{0,16},{8,24},{16,0},{24,8},{32,48},{40,56},{48,32},{56,40},{64,80... | collective-permute-start | bytes 1572872 | tf_op jit(solution)/shard_map/ppermute | solution.py:449
  41.4 11.6 %all-to-all-start = ((f32[512,2,128]{2,1,0:T(2,128)}), f32[512,2,128]{2,1,0:T(2,128)S(1)}, u32[]{:S(2)}, u32[]{:S(2)}) async-start(f32[512,2,128]{2,1,0:T(2,128)} %bitcast.3), calls=%async_computation | async-start | bytes 1048576 | tf_op jit(solution)/shard_map/all_to_all | solution.py:473
  53.0 6.2 %collective-permute-start.1 = (f32[1024,128]{1,0:T(8,128)S(1)}, f32[1024,128]{1,0:T(8,128)S(1)}, u32[]{:S(2)}, u32[]{:S(2)}) collective-permute-start(f32[1024,128]{1,0:T(8,128)S(1)} %shard_map.84.p0), channel_id=1, source_target_pairs={{0,8},{8,0},{16,24},{24,16},{32,40},{40,32},{48,56},{56,48},{64,72... | collective-permute-start | bytes 1572872 | tf_op jit(solution)/shard_map/ppermute | solution.py:449
  59.2 0.0 collective-permute-done.2.p2
  59.3 1.9 %collective-permute-start.3 = (f32[1024,128]{1,0:T(8,128)S(1)}, f32[1024,128]{1,0:T(8,128)}, u32[]{:S(2)}, u32[]{:S(2)}) collective-permute-start(f32[1024,128]{1,0:T(8,128)S(1)} %collective-permute-done.2.p2), channel_id=1, source_target_pairs={{0,8},{8,0},{16,24},{24,16},{32,40},{40,32},{48,56},{56,48},{64,72... | collective-permute-start | bytes 1572872 | tf_op jit(solution)/shard_map/ppermute | solution.py:449
  61.2 0.0 collective-permute-done.1.p1
  61.2 2.0 %collective-permute-done.3.p3 = f32[1024,128]{1,0:T(8,128)} collective-permute-done((f32[1024,128]{1,0:T(8,128)S(1)}, f32[1024,128]{1,0:T(8,128)}, u32[]{:S(2)}, u32[]{:S(2)}) %collective-permute-start.3) | collective-permute-done | bytes 524320 | tf_op jit(solution)/shard_map/ppermute | solution.py:449
  63.2 7.2 %shard_map.85.spectrum = f32[8,256,256]{2,1,0:T(8,128)} custom-call(s32[1]{0:T(128)} %bitcast.me_ref, f32[4,1056,128]{2,1,0:T(8,128)} %constant.24.clone.pages, bf16[4,256,256]{2,1,0:T(8,128)(2,1)} %constant.23.clone.matrices, f32[1024,128]{1,0:T(8,128)} %copy-done, f32[1024,128]{1,0:T(8,128)} %copy-done.5, f32[1024,128]{1,0:T(8,128)} %copy-done.4, ...), custom_call_target="tpu_custom_call" | custom-call | flops 1610612736 | bytes 6881284 | tf_op jit(solution)/shard_map/pallas_call | solution.py:401
  70.5 4.4 %all-to-all-done = f32[512,2,128]{2,1,0:T(2,128)S(1)} async-done(((f32[512,2,128]{2,1,0:T(2,128)}), f32[512,2,128]{2,1,0:T(2,128)S(1)}, u32[]{:S(2)}, u32[]{:S(2)}) %all-to-all-start) | async-done | bytes 524320 | tf_op jit(solution)/shard_map/all_to_all | solution.py:473
  74.9 3.0 %shard_map.86 = (f32[2,2,256,128]{3,2,1,0:T(8,128)S(1)}, f32[2,2,256,128]{3,2,1,0:T(8,128)S(1)}, f32[1056,128]{1,0:T(8,128)S(1)}, bf16[4,256,256]{2,1,0:T(8,128)(2,1)S(1)}, f32[8,256,256]{2,1,0:T(8,128)S(1)}) custom-call(s32[1]{0:T(128)} %bitcast.me_ref, f32[4,1056,128]{2,1,0:T(8,128)} %constant.24.clone.pages, ...), custom_call_target="tpu_custom_call" | custom-call | flops 805306368 | bytes 10043396 | tf_op jit(solution)/shard_map/pallas_call | solution.py:401
  77.9 3.7 %collective-permute-start.4 = (f32[2,2,256,128]{3,2,1,0:T(8,128)S(1)}, f32[2,2,256,128]{3,2,1,0:T(8,128)S(1)}, u32[]{:S(2)}, u32[]{:S(2)}) collective-permute-start(f32[2,2,256,128]{3,2,1,0:T(8,128)S(1)} %get-tuple-element.21), channel_id=1, source_target_pairs={{0,8},{8,0},{16,24},{24,16},{32,40},{40,32},{48,56},{56,48},{64,72... | collective-permute-start | bytes 1572872 | tf_op jit(solution)/shard_map/ppermute | solution.py:449
  81.6 1.3 collective-permute-done.4.peer_ref
  83.0 4.8 %shard_map.87 = (f32[2048,128]{1,0:T(8,128)S(1)}, bf16[4,256,256]{2,1,0:T(8,128)(2,1)S(1)}, bf16[4,256,256]{2,1,0:T(8,128)(2,1)S(1)}) custom-call(s32[1]{0:T(128)} %bitcast.me_ref, f32[2,2,256,128]{3,2,1,0:T(8,128)S(1)} %get-tuple-element.20.own_ref, f32[2,2,256,128]{3,2,1,0:T(8,128)S(1)} %collective-permute-done.4.peer_ref, ...), custom_call_target="tpu_custom_call" | custom-call | flops 2415919104 | bytes 7356420 | tf_op jit(solution)/shard_map/pallas_call | solution.py:401
  87.8 2.2 %collective-permute-start.5 = (f32[2048,128]{1,0:T(8,128)S(1)}, f32[2048,128]{1,0:T(8,128)S(1)}, u32[]{:S(2)}, u32[]{:S(2)}) collective-permute-start(f32[2048,128]{1,0:T(8,128)S(1)} %get-tuple-element.27), channel_id=1, source_target_pairs={{0,8},{8,0},{16,24},{24,16},{32,40},{40,32},{48,56},{56,48},{64,72... | collective-permute-start | bytes 3145736 | tf_op jit(solution)/shard_map/ppermute | solution.py:449
  90.1 0.7 shard_map.88
  90.8 1.6 %collective-permute-done.5 = f32[2048,128]{1,0:T(8,128)S(1)} collective-permute-done((f32[2048,128]{1,0:T(8,128)S(1)}, f32[2048,128]{1,0:T(8,128)S(1)}, u32[]{:S(2)}, u32[]{:S(2)}) %collective-permute-start.5) | collective-permute-done | bytes 1048608 | tf_op jit(solution)/shard_map/ppermute | solution.py:449
  92.4 1.1 add.8
  93.4 9.5 %all-to-all-start.2 = ((f32[512,4,128]{2,1,0:T(4,128)}), f32[512,4,128]{2,1,0:T(4,128)S(1)}, u32[]{:S(2)}, u32[]{:S(2)}) async-start(f32[512,4,128]{2,1,0:T(4,128)} %bitcast.19), calls=%async_computation.2 | async-start | bytes 2097152 | tf_op jit(solution)/shard_map/all_to_all | solution.py:516
  102.9 0.5 shard_map.89
  103.5 32.5 %all-to-all-done.2 = f32[512,4,128]{2,1,0:T(4,128)S(1)} async-done(((f32[512,4,128]{2,1,0:T(4,128)}), f32[512,4,128]{2,1,0:T(4,128)S(1)}, u32[]{:S(2)}, u32[]{:S(2)}) %all-to-all-start.2) | async-done | bytes 1048608 | tf_op jit(solution)/shard_map/all_to_all | solution.py:516
  136.0 1.4 %shard_map.90 = f32[128,1024]{1,0:T(8,128)} custom-call(f32[2048,128]{1,0:T(8,128)S(1)} %bitcast.15, f32[128,1024]{1,0:T(8,128)S(1)} %get-tuple-element.29.gain_ref, f32[128,1024]{1,0:T(8,128)S(1)} %get-tuple-element.30.direct_ref), custom_call_target="tpu_custom_call" | custom-call | bytes 2621440 | tf_op jit(solution)/shard_map/pallas_call | solution.py:401
  (19 shorter events, 0.1 us)
Async XLA Ops:
  0.0 18.3 %copy-start.1 = (f32[128,1024]{1,0:T(8,128)S(1)}, f32[128,1024]{1,0:T(8,128)}, u32[]{:S(2)}) copy-start(f32[128,1024]{1,0:T(8,128)} %keys_ref.1) | copy-start | bytes 1572868
  0.0 18.5 %copy-start.2 = (f32[128,1024]{1,0:T(8,128)S(1)}, f32[128,1024]{1,0:T(8,128)}, u32[]{:S(2)}) copy-start(f32[128,1024]{1,0:T(8,128)} %values_ref.1) | copy-start | bytes 1572868
  0.0 18.7 %copy-start.3 = (f32[128,1024]{1,0:T(8,128)S(1)}, f32[128,1024]{1,0:T(8,128)}, u32[]{:S(2)}) copy-start(f32[128,1024]{1,0:T(8,128)} %queries_ref.1) | copy-start | bytes 1572868
  0.0 22.0 %copy-start.6 = (f32[3,3,128]{2,1,0:T(4,128)S(1)}, f32[3,3,128]{2,1,0:T(4,128)}, u32[]{:S(2)}) copy-start(f32[3,3,128]{2,1,0:T(4,128)} %param.11) | copy-start | bytes 13828
  0.0 31.3 %copy-start.7 = (f32[128]{0:T(128)S(1)}, f32[128]{0:T(128)}, u32[]{:S(2)}) copy-start(f32[128]{0:T(128)} %param.13) | copy-start | bytes 1540
  2.1 36.7 %all-to-all-start.1 = ((f32[16,64,128]{2,1,0:T(8,128)}), f32[16,64,128]{2,1,0:T(8,128)S(1)}, u32[]{:S(2)}, u32[]{:S(2)}) async-start(f32[16,64,128]{2,1,0:T(8,128)} %shard_map.83), calls=%async_computation.1 | async-start | bytes 1048576 | tf_op jit(solution)/shard_map/all_to_all | solution.py:462
  18.9 12.4 %collective-permute-start = (f32[6,128]{1,0:T(8,128)S(1)}, f32[6,128]{1,0:T(8,128)S(1)}, u32[]{:S(2)}, u32[]{:S(2)}) collective-permute-start(f32[6,128]{1,0:T(8,128)S(1)} %stack.3), channel_id=1, source_target_pairs={{0,1},{1,2},{2,3},{3,4},{4,5},{5,6},{6,7},{7,8},{8,9},{9,10},{10,1... | collective-permute-start | bytes 9224 | tf_op jit(solution)/shard_map/ppermute | solution.py:467
  38.7 24.5 %copy-start = (f32[1024,128]{1,0:T(8,128)}, f32[1024,128]{1,0:T(8,128)S(1)}, u32[]{:S(2)}) copy-start(f32[1024,128]{1,0:T(8,128)S(1)} %shard_map.84.p0) | copy-start | bytes 1572868
  38.7 20.5 %collective-permute-start.2 = (f32[1024,128]{1,0:T(8,128)S(1)}, f32[1024,128]{1,0:T(8,128)S(1)}, u32[]{:S(2)}, u32[]{:S(2)}) collective-permute-start(f32[1024,128]{1,0:T(8,128)S(1)} %shard_map.84.p0), channel_id=1, source_target_pairs={{0,16},{8,24},{16,0},{24,8},{32,48},{40,56},{48,32},{56,40},{64,80... | collective-permute-start | bytes 1572872 | tf_op jit(solution)/shard_map/ppermute | solution.py:449
  41.4 33.5 %all-to-all-start = ((f32[512,2,128]{2,1,0:T(2,128)}), f32[512,2,128]{2,1,0:T(2,128)S(1)}, u32[]{:S(2)}, u32[]{:S(2)}) async-start(f32[512,2,128]{2,1,0:T(2,128)} %bitcast.3), calls=%async_computation | async-start | bytes 1048576 | tf_op jit(solution)/shard_map/all_to_all | solution.py:473
  53.0 8.2 %collective-permute-start.1 = (f32[1024,128]{1,0:T(8,128)S(1)}, f32[1024,128]{1,0:T(8,128)S(1)}, u32[]{:S(2)}, u32[]{:S(2)}) collective-permute-start(f32[1024,128]{1,0:T(8,128)S(1)} %shard_map.84.p0), channel_id=1, source_target_pairs={{0,8},{8,0},{16,24},{24,16},{32,40},{40,32},{48,56},{56,48},{64,72... | collective-permute-start | bytes 1572872 | tf_op jit(solution)/shard_map/ppermute | solution.py:449
  59.2 4.0 %copy-start.4 = (f32[1024,128]{1,0:T(8,128)}, f32[1024,128]{1,0:T(8,128)S(1)}, u32[]{:S(2)}) copy-start(f32[1024,128]{1,0:T(8,128)S(1)} %collective-permute-done.2.p2) | copy-start | bytes 1572868
  59.3 3.9 %collective-permute-start.3 = (f32[1024,128]{1,0:T(8,128)S(1)}, f32[1024,128]{1,0:T(8,128)}, u32[]{:S(2)}, u32[]{:S(2)}) collective-permute-start(f32[1024,128]{1,0:T(8,128)S(1)} %collective-permute-done.2.p2), channel_id=1, source_target_pairs={{0,8},{8,0},{16,24},{24,16},{32,40},{40,32},{48,56},{56,48},{64,72... | collective-permute-start | bytes 1572872 | tf_op jit(solution)/shard_map/ppermute | solution.py:449
  61.2 2.0 %copy-start.5 = (f32[1024,128]{1,0:T(8,128)}, f32[1024,128]{1,0:T(8,128)S(1)}, u32[]{:S(2)}) copy-start(f32[1024,128]{1,0:T(8,128)S(1)} %collective-permute-done.1.p1) | copy-start | bytes 1572868
  77.9 5.1 %collective-permute-start.4 = (f32[2,2,256,128]{3,2,1,0:T(8,128)S(1)}, f32[2,2,256,128]{3,2,1,0:T(8,128)S(1)}, u32[]{:S(2)}, u32[]{:S(2)}) collective-permute-start(f32[2,2,256,128]{3,2,1,0:T(8,128)S(1)} %get-tuple-element.21), channel_id=1, source_target_pairs={{0,8},{8,0},{16,24},{24,16},{32,40},{40,32},{48,56},{56,48},{64,72... | collective-permute-start | bytes 1572872 | tf_op jit(solution)/shard_map/ppermute | solution.py:449
  87.8 4.6 %collective-permute-start.5 = (f32[2048,128]{1,0:T(8,128)S(1)}, f32[2048,128]{1,0:T(8,128)S(1)}, u32[]{:S(2)}, u32[]{:S(2)}) collective-permute-start(f32[2048,128]{1,0:T(8,128)S(1)} %get-tuple-element.27), channel_id=1, source_target_pairs={{0,8},{8,0},{16,24},{24,16},{32,40},{40,32},{48,56},{56,48},{64,72... | collective-permute-start | bytes 3145736 | tf_op jit(solution)/shard_map/ppermute | solution.py:449
  93.4 42.6 %all-to-all-start.2 = ((f32[512,4,128]{2,1,0:T(4,128)}), f32[512,4,128]{2,1,0:T(4,128)S(1)}, u32[]{:S(2)}, u32[]{:S(2)}) async-start(f32[512,4,128]{2,1,0:T(4,128)} %bitcast.19), calls=%async_computation.2 | async-start | bytes 2097152 | tf_op jit(solution)/shard_map/all_to_all | solution.py:516
